TPU v7x, 32 devices: a whole 2x2x4 slice. The times are simulated.
32 devices in a mesh: section: 2 (over core), dp: 8 (over z, x), tensor: 2 (over y).
Axes of the slice: x: 2, y: 2, z: 4, core: 2. Of those that a mesh axis runs over, the one named last changes fastest.
Arguments:
- ends_in: bfloat16 [2, 16, 1024, 768], P('section', 'dp', 'tensor'), may hold values from -6 to 6
- lengths: int32 [16], P('dp'), may hold values from 256 to 1024, as said below
- vectors: float32 [2, 12, 768], P('section', None, ('dp', 'tensor')), may hold values from -1.5 to 1.5
- w_qkv: bfloat16 [2, 768, 3, 768], P('section', 'dp', None, 'tensor'), may hold values from -0.21875 to 0.21875
- w_out: bfloat16 [2, 768, 768], P('section', 'tensor', 'dp'), may hold values from -0.875 to 0.875
- w_up: bfloat16 [2, 768, 3072], P('section', 'dp', 'tensor'), may hold values from -0.21875 to 0.21875
- w_down: bfloat16 [2, 3072, 768], P('section', 'tensor', 'dp'), may hold values from -0.109375 to 0.109375
Outputs:
- boundary: float32 [2, 16, 1024, 768], P('section', 'dp', 'tensor')
- vectors_grad: float32 [2, 12, 768], P('section', None, ('dp', 'tensor'))
- w_qkv_grad: float32 [2, 768, 3, 768], P('section', 'dp', None, 'tensor')
- w_out_grad: float32 [2, 768, 768], P('section', 'tensor', 'dp')
- w_up_grad: float32 [2, 768, 3072], P('section', 'dp', 'tensor')
- w_down_grad: float32 [2, 3072, 768], P('section', 'tensor', 'dp')
Inputs may be any that keep to these rules, and one draw needn't show every extreme that they name: `lengths`: among the 2 clips c with the same c // 2, at least one has all 1024 frames live.
All inputs are finite; a program needn't handle non-finite values.
Results may differ from a plain program's by a relative error of at most 0.013.
Values may be sent and summed in bfloat16 or wider, within the bound.
No kernel may reach another device: no remote copies, remote signals or barrier semaphores. Data moves between devices by JAX's collectives and lax.ppermute only.
A program may use at most 192 MiB of HBM per device.

v0:
```python
from functools import partial

import jax
import jax.numpy as jnp
from jax import lax
from jax.sharding import PartitionSpec as P

CONTRACT_ROWS = (((0,), (0,)), ((), ()))
CONTRACT_COLS = (((1,), (1,)), ((), ()))


def shortened(array):

    def short(part):
        return part.astype(jnp.bfloat16) if part.dtype == jnp.float32 else part

    return jax.tree.map(short, array)


def passed_along(array, axis, by):
    count = lax.axis_size(axis)
    pairs = [(i, i + by) for i in range(count) if 0 <= i + by < count]
    return lax.ppermute(array, axis, pairs)


def layer_norm(values, gain, shift):
    centre = jnp.mean(values, -1, keepdims=True)
    centred = values - centre
    spread = jnp.mean(centred * centred, -1, keepdims=True)
    return centred * lax.rsqrt(spread + 1e-05) * (1.0 + gain) + shift


def gather_rows(values):
    return lax.all_gather(values, "tensor", axis=0, tiled=True)


def gather_grads(values):
    return lax.all_gather(values, "tensor", axis=0, tiled=True)


def project_rows(left, right):
    rows = left.shape[0] // lax.axis_size("tensor")
    block = lax.dynamic_slice_in_dim(left, jnp.int32(0), lax.axis_size("tensor") * rows, 0)
    return lax.psum_scatter(
        jnp.dot(block, right, preferred_element_type=jnp.float32).astype(jnp.bfloat16),
        "tensor",
        scatter_dimension=0,
        tiled=True,
    ).astype(jnp.float32)


def back_rows(left, right):
    rows = left.shape[0] // lax.axis_size("tensor")
    block = lax.dynamic_slice_in_dim(left, jnp.int32(0), lax.axis_size("tensor") * rows, 0)
    return lax.psum_scatter(
        lax.dot_general(block, right, CONTRACT_COLS, preferred_element_type=jnp.float32).astype(
            jnp.bfloat16
        ),
        "tensor",
        scatter_dimension=0,
        tiled=True,
    ).astype(jnp.float32)


def split_heads(block, group):
    length, width = block.shape
    return block.reshape(length, width // group, group).transpose(1, 0, 2)


def merge_heads(block):
    count, length, group = block.shape
    return block.transpose(1, 0, 2).reshape(length, count * group)


def attention_forward(mixed, mask):
    length, _, head_width = mixed.shape
    group = 128 if head_width % 128 == 0 else 64
    per_group = group // 64
    span = min(512, length)

    def one_group(item):
        query, keys, value = item
        key_heads = keys.reshape(length, per_group, 64)
        value_heads = value.reshape(length, per_group, 64)
        pieces, logs = ([], [])
        for start in range(0, length, span):
            block = query[start : start + span].reshape(span, per_group, 64)
            scores = (
                jnp.einsum("qhd,khd->hqk", block, key_heads, preferred_element_type=jnp.float32)
                * 0.125
            )
            scores = jnp.where(mask[None, None, :], scores, -1e30)
            peak = jnp.max(scores, -1, keepdims=True)
            raised = jnp.exp(scores - peak)
            total = jnp.sum(raised, -1, keepdims=True)
            weights = (raised / total).astype(jnp.bfloat16)
            piece = jnp.einsum(
                "hqk,khd->qhd", weights, value_heads, preferred_element_type=jnp.float32
            )
            pieces.append(piece.reshape(span, group))
            logs.append((peak + jnp.log(total))[:, :, 0])
        return (jnp.concatenate(pieces, 0).astype(jnp.bfloat16), jnp.concatenate(logs, 1))

    items = (
        split_heads(mixed[:, 0], group),
        split_heads(mixed[:, 1], group),
        split_heads(mixed[:, 2], group),
    )
    attended, log_total = lax.map(one_group, items)
    return (merge_heads(attended), log_total)


def attention_backward(mixed, log_total, grad_out, mask):
    length, _, head_width = mixed.shape
    group = 128 if head_width % 128 == 0 else 64
    per_group = group // 64
    span = min(512, length)

    def one_group(item):
        query, keys, value, upstream, logs = item
        key_heads = keys.reshape(length, per_group, 64)
        value_heads = value.reshape(length, per_group, 64)
        grad_keys = jnp.zeros((length, per_group, 64), jnp.float32)
        grad_value = jnp.zeros((length, per_group, 64), jnp.float32)
        grad_query = []
        for start in range(0, length, span):
            block = query[start : start + span].reshape(span, per_group, 64)
            above = upstream[start : start + span].reshape(span, per_group, 64)
            scores = (
                jnp.einsum("qhd,khd->hqk", block, key_heads, preferred_element_type=jnp.float32)
                * 0.125
            )
            scores = jnp.where(mask[None, None, :], scores, -1e30)
            probs = jnp.exp(scores - logs[:, start : start + span, None])
            pushed = jnp.einsum(
                "qhd,khd->hqk", above, value_heads, preferred_element_type=jnp.float32
            )
            inner = jnp.sum(probs * pushed, -1, keepdims=True)
            slopes = (probs * (pushed - inner)).astype(jnp.bfloat16)
            piece = (
                jnp.einsum("hqk,khd->qhd", slopes, key_heads, preferred_element_type=jnp.float32)
                * 0.125
            )
            grad_query.append(piece.reshape(span, group))
            grad_keys = (
                grad_keys
                + jnp.einsum("hqk,qhd->khd", slopes, block, preferred_element_type=jnp.float32)
                * 0.125
            )
            grad_value = grad_value + jnp.einsum(
                "hqk,qhd->khd",
                probs.astype(jnp.bfloat16),
                above,
                preferred_element_type=jnp.float32,
            )
        return (
            jnp.concatenate(grad_query, 0).astype(jnp.bfloat16),
            grad_keys.reshape(length, group).astype(jnp.bfloat16),
            grad_value.reshape(length, group).astype(jnp.bfloat16),
        )

    items = (
        split_heads(mixed[:, 0], group),
        split_heads(mixed[:, 1], group),
        split_heads(mixed[:, 2], group),
        split_heads(grad_out, group),
        log_total,
    )
    parts = lax.map(one_group, items)
    return jnp.stack([merge_heads(parts[0]), merge_heads(parts[1]), merge_heads(parts[2])], 1)


def unpack(table, place, head_width, unit_width):
    query_bias = lax.dynamic_slice_in_dim(table[2], place * head_width, head_width)
    value_bias = lax.dynamic_slice_in_dim(table[3], place * head_width, head_width)
    mixed_bias = jnp.concatenate([query_bias, jnp.zeros_like(query_bias), value_bias])
    rise_bias = lax.dynamic_slice_in_dim(table[8:12].reshape(-1), place * unit_width, unit_width)
    return (table[0], table[1], mixed_bias, table[4], table[5], table[6], rise_bias, table[7])


def forward_layer(values, frames, mats, biases):
    w_mixed, w_proj, w_rise, w_fall = mats
    gain_one, shift_one, mixed_bias, proj_bias, gain_two, shift_two, rise_bias, fall_bias = biases
    width = values.shape[-1]
    normed = gather_rows(layer_norm(values, gain_one, shift_one).astype(jnp.bfloat16))
    length = normed.shape[0]
    mixed = (
        jnp.dot(normed, w_mixed.reshape(width, -1), preferred_element_type=jnp.float32) + mixed_bias
    )
    mixed = mixed.astype(jnp.bfloat16).reshape(length, 3, -1)
    mask = jnp.arange(length) < frames
    attended, log_total = attention_forward(mixed, mask)
    middle = values + project_rows(attended, w_proj) + proj_bias
    normed_two = gather_rows(layer_norm(middle, gain_two, shift_two).astype(jnp.bfloat16))
    before = jnp.dot(normed_two, w_rise, preferred_element_type=jnp.float32) + rise_bias
    hidden = jax.nn.gelu(before, approximate=False).astype(jnp.bfloat16)
    result = middle + project_rows(hidden, w_fall) + fall_bias
    return (
        result,
        (values, normed, mixed, log_total, attended, middle, normed_two, before, hidden, frames),
    )


def backward_layer(saved, incoming, mats, biases):
    values, normed, mixed, log_total, attended, middle, normed_two, before, hidden, frames = saved
    w_mixed, w_proj, w_rise, w_fall = mats
    gain_one, shift_one, _, _, gain_two, shift_two, _, _ = biases
    width = values.shape[-1]
    length = normed.shape[0]
    fall_in = gather_grads(incoming.astype(jnp.bfloat16))
    grad_fall = lax.dot_general(hidden, fall_in, CONTRACT_ROWS, preferred_element_type=jnp.float32)
    grad_hidden = lax.dot_general(
        fall_in, w_fall, CONTRACT_COLS, preferred_element_type=jnp.float32
    )
    _, gelu_back = jax.vjp(partial(jax.nn.gelu, approximate=False), before)
    grad_before = gelu_back(grad_hidden)[0].astype(jnp.bfloat16)
    grad_rise = lax.dot_general(
        normed_two, grad_before, CONTRACT_ROWS, preferred_element_type=jnp.float32
    )
    grad_rise_bias = jnp.sum(grad_before, 0, dtype=jnp.float32)
    grad_norm_two = back_rows(grad_before, w_rise)
    _, norm_back = jax.vjp(layer_norm, middle, gain_two, shift_two)
    grad_mid, grad_gain_two, grad_shift_two = norm_back(grad_norm_two)
    grad_middle = incoming + grad_mid
    proj_in = gather_grads(grad_middle.astype(jnp.bfloat16))
    grad_proj = lax.dot_general(
        attended, proj_in, CONTRACT_ROWS, preferred_element_type=jnp.float32
    )
    grad_attended = lax.dot_general(
        proj_in, w_proj, CONTRACT_COLS, preferred_element_type=jnp.float32
    )
    mask = jnp.arange(length) < frames
    grad_mixed = attention_backward(mixed, log_total, grad_attended.astype(jnp.bfloat16), mask)
    flat = grad_mixed.reshape(length, -1)
    grad_weights_mixed = lax.dot_general(
        normed, flat, CONTRACT_ROWS, preferred_element_type=jnp.float32
    )
    grad_bias_mixed = jnp.sum(flat, 0, dtype=jnp.float32).reshape(3, -1)
    grad_norm_one = back_rows(flat, w_mixed.reshape(width, -1))
    _, first_back = jax.vjp(layer_norm, values, gain_one, shift_one)
    grad_input, grad_gain_one, grad_shift_one = first_back(grad_norm_one)
    terms = (
        grad_weights_mixed.reshape(width, 3, -1),
        grad_proj,
        grad_rise,
        grad_fall,
        grad_gain_one,
        grad_shift_one,
        grad_bias_mixed[0],
        grad_bias_mixed[2],
        jnp.sum(grad_middle, 0),
        grad_gain_two,
        grad_shift_two,
        jnp.sum(incoming, 0),
        grad_rise_bias,
    )
    return (grad_middle + grad_input, terms)


def body(ends_in, lengths, vectors, w_qkv, w_out, w_up, w_down):
    first = lax.axis_index("section") == 0
    micro = ends_in.shape[1]
    place = lax.axis_index("tensor")
    gathered = (
        lax.all_gather(w_qkv[0], "dp", axis=0, tiled=True),
        lax.all_gather(w_out[0], "dp", axis=1, tiled=True),
        lax.all_gather(w_up[0], "dp", axis=0, tiled=True),
        lax.all_gather(w_down[0], "dp", axis=1, tiled=True),
    )
    head_width = gathered[0].shape[-1]
    unit_width = gathered[2].shape[-1]
    table = lax.all_gather(vectors[0], ("dp", "tensor"), axis=1, tiled=True)
    width = table.shape[1]
    biases = unpack(table, place, head_width, unit_width)
    received = jnp.zeros(ends_in.shape[2:], jnp.float32)
    kept, outputs = ([], [])
    for tick in range(micro + 1):
        own = ends_in[0, min(tick, micro - 1)].astype(jnp.float32)
        values = jnp.where(first, own, received)
        frames = jnp.where(first, lengths[min(tick, micro - 1)], lengths[max(tick - 1, 0)])
        result, saved = forward_layer(values, frames, gathered, biases)
        kept.append(saved)
        outputs.append(result)
        if tick < micro:
            received = passed_along(shortened(result), "section", 1).astype(result.dtype)
    stacked = jax.tree.map(lambda *items: jnp.stack(items), *kept)
    again = (
        lax.all_gather(w_qkv[0], "dp", axis=0, tiled=True),
        lax.all_gather(w_out[0], "dp", axis=1, tiled=True),
        lax.all_gather(w_up[0], "dp", axis=0, tiled=True),
        lax.all_gather(w_down[0], "dp", axis=1, tiled=True),
    )
    grad_back = jnp.zeros(ends_in.shape[2:], jnp.float32)
    totals = None
    gradients_in = []
    for tick in range(micro + 1):
        upstream = ends_in[0, min(tick, micro - 1)].astype(jnp.float32)
        incoming = jnp.where(first, grad_back, upstream)
        active = jnp.where(first, tick >= 1, tick < micro)
        incoming = jnp.where(active, incoming, 0.0)
        slot = jnp.where(first, max(tick - 1, 0), min(tick + 1, micro))
        saved = jax.tree.map(
            lambda item: lax.dynamic_index_in_dim(item, slot, 0, keepdims=False), stacked
        )
        grad_values, terms = backward_layer(saved, incoming, again, biases)
        totals = terms if totals is None else jax.tree.map(jnp.add, totals, terms)
        gradients_in.append(grad_values)
        if tick < micro:
            grad_back = passed_along(shortened(grad_values), "section", -1).astype(
                grad_values.dtype
            )
    boundary = jnp.stack(
        [jnp.where(first, gradients_in[index + 1], outputs[index + 1]) for index in range(micro)]
    )
    matrices = (totals[0], totals[1], totals[2], totals[3])
    matrix_terms = (
        lax.psum_scatter(matrices[0], "dp", scatter_dimension=0, tiled=True),
        lax.psum_scatter(matrices[1], "dp", scatter_dimension=1, tiled=True),
        lax.psum_scatter(matrices[2], "dp", scatter_dimension=0, tiled=True),
        lax.psum_scatter(matrices[3], "dp", scatter_dimension=1, tiled=True),
    )
    empty = jnp.zeros((width,), jnp.float32)
    query_full = lax.dynamic_update_slice_in_dim(empty, totals[6], place * head_width, 0)
    value_full = lax.dynamic_update_slice_in_dim(empty, totals[7], place * head_width, 0)
    rise_full = lax.dynamic_update_slice_in_dim(
        jnp.zeros((4 * width,), jnp.float32), totals[12], place * unit_width, 0
    )
    rows_head = jnp.stack(
        [totals[4], totals[5], query_full, value_full, totals[8], totals[9], totals[10], totals[11]]
    )
    table_grad = jnp.concatenate([rows_head, rise_full.reshape(4, width)], 0)
    vector_terms = lax.psum_scatter(table_grad, ("dp", "tensor"), scatter_dimension=1, tiled=True)
    return (
        boundary[None],
        vector_terms[None],
        matrix_terms[0][None],
        matrix_terms[1][None],
        matrix_terms[2][None],
        matrix_terms[3][None],
    )


def solution(mesh):
    in_specs = (
        P("section", "dp", "tensor", None),
        P("dp"),
        P("section", None, ("dp", "tensor")),
        P("section", "dp", None, "tensor"),
        P("section", "tensor", "dp"),
        P("section", "dp", "tensor"),
        P("section", "tensor", "dp"),
    )
    out_specs = (
        P("section", "dp", "tensor", None),
        P("section", None, ("dp", "tensor")),
        P("section", "dp", None, "tensor"),
        P("section", "tensor", "dp"),
        P("section", "dp", "tensor"),
        P("section", "tensor", "dp"),
    )
    return jax.shard_map(body, mesh=mesh, in_specs=in_specs, out_specs=out_specs, check_vma=False)
```

profile of v0, /device:TPU:1, one launch (start us, length us, event | category | flops | bytes accessed | tf_op | source)
XLA Modules:
  0.0 1852.3 jit_solution(13685025068605210191)
XLA Ops:
  8.7 38.5 %all-gather = f32[1,12,768]{1,0,2:T(1,128)S(1)} all-gather(f32[1,12,48]{1,0,2:T(1,128)S(1)} %copy.135), channel_id=2, replica_groups=mesh['section'=2,'dp'=8,'tensor'=2] {'dp','tensor'}, dimensions={2}, use_global_device_ids=true | all-gather | bytes 39168 | tf_op jit(solution)/shard_map/all_gather | solution.py:272
  68.0 27.2 %all-gather.2 = bf16[1,384,768]{1,2,0:T(8,128)(2,1)} all-gather(bf16[1,384,96]{1,2,0:T(8,128)(2,1)S(1)} %copy-done.55), channel_id=4, replica_groups=mesh['section'=2,'dp'=8,'tensor'=2] {'dp'}, dimensions={2}, use_global_device_ids=true | all-gather | bytes 663552 | tf_op jit(solution)/shard_map/all_gather | solution.py:266
  112.9 27.1 %while.84 = (s32[]{:T(128)}, bf16[3,1024,128]{1,2,0:T(8,128)(2,1)}, f32[3,2,1024]{2,1,0:T(2,128)S(1)}, bf16[3,1024,128]{1,2,0:T(8,128)(2,1)}, bf16[3,1024,128]{1...) while((s32[]{:T(128)}, bf16[3,1024,128]{1,2,0:T(8,128)(2,1)}, ...), condition=%wide.region_7.8_spmd.clone, body=%wide.region_2.7_spmd.clone.sunk | while | flops 562693120 | bytes 28924548 | solution.py:109
  144.1 35.0 %reduce-scatter.20.cloned.1.call-done = bf16[512,768]{1,0:T(8,128)(2,1)} async-done(((bf16[1024,768]{1,0:T(8,128)(2,1)}), bf16[512,768]{1,0:T(8,128)(2,1)}) %reduce-scatter.20.cloned.1.call-update) | async-done | bytes 786448 | tf_op jit(solution)/shard_map/reduce_scatter | solution.py:44
  187.1 45.2 %all-gather.47.cloned.1.call-done = bf16[1,768,1536]{2,1,0:T(8,128)(2,1)} async-done(((bf16[1,96,1536]{2,1,0:T(8,128)(2,1)}), bf16[1,768,1536]{2,1,0:T(8,128)(2,1)}) %all-gather.47.cloned.1.call-update) | async-done | bytes 2359312 | tf_op jit(solution)/shard_map/all_gather | solution.py:267
  232.3 29.0 %all-gather.23.cloned.1.call-done = bf16[1024,768]{1,0:T(8,128)(2,1)} async-done(((bf16[512,768]{1,0:T(8,128)(2,1)}), bf16[1024,768]{1,0:T(8,128)(2,1)}) %all-gather.23.cloned.1.call-update) | async-done | bytes 1572880 | tf_op jit(solution)/shard_map/all_gather | solution.py:34
  280.8 33.7 %all-gather.49.cloned.1.call-done = bf16[1,1536,768]{1,2,0:T(8,128)(2,1)} async-done(((bf16[1,1536,96]{1,2,0:T(8,128)(2,1)}), bf16[1,1536,768]{1,2,0:T(8,128)(2,1)}) %all-gather.49.cloned.1.call-update) | async-done | bytes 2359312 | tf_op jit(solution)/shard_map/all_gather | solution.py:268
  321.0 25.9 %reduce-scatter.22.cloned.1.call-done = bf16[512,768]{1,0:T(8,128)(2,1)} async-done(((bf16[1024,768]{1,0:T(8,128)(2,1)}), bf16[512,768]{1,0:T(8,128)(2,1)}) %reduce-scatter.22.cloned.1.call-update) | async-done | bytes 786448 | tf_op jit(solution)/shard_map/reduce_scatter | solution.py:44
  357.4 25.5 %all-gather.25.cloned.1.call-done = bf16[1024,768]{1,0:T(8,128)(2,1)} async-done(((bf16[512,768]{1,0:T(8,128)(2,1)}), bf16[1024,768]{1,0:T(8,128)(2,1)}) %all-gather.25.cloned.1.call-update) | async-done | bytes 1572880 | tf_op jit(solution)/shard_map/all_gather | solution.py:34
  396.3 25.4 %while.85 = (s32[]{:T(128)}, bf16[3,1024,128]{1,2,0:T(8,128)(2,1)}, f32[3,2,1024]{2,1,0:T(2,128)S(1)}, bf16[3,1024,128]{1,2,0:T(8,128)(2,1)}, bf16[3,1024,128]{1...) while((s32[]{:T(128)}, bf16[3,1024,128]{1,2,0:T(8,128)(2,1)}, ...), condition=%wide.region_19.20_spmd.clone, body=%wide.region_14.19_spmd.clone.sunk | while | flops 562693120 | bytes 28924548 | solution.py:109
  425.3 26.2 %reduce-scatter.24.cloned.1.call-done = bf16[512,768]{1,0:T(8,128)(2,1)} async-done(((bf16[1024,768]{1,0:T(8,128)(2,1)}), bf16[512,768]{1,0:T(8,128)(2,1)}) %reduce-scatter.24.cloned.1.call-update) | async-done | bytes 786448 | tf_op jit(solution)/shard_map/reduce_scatter | solution.py:44
  455.1 27.1 %all-gather.27.cloned.1.call-done = bf16[1024,768]{1,0:T(8,128)(2,1)} async-done(((bf16[512,768]{1,0:T(8,128)(2,1)}), bf16[1024,768]{1,0:T(8,128)(2,1)}) %all-gather.27.cloned.1.call-update) | async-done | bytes 1572880 | tf_op jit(solution)/shard_map/all_gather | solution.py:34
  507.1 26.2 %reduce-scatter.26.cloned.1.call-done = bf16[512,768]{1,0:T(8,128)(2,1)} async-done(((bf16[1024,768]{1,0:T(8,128)(2,1)}), bf16[512,768]{1,0:T(8,128)(2,1)}) %reduce-scatter.26.cloned.1.call-update) | async-done | bytes 786448 | tf_op jit(solution)/shard_map/reduce_scatter | solution.py:44
  542.2 26.6 %all-gather.29.cloned.1.call-done = bf16[1024,768]{1,0:T(8,128)(2,1)} async-done(((bf16[512,768]{1,0:T(8,128)(2,1)}), bf16[1024,768]{1,0:T(8,128)(2,1)}) %all-gather.29.cloned.1.call-update) | async-done | bytes 1572880 | tf_op jit(solution)/shard_map/all_gather | solution.py:34
  582.7 30.3 %while.86 = (s32[]{:T(128)}, bf16[3,1024,128]{1,2,0:T(8,128)(2,1)}, f32[3,2,1024]{2,1,0:T(2,128)S(1)}, bf16[3,1024,128]{1,2,0:T(8,128)(2,1)}, bf16[3,1024,128]{1...) while((s32[]{:T(128)}, bf16[3,1024,128]{1,2,0:T(8,128)(2,1)}, ...), condition=%wide.region_31.32_spmd.clone, body=%wide.region_26.31_spmd.clone.sunk | while | flops 562693120 | bytes 28924548 | solution.py:109
  616.5 26.2 %reduce-scatter.28.cloned.1.call-done = bf16[512,768]{1,0:T(8,128)(2,1)} async-done(((bf16[1024,768]{1,0:T(8,128)(2,1)}), bf16[512,768]{1,0:T(8,128)(2,1)}) %reduce-scatter.28.cloned.1.call-update) | async-done | bytes 786448 | tf_op jit(solution)/shard_map/reduce_scatter | solution.py:44
  647.8 26.3 %all-gather.31.cloned.1.call-done = bf16[1024,768]{1,0:T(8,128)(2,1)} async-done(((bf16[512,768]{1,0:T(8,128)(2,1)}), bf16[1024,768]{1,0:T(8,128)(2,1)}) %all-gather.31.cloned.1.call-update) | async-done | bytes 1572880 | tf_op jit(solution)/shard_map/all_gather | solution.py:34
  736.4 20.7 %reduce-scatter.30.cloned.1.call-done = bf16[512,768]{1,0:T(8,128)(2,1)} async-done(((bf16[1024,768]{1,0:T(8,128)(2,1)}), bf16[512,768]{1,0:T(8,128)(2,1)}) %reduce-scatter.30.cloned.1.call-update) | async-done | bytes 786448 | tf_op jit(solution)/shard_map/reduce_scatter | solution.py:55
  800.4 53.3 %while.87 = (s32[]{:T(128)}, bf16[3,1024,128]{1,2,0:T(8,128)(2,1)}, bf16[3,1024,128]{1,2,0:T(8,128)(2,1)}, bf16[3,1024,128]{1,2,0:T(8,128)(2,1)}, bf16[3,1024,12...) while((s32[]{:T(128)}, bf16[3,1024,128]{1,2,0:T(8,128)(2,1)}, ...), condition=%wide.region_43.44_spmd.clone, body=%wide.region_40.43_spmd.clone.sunk | while | flops 1375075328 | bytes 76363944 | solution.py:169
  874.5 20.2 %reduce-scatter.32.cloned.1.call-done = bf16[512,768]{1,0:T(8,128)(2,1)} async-done(((bf16[1024,768]{1,0:T(8,128)(2,1)}), bf16[512,768]{1,0:T(8,128)(2,1)}) %reduce-scatter.32.cloned.1.call-update) | async-done | bytes 786448 | tf_op jit(solution)/shard_map/reduce_scatter | solution.py:55
  909.1 27.0 %all-gather.37.cloned.1.call-done = bf16[1024,768]{1,0:T(8,128)(2,1)} async-done(((bf16[512,768]{1,0:T(8,128)(2,1)}), bf16[1024,768]{1,0:T(8,128)(2,1)}) %all-gather.37.cloned.1.call-update) | async-done | bytes 1572880 | tf_op jit(solution)/shard_map/all_gather | solution.py:38
  961.8 26.2 %reduce-scatter.34.cloned.1.call-done = bf16[512,768]{1,0:T(8,128)(2,1)} async-done(((bf16[1024,768]{1,0:T(8,128)(2,1)}), bf16[512,768]{1,0:T(8,128)(2,1)}) %reduce-scatter.34.cloned.1.call-update) | async-done | bytes 786448 | tf_op jit(solution)/shard_map/reduce_scatter | solution.py:55
  1032.5 49.4 %while.88 = (s32[]{:T(128)}, bf16[3,1024,128]{1,2,0:T(8,128)(2,1)}, bf16[3,1024,128]{1,2,0:T(8,128)(2,1)}, bf16[3,1024,128]{1,2,0:T(8,128)(2,1)}, bf16[3,1024,12...) while((s32[]{:T(128)}, bf16[3,1024,128]{1,2,0:T(8,128)(2,1)}, ...), condition=%wide.region_57.58_spmd.clone, body=%wide.region_54.57_spmd.clone.sunk | while | flops 1375075328 | bytes 76363944 | solution.py:169
  1094.6 26.1 %reduce-scatter.36.cloned.1.call-done = bf16[512,768]{1,0:T(8,128)(2,1)} async-done(((bf16[1024,768]{1,0:T(8,128)(2,1)}), bf16[512,768]{1,0:T(8,128)(2,1)}) %reduce-scatter.36.cloned.1.call-update) | async-done | bytes 786448 | tf_op jit(solution)/shard_map/reduce_scatter | solution.py:55
  1134.1 27.0 %all-gather.41.cloned.1.call-done = bf16[1024,768]{1,0:T(8,128)(2,1)} async-done(((bf16[512,768]{1,0:T(8,128)(2,1)}), bf16[1024,768]{1,0:T(8,128)(2,1)}) %all-gather.41.cloned.1.call-update) | async-done | bytes 1572880 | tf_op jit(solution)/shard_map/all_gather | solution.py:38
  1186.2 26.2 %reduce-scatter.38.cloned.1.call-done = bf16[512,768]{1,0:T(8,128)(2,1)} async-done(((bf16[1024,768]{1,0:T(8,128)(2,1)}), bf16[512,768]{1,0:T(8,128)(2,1)}) %reduce-scatter.38.cloned.1.call-update) | async-done | bytes 786448 | tf_op jit(solution)/shard_map/reduce_scatter | solution.py:55
  1255.2 49.6 %while.89 = (s32[]{:T(128)}, bf16[3,1024,128]{1,2,0:T(8,128)(2,1)}, bf16[3,1024,128]{1,2,0:T(8,128)(2,1)}, bf16[3,1024,128]{1,2,0:T(8,128)(2,1)}, bf16[3,1024,12...) while((s32[]{:T(128)}, bf16[3,1024,128]{1,2,0:T(8,128)(2,1)}, ...), condition=%wide.region_71.72_spmd.clone, body=%wide.region_68.71_spmd.clone.sunk | while | flops 1375075328 | bytes 76363944 | solution.py:169
  1421.4 72.4 %reduce-scatter.52.cloned.1.call-done = f32[48,12]{1,0:T(8,128)} async-done(((f32[768,12]{1,0:T(8,128)}), f32[48,12]{1,0:T(8,128)}) %reduce-scatter.52.cloned.1.call-update) | async-done | bytes 2320
  1495.1 66.1 %reduce-scatter.46.cloned.1.call-done = f32[384,96]{0,1:T(8,128)} async-done(((f32[384,768]{0,1:T(8,128)}), f32[384,96]{0,1:T(8,128)}) %reduce-scatter.46.cloned.1.call-update) | async-done | bytes 147472 | tf_op jit(solution)/shard_map/reduce_scatter | solution.py:318
  1561.3 100.9 %reduce-scatter.50.cloned.1.call-done = f32[1536,96]{0,1:T(8,128)} async-done(((f32[1536,768]{0,1:T(8,128)}), f32[1536,96]{0,1:T(8,128)}) %reduce-scatter.50.cloned.1.call-update) | async-done | bytes 589840 | tf_op jit(solution)/shard_map/reduce_scatter | solution.py:320
  1662.2 99.7 %reduce-scatter.48.cloned.1.call-done = f32[96,1536]{1,0:T(8,128)} async-done(((f32[768,1536]{1,0:T(8,128)}), f32[96,1536]{1,0:T(8,128)}) %reduce-scatter.48.cloned.1.call-update) | async-done | bytes 589840 | tf_op jit(solution)/shard_map/reduce_scatter | solution.py:319
  1761.9 83.4 %reduce-scatter.44.cloned.1.call-done = f32[96,3,384]{2,0,1:T(8,128)} async-done(((f32[768,3,384]{2,0,1:T(8,128)}), f32[96,3,384]{2,0,1:T(8,128)}) %reduce-scatter.44.cloned.1.call-update) | async-done | bytes 442384 | tf_op jit(solution)/shard_map/reduce_scatter | solution.py:317
  (759 shorter events, 819.1 us)
Async XLA Ops:
  7.2 88.0 %all-gather.45.cloned.1.call-start = ((), (), s32[]{:S(2)}) async-start(), calls=%async_computation.45 | async-start | bytes 1990656 | tf_op jit(solution)/shard_map/all_gather | solution.py:265
  7.9 91.1 %all-gather.21.cloned.1.call-start = ((), (), s32[]{:S(2)}) async-start(), calls=%async_computation.17 | async-start | bytes 2359296 | tf_op jit(solution)/shard_map/all_gather | solution.py:34
  65.9 113.2 %reduce-scatter.20.cloned.1.call-start = ((), (), s32[]{:S(2)}) async-start(), calls=%async_computation.18 | async-start | bytes 2359296 | tf_op jit(solution)/shard_map/reduce_scatter | solution.py:44
  143.4 88.8 %all-gather.47.cloned.1.call-start = ((), (), s32[]{:S(2)}) async-start(), calls=%async_computation.46 | async-start | bytes 2654208 | tf_op jit(solution)/shard_map/all_gather | solution.py:267
  144.0 117.3 %all-gather.23.cloned.1.call-start = ((), (), s32[]{:S(2)}) async-start(), calls=%async_computation.19 | async-start | bytes 2359296 | tf_op jit(solution)/shard_map/all_gather | solution.py:34
  184.9 129.6 %all-gather.49.cloned.1.call-start = ((), (), s32[]{:S(2)}) async-start(), calls=%async_computation.47 | async-start | bytes 2654208 | tf_op jit(solution)/shard_map/all_gather | solution.py:268
  185.4 161.5 %reduce-scatter.22.cloned.1.call-start = ((), (), s32[]{:S(2)}) async-start(), calls=%async_computation.20 | async-start | bytes 2359296 | tf_op jit(solution)/shard_map/reduce_scatter | solution.py:44
  321.0 61.9 %all-gather.25.cloned.1.call-start = ((), (), s32[]{:S(2)}) async-start(), calls=%async_computation.21 | async-start | bytes 2359296 | tf_op jit(solution)/shard_map/all_gather | solution.py:34
  356.0 95.5 %reduce-scatter.24.cloned.1.call-start = ((), (), s32[]{:S(2)}) async-start(), calls=%async_computation.22 | async-start | bytes 2359296 | tf_op jit(solution)/shard_map/reduce_scatter | solution.py:44
  425.3 57.0 %all-gather.27.cloned.1.call-start = ((), (), s32[]{:S(2)}) async-start(), calls=%async_computation.23 | async-start | bytes 2359296 | tf_op jit(solution)/shard_map/all_gather | solution.py:34
  454.9 78.4 %reduce-scatter.26.cloned.1.call-start = ((), (), s32[]{:S(2)}) async-start(), calls=%async_computation.24 | async-start | bytes 2359296 | tf_op jit(solution)/shard_map/reduce_scatter | solution.py:44
  507.0 61.7 %all-gather.29.cloned.1.call-start = ((), (), s32[]{:S(2)}) async-start(), calls=%async_computation.25 | async-start | bytes 2359296 | tf_op jit(solution)/shard_map/all_gather | solution.py:34
  541.9 100.8 %reduce-scatter.28.cloned.1.call-start = ((), (), s32[]{:S(2)}) async-start(), calls=%async_computation.26 | async-start | bytes 2359296 | tf_op jit(solution)/shard_map/reduce_scatter | solution.py:44
  616.5 57.6 %all-gather.31.cloned.1.call-start = ((), (), s32[]{:S(2)}) async-start(), calls=%async_computation.27 | async-start | bytes 2359296 | tf_op jit(solution)/shard_map/all_gather | solution.py:34
  646.7 58.4 %all-gather.33.cloned.1.call-start = ((), (), s32[]{:S(2)}) async-start(), calls=%async_computation.28 | async-start | bytes 2359296 | tf_op jit(solution)/shard_map/all_gather | solution.py:38
  647.3 109.8 %reduce-scatter.30.cloned.1.call-start = ((), (), s32[]{:S(2)}) async-start(), calls=%async_computation.29 | async-start | bytes 2359296 | tf_op jit(solution)/shard_map/reduce_scatter | solution.py:55
  730.9 63.4 %all-gather.35.cloned.1.call-start = ((), (), s32[]{:S(2)}) async-start(), calls=%async_computation.30 | async-start | bytes 2359296 | tf_op jit(solution)/shard_map/all_gather | solution.py:38
  766.9 127.8 %reduce-scatter.32.cloned.1.call-start = ((), (), s32[]{:S(2)}) async-start(), calls=%async_computation.31 | async-start | bytes 2359296 | tf_op jit(solution)/shard_map/reduce_scatter | solution.py:55
  868.4 67.7 %all-gather.37.cloned.1.call-start = ((), (), s32[]{:S(2)}) async-start(), calls=%async_computation.32 | async-start | bytes 2359296 | tf_op jit(solution)/shard_map/all_gather | solution.py:38
  909.0 79.0 %reduce-scatter.34.cloned.1.call-start = ((), (), s32[]{:S(2)}) async-start(), calls=%async_computation.33 | async-start | bytes 2359296 | tf_op jit(solution)/shard_map/reduce_scatter | solution.py:55
  961.8 64.5 %all-gather.39.cloned.1.call-start = ((), (), s32[]{:S(2)}) async-start(), calls=%async_computation.34 | async-start | bytes 2359296 | tf_op jit(solution)/shard_map/all_gather | solution.py:38
  998.9 121.8 %reduce-scatter.36.cloned.1.call-start = ((), (), s32[]{:S(2)}) async-start(), calls=%async_computation.35 | async-start | bytes 2359296 | tf_op jit(solution)/shard_map/reduce_scatter | solution.py:55
  1094.5 66.6 %all-gather.41.cloned.1.call-start = ((), (), s32[]{:S(2)}) async-start(), calls=%async_computation.36 | async-start | bytes 2359296 | tf_op jit(solution)/shard_map/all_gather | solution.py:38
  1134.0 78.4 %reduce-scatter.38.cloned.1.call-start = ((), (), s32[]{:S(2)}) async-start(), calls=%async_computation.37 | async-start | bytes 2359296 | tf_op jit(solution)/shard_map/reduce_scatter | solution.py:55
  1186.1 62.8 %all-gather.43.cloned.1.call-start = ((), (), s32[]{:S(2)}) async-start(), calls=%async_computation.38 | async-start | bytes 2359296 | tf_op jit(solution)/shard_map/all_gather | solution.py:38
  1221.6 119.3 %reduce-scatter.40.cloned.1.call-start = ((), (), s32[]{:S(2)}) async-start(), calls=%async_computation.39 | async-start | bytes 2359296 | tf_op jit(solution)/shard_map/reduce_scatter | solution.py:55
  1314.6 100.2 %reduce-scatter.42.cloned.1.call-start = ((), (), s32[]{:S(2)}) async-start(), calls=%async_computation.40 | async-start | bytes 2359296 | tf_op jit(solution)/shard_map/reduce_scatter | solution.py:44
  1324.5 169.2 %reduce-scatter.52.cloned.1.call-start = ((), (), s32[]{:S(2)}) async-start(), calls=%async_computation.48 | async-start | bytes 417792
  1346.8 214.5 %reduce-scatter.46.cloned.1.call-start = ((), (), s32[]{:S(2)}) async-start(), calls=%async_computation.42 | async-start | bytes 1327104 | tf_op jit(solution)/shard_map/reduce_scatter | solution.py:318
  1350.1 312.1 %reduce-scatter.50.cloned.1.call-start = ((), (), s32[]{:S(2)}) async-start(), calls=%async_computation.44 | async-start | bytes 5308416 | tf_op jit(solution)/shard_map/reduce_scatter | solution.py:320
  1365.7 396.2 %reduce-scatter.48.cloned.1.call-start = ((), (), s32[]{:S(2)}) async-start(), calls=%async_computation.43 | async-start | bytes 5308416 | tf_op jit(solution)/shard_map/reduce_scatter | solution.py:319
  1380.0 465.3 %reduce-scatter.44.cloned.1.call-start = ((), (), s32[]{:S(2)}) async-start(), calls=%async_computation.41 | async-start | bytes 3981312 | tf_op jit(solution)/shard_map/reduce_scatter | solution.py:317
  (94 other events, 2639.2 us)
Sparse Core Ops, SparseCore 0:
  10.2 47.4 all-gather.44
  66.0 29.7 all-gather.20
  143.6 35.5 reduce-scatter.19
  181.4 50.8 all-gather.46
  234.3 26.9 all-gather.22
  263.6 50.8 all-gather.48
  321.1 25.7 reduce-scatter.21
  356.1 26.7 all-gather.24
  425.4 26.0 reduce-scatter.23
  455.0 27.2 all-gather.26
  507.2 26.0 reduce-scatter.25
  542.0 26.7 all-gather.28
  616.6 26.0 reduce-scatter.27
  646.8 27.2 all-gather.30
  675.5 27.2 all-gather.32
  731.0 26.0 reduce-scatter.29
  767.0 27.2 all-gather.34
  868.5 26.1 reduce-scatter.31
  909.2 26.9 all-gather.36
  961.9 26.0 reduce-scatter.33
  999.0 27.2 all-gather.38
  1094.6 26.0 reduce-scatter.35
  1134.1 26.9 all-gather.40
  1186.3 26.0 reduce-scatter.37
  1221.7 27.2 all-gather.42
  1314.7 26.0 reduce-scatter.39
  1343.0 26.0 reduce-scatter.41
  1373.8 119.8 reduce-scatter.51
  1498.1 63.1 reduce-scatter.45
  1565.8 96.3 reduce-scatter.49
  1666.9 94.9 reduce-scatter.47
  1766.6 78.6 reduce-scatter.43
where the time goes:
time: 1860 us; the launch traced here: 1850 us
  waiting for transfers between devices  1010 us (54%)
  matrix products  369 us (20%)
  other arithmetic  193 us (10%)
  local copies, waits for them, and re-layouts  184 us (10%)
  blocking collectives  65.7 us (4%)
    reduce_scatter x6, waiting for transfers between devices, project_rows(): lax.psum_scatter(jnp.dot(block, right, preferred_element_type=jnp.float32...  140 us
    all_gather x6, waiting for transfers between devices, gather_rows(): return lax.all_gather(values, 'tensor', axis=0, tiled=True)  134 us
    reduce_scatter x6, waiting for transfers between devices, back_rows(): lax.psum_scatter(lax.dot_general(block, right, CONTRACT_COLS, preferred_e...  130 us
    reduce_scatter x1, waiting for transfers between devices, body(): lax.psum_scatter(matrices[3], 'dp', scatter_dimension=1, tiled=True)  101 us
    reduce_scatter x1, waiting for transfers between devices, body(): lax.psum_scatter(matrices[2], 'dp', scatter_dimension=0, tiled=True)  99.7 us
    all_gather x6, waiting for transfers between devices, gather_grads(): return lax.all_gather(values, 'tensor', axis=0, tiled=True)  92.2 us
    reduce_scatter x1, waiting for transfers between devices, body(): lax.psum_scatter(matrices[0], 'dp', scatter_dimension=0, tiled=True)  83.4 us
    unnamed x33, waiting for transfers between devices  75.1 us
  transfers between devices with their start and end apart: 36, of which 32 were waited for; matrix products, arithmetic and copies ran while one was open for 12% of the time, Pallas kernels for 0%

commit v1 on v0

v1 whole, which is shorter than its diff:
```python
from functools import partial

import jax
import jax.numpy as jnp
from jax import lax
from jax.experimental import pallas as pl
from jax.experimental.pallas import tpu as pltpu
from jax.sharding import PartitionSpec as P

BF16 = jnp.bfloat16
F32 = jnp.float32
ROWS = (((0,), (0,)), ((), ()))
COLS = (((1,), (1,)), ((), ()))
PLAIN = (((1,), (0,)), ((), ()))
CROSS = ((0, 1), (1, 0))


def dot(left, right, dims=PLAIN):
    return lax.dot_general(left, right, dims, preferred_element_type=F32)


def swap(array, axis):
    return lax.ppermute(array, axis, CROSS)


def pair_swap(array, bit=1):
    return lax.ppermute(array, "dp", [(i, i ^ bit) for i in range(lax.axis_size("dp"))])


def ring_shift(array, by):
    ring = lax.axis_size("dp") // 2
    pairs = [(2 * z + x, 2 * ((z + by) % ring) + x) for z in range(ring) for x in (0, 1)]
    return lax.ppermute(array, "dp", pairs)


def added(left, right, kind=BF16):
    return (left.astype(F32) + right.astype(F32)).astype(kind)


class Line:
    def __init__(self, steps):
        self.steps, self.result, self.done = steps, None, False
        self.pending = next(steps)

    def advance(self, arrays):
        try:
            self.pending = self.steps.send(arrays)
        except StopIteration as end:
            self.result, self.done, self.pending = end.value, True, ()


def join(state, *lines):
    lines = [line for line in lines if not line.done]
    state, arrays = lax.optimization_barrier((state, [tuple(line.pending) for line in lines]))
    for line, own in zip(lines, arrays):
        line.advance(own)
    return state


def ring_gather(piece):
    ring = lax.axis_size("dp") // 2
    if ring <= 4:
        pieces = [piece]
        for _ in range(ring - 1):
            (piece,) = yield (ring_shift(pieces[-1], 1),)
            pieces.append(piece)
        return jnp.stack(pieces)

    def step(k, state):
        moving, held = state
        moving = ring_shift(moving, 1)
        return moving, lax.dynamic_update_index_in_dim(held, moving, k, 0)

    held = jnp.zeros((ring,) + piece.shape, piece.dtype).at[0].set(piece)
    return lax.fori_loop(1, ring, step, (piece, held))[1]


def ring_scatter(parts):
    ring = lax.axis_size("dp") // 2
    if ring <= 4:
        total = parts[ring - 1]
        for k in reversed(range(ring - 1)):
            (came,) = yield (ring_shift(total.astype(BF16), -1),)
            total = parts[k] + came.astype(F32)
        return total

    def step(k, total):
        mine = lax.dynamic_index_in_dim(parts, ring - 1 - k, 0, keepdims=False)
        return mine + ring_shift(total.astype(BF16), -1).astype(F32)

    return lax.fori_loop(1, ring, step, parts[ring - 1])


def copy_kernel(plan, count, *refs):
    sources, outs, sems = refs[:count], refs[count:-1], refs[-1]
    copies = []
    for source, (out, row) in zip(sources, plan):
        copies.append(
            pltpu.make_async_copy(
                source, outs[out].at[pl.ds(row, source.shape[0])], sems.at[len(copies)]
            )
        )
    for copy in copies:
        copy.start()
    for copy in copies:
        copy.wait()


def stack_rows(*groups):
    sources = [part for group in groups for part in group]
    plan, outs = [], []
    for index, group in enumerate(groups):
        row = 0
        for part in group:
            plan.append((index, row))
            row += part.shape[0]
        outs.append(jax.ShapeDtypeStruct((row,) + group[0].shape[1:], group[0].dtype))
    return pl.pallas_call(
        partial(copy_kernel, plan, len(sources)),
        out_shape=outs,
        in_specs=[pl.BlockSpec(memory_space=pl.ANY)] * len(sources),
        out_specs=[pl.BlockSpec(memory_space=pltpu.VMEM)] * len(outs),
        scratch_shapes=[pltpu.SemaphoreType.DMA((len(sources),))],
        compiler_params=pltpu.CompilerParams(vmem_limit_bytes=24 * 1024 * 1024),
        cost_estimate=pl.CostEstimate(
            flops=0, bytes_accessed=sum(4 * part.size for part in sources), transcendentals=0
        ),
        name="stack_rows",
    )(*sources)


def gather_chunk(piece):
    columns = piece.shape[1]
    ring = lax.axis_size("dp") // 2
    half = ring // 2
    near = yield from ring_gather(piece)
    over_x, over_y = yield (pair_swap(near), swap(near, "tensor"))
    first, second = yield (swap(over_x[:half], "tensor"), pair_swap(over_y[half:]))
    flat = lambda part: part.reshape(-1, columns)
    if piece.shape[0] % 16 == 0:
        mine = stack_rows([near, over_x, over_y, first, second])[0]
        mine = mine.reshape(2, -1, columns)
        (theirs,) = yield (swap(mine, "section"),)
        return stack_rows([mine[0], theirs[0]], [mine[1], theirs[1]])
    mine = jnp.concatenate([near, over_x, over_y, first, second]).reshape(2, -1, columns)
    (theirs,) = yield (swap(mine, "section"),)
    return [jnp.concatenate([mine[t], theirs[t]]) for t in (0, 1)]


def scatter_chunk(own, other):
    ring = lax.axis_size("dp") // 2
    half = ring // 2
    columns = own[0].shape[1]
    rows = own[0].shape[0] // (2 * ring)
    came = yield tuple(swap(part, "section") for part in other)
    quarter = ring * rows

    def part(dx, dy, low, high, kind):
        cut = slice(dx * quarter + low * rows, dx * quarter + high * rows)
        return added(own[dy][cut], came[dy][cut], kind).reshape(high - low, rows, columns)

    first, second = yield (
        swap(part(1, 1, 0, half, BF16), "tensor"),
        pair_swap(part(1, 1, half, ring, BF16)),
    )
    over_x = jnp.concatenate(
        [added(part(1, 0, 0, half, F32), first), part(1, 0, half, ring, BF16)]
    )
    over_y = jnp.concatenate(
        [part(0, 1, 0, half, BF16), added(part(0, 1, half, ring, F32), second)]
    )
    over_x, over_y = yield (pair_swap(over_x), swap(over_y, "tensor"))
    near = part(0, 0, 0, ring, F32) + over_x.astype(F32) + over_y.astype(F32)
    total = yield from ring_scatter(near)
    return total


def finish(line):
    while not line.done:
        join((), line)
    return line.result


def attend_kernel(scale, q_ref, k0_ref, k1_ref, v0_ref, v1_ref, b0_ref, b1_ref, o_ref, lse_ref):
    span = q_ref.shape[0]
    lane = lax.broadcasted_iota(jnp.int32, (span, 128), 1)
    q = q_ref[...]
    k0, k1 = k0_ref[...], k1_ref[...]
    v0, v1 = v0_ref[...], v1_ref[...]
    b0, b1 = b0_ref[...], b1_ref[...]
    outs = []
    for head in (0, 1):
        own = (lane >= 64 * head) & (lane < 64 * head + 64)
        qh = jnp.where(own, q * jnp.asarray(scale, BF16), jnp.zeros_like(q))
        s0 = dot(k0, qh, COLS) + b0
        s1 = dot(k1, qh, COLS) + b1
        peak = jnp.maximum(jnp.max(s0, 0, keepdims=True), jnp.max(s1, 0, keepdims=True))
        p0 = jnp.exp(s0 - peak)
        p1 = jnp.exp(s1 - peak)
        total = jnp.sum(p0, 0, keepdims=True) + jnp.sum(p1, 0, keepdims=True)
        out = dot(v0, p0.astype(BF16), ROWS) + dot(v1, p1.astype(BF16), ROWS)
        outs.append(out / total)
        lse_ref[0, head : head + 1, :] = peak + jnp.log(total)
    row = lax.broadcasted_iota(jnp.int32, (128, span), 0)
    o_ref[...] = jnp.where(row < 64, outs[0], outs[1]).T.astype(BF16)


def attend(mixed, other, biases):
    span, width = mixed.shape
    groups = width // (3 * 128)
    block = lambda first: pl.BlockSpec((span, 128), lambda g, first=first: (0, first * groups + g))
    bias = pl.BlockSpec((span, 1), lambda g: (0, 0))
    return pl.pallas_call(
        partial(attend_kernel, 0.125),
        grid=(groups,),
        out_shape=[
            jax.ShapeDtypeStruct((span, width // 3), BF16),
            jax.ShapeDtypeStruct((groups, 8, span), F32),
        ],
        in_specs=[block(0), block(1), block(0), block(2), block(1), bias, bias],
        out_specs=[block(0), pl.BlockSpec((1, 8, span), lambda g: (g, 0, 0))],
        compiler_params=pltpu.CompilerParams(vmem_limit_bytes=48 * 1024 * 1024),
        cost_estimate=pl.CostEstimate(
            flops=16 * groups * span * span * 2 * 128,
            bytes_accessed=8 * span * width,
            transcendentals=4 * groups * span * span,
        ),
        name="attend",
    )(mixed, mixed, other, mixed, other, *biases)


def attend_back_kernel(
    scale, q_ref, k0_ref, k1_ref, v0_ref, v1_ref, b0_ref, b1_ref, lse_ref, do_ref,
    dq_ref, dk0_ref, dk1_ref, dv0_ref, dv1_ref,
):
    span = q_ref.shape[0]
    lane = lax.broadcasted_iota(jnp.int32, (span, 128), 1)
    q, above = q_ref[...], do_ref[...]
    keys = (k0_ref[...], k1_ref[...])
    values = (v0_ref[...], v1_ref[...])
    biases = (b0_ref[...], b1_ref[...])
    dqs, dks, dvs = [], [], []
    for head in (0, 1):
        own = (lane >= 64 * head) & (lane < 64 * head + 64)
        qh = jnp.where(own, q * jnp.asarray(scale, BF16), jnp.zeros_like(q))
        ah = jnp.where(own, above, jnp.zeros_like(above))
        lse = lse_ref[0, head : head + 1, :]
        probs, pushed = [], []
        for part in (0, 1):
            probs.append(jnp.exp(dot(keys[part], qh, COLS) + biases[part] - lse))
            pushed.append(dot(values[part], ah, COLS))
        inner = jnp.sum(probs[0] * pushed[0], 0, keepdims=True) + jnp.sum(
            probs[1] * pushed[1], 0, keepdims=True
        )
        dq = None
        for part in (0, 1):
            slopes = (probs[part] * (pushed[part] - inner)).astype(BF16)
            piece = dot(keys[part], slopes, ROWS)
            dq = piece if dq is None else dq + piece
            dk = dot(slopes, qh)
            dv = dot(probs[part].astype(BF16), ah)
            if head == 0:
                dks.append(dk)
                dvs.append(dv)
            else:
                dks[part] = dks[part] + dk
                dvs[part] = dvs[part] + dv
        dqs.append(dq)
    row = lax.broadcasted_iota(jnp.int32, (128, span), 0)
    dq_ref[...] = (jnp.where(row < 64, dqs[0], dqs[1]) * scale).T.astype(BF16)
    dk0_ref[...] = dks[0].astype(BF16)
    dk1_ref[...] = dks[1].astype(BF16)
    dv0_ref[...] = dvs[0].astype(BF16)
    dv1_ref[...] = dvs[1].astype(BF16)


def attend_back(mixed, other, biases, lse, above):
    span, width = mixed.shape
    groups = width // (3 * 128)
    block = lambda first: pl.BlockSpec((span, 128), lambda g, first=first: (0, first * groups + g))
    bias = pl.BlockSpec((span, 1), lambda g: (0, 0))
    out = jax.ShapeDtypeStruct((span, width // 3), BF16)
    return pl.pallas_call(
        partial(attend_back_kernel, 0.125),
        grid=(groups,),
        out_shape=[out] * 5,
        in_specs=[block(0), block(1), block(0), block(2), block(1), bias, bias]
        + [pl.BlockSpec((1, 8, span), lambda g: (g, 0, 0)), block(0)],
        out_specs=[block(0)] * 5,
        compiler_params=pltpu.CompilerParams(vmem_limit_bytes=56 * 1024 * 1024),
        cost_estimate=pl.CostEstimate(
            flops=40 * groups * span * span * 2 * 128,
            bytes_accessed=12 * span * width,
            transcendentals=4 * groups * span * span,
        ),
        name="attend_back",
    )(mixed, mixed, other, mixed, other, *biases, lse, above)


def layer_norm(values, gain, shift):
    centre = jnp.mean(values, -1, keepdims=True)
    centred = values - centre
    spread = jnp.mean(centred * centred, -1, keepdims=True)
    return centred * lax.rsqrt(spread + 1e-05) * (1.0 + gain) + shift


def attention_forward(values, w_a, table, biases):
    third = w_a[0].shape[-1] // 4
    normed = layer_norm(values, table[0], table[1]).astype(BF16)
    mixed, other = [], []
    for t in (0, 1):
        cut = slice(t * third, (t + 1) * third)
        bias = jnp.concatenate([table[2, cut], jnp.zeros((third,), F32), table[3, cut]])
        mixed.append((dot(normed, w_a[t][:, : 3 * third]) + bias).astype(BF16))
        other.append(swap(mixed[t][:, third:], "section"))
    attended, logs = [], []
    for t in (0, 1):
        o, lse = attend(mixed[t], other[t], biases)
        attended.append(o)
        logs.append(lse)
    return normed, mixed, other, attended, logs


def middle_forward(values, attended, w_a, table):
    third = w_a[0].shape[-1] // 4
    branch = sum(dot(attended[t], w_a[t][:, 3 * third :], COLS) for t in (0, 1))
    middle = values + branch + table[4]
    return middle, layer_norm(middle, table[5], table[6]).astype(BF16)


def hidden_forward(normed_two, w_b, table):
    rise = table[8:12].reshape(2, -1)
    hidden, slope = [], []
    for t in (0, 1):
        before = dot(normed_two, w_b[t]) + rise[t]
        share = 0.5 * (1.0 + lax.erf(before * (0.5**0.5)))
        hidden.append((before * share).astype(BF16))
        bell = jnp.exp(-0.5 * before * before) * 0.3989422804014327
        slope.append((share + before * bell).astype(BF16))
    return hidden, slope


def hidden_down(middle, hidden, w_c, table):
    return middle + sum(dot(hidden[t], w_c[t], COLS) for t in (0, 1)) + table[7]


def by_core(left, rights):
    half = left.shape[1] // 2
    return [
        [dot(left[:, cut], right, ROWS).astype(BF16) for right in rights]
        for cut in (slice(0, half), slice(half, None))
    ]


def hidden_back(incoming, w_c, slope):
    short = incoming.astype(BF16)
    return [(dot(short, w_c[t]) * slope[t].astype(F32)).astype(BF16) for t in (0, 1)]


def middle_back(incoming, pushed, middle, w_a, w_b, table):
    third = w_a[0].shape[-1] // 4
    grad_normed = sum(dot(pushed[t], w_b[t], COLS) for t in (0, 1))
    _, back = jax.vjp(layer_norm, middle, table[5], table[6])
    grad_mid, gain, shift = back(grad_normed)
    grad_middle = incoming + grad_mid
    proj_in = grad_middle.astype(BF16)
    above = [dot(proj_in, w_a[t][:, 3 * third :]).astype(BF16) for t in (0, 1)]
    return grad_middle, proj_in, above, gain, shift


def input_back(grad_middle, flats, values, w_a, table):
    third = w_a[0].shape[-1] // 4
    grad_normed = sum(dot(flats[t], w_a[t][:, : 3 * third], COLS) for t in (0, 1))
    _, back = jax.vjp(layer_norm, values, table[0], table[1])
    grad_input, gain, shift = back(grad_normed)
    return grad_middle + grad_input, gain, shift


def table_back(incoming, pushed, grad_middle, flats, gains):
    third = flats[0].shape[1] // 3
    sums = [jnp.sum(flat, 0, dtype=F32) for flat in flats]
    rows = [
        gains[0],
        gains[1],
        jnp.concatenate([part[:third] for part in sums]),
        jnp.concatenate([part[2 * third :] for part in sums]),
        jnp.sum(grad_middle, 0),
        gains[2],
        gains[3],
        jnp.sum(incoming, 0),
    ]
    rise = jnp.concatenate([jnp.sum(part, 0, dtype=F32) for part in pushed]).reshape(4, -1)
    return jnp.concatenate([jnp.stack(rows), rise])


def attention_back(mixed, other, biases, logs, above):
    dq, dk, dk_far, dv, dv_far = attend_back(mixed, other, biases, logs, above)
    far = swap(jnp.concatenate([dk_far, dv_far], 1), "section")
    return dq, jnp.concatenate([dk, dv], 1), far


def far_back(parts):
    query, near, far = parts
    return jnp.concatenate([query, added(near, far)], 1)


def beside(left, right):
    return [[jnp.concatenate(pair, 1) for pair in zip(*sides)] for sides in zip(left, right)]


def iter_swaps(rows, first, side, core):
    span, width = rows.shape
    (came,) = yield (lax.ppermute(rows.astype(BF16), "section", [(1 - core, core)]),)
    came = came.astype(F32)
    full = jnp.stack([rows, came] if core == 0 else [came, rows])
    keep = lax.dynamic_index_in_dim(full, side, 0, keepdims=False)
    gone = lax.dynamic_index_in_dim(full, 1 - side, 0, keepdims=False).astype(BF16)
    pairs = [(2 * core, 2 * core + 1), (2 * core + 1, 2 * core)]
    (came,) = yield (lax.ppermute(gone, ("section", "tensor"), pairs),)
    came = came.astype(F32)
    return jnp.where(side == 0, jnp.stack([keep, came]), jnp.stack([came, keep]))


def iter_tables(tables, count):
    (came,) = yield (swap(tables, "section"),)
    tables = tables + came
    (came,) = yield (swap(tables, "tensor"),)
    tables = tables + came
    bit = 1
    while bit < count:
        (came,) = yield (pair_swap(tables, bit),)
        tables = tables + came
        bit *= 2
    return tables


FEATURE_ROWS = (True, True, False, False, True, True, True, True, False, False, False, False)


def body(ends_in, lengths, vectors, w_qkv, w_out, w_up, w_down):
    core = lax.axis_index("section")
    first = core == 0
    side = lax.axis_index("tensor")
    count = lax.axis_size("dp")
    ring = count // 2
    rows = w_qkv.shape[1]
    half = rows // 2
    span, width = ends_in.shape[2:]
    third, unit = w_qkv.shape[-1], w_up.shape[-1]

    at = jnp.arange(width, dtype=jnp.int32)
    row, rest = at % half, at // half
    step, rest = rest % ring, rest // ring
    spot = lax.axis_index("dp")
    owner = 2 * ((spot // 2 - step + ring) % ring) + (spot % 2 + rest % 2) % 2
    source = owner * rows + ((core + rest // 2) % 2) * half + row
    order = at[:, None] == source[None, :]
    order_low = order.astype(BF16)

    def to_own(array):
        return jnp.dot(array, order.astype(F32), precision=lax.Precision.HIGHEST)

    def from_own(array):
        return lax.dot_general(array, order.astype(F32), COLS, precision=lax.Precision.HIGHEST)

    keep = lax.dynamic_index_in_dim(ends_in[0], side, 0, keepdims=False)
    gone = lax.dynamic_index_in_dim(ends_in[0], 1 - side, 0, keepdims=False)
    came = swap(gone, "tensor")
    upper, lower = jnp.where(side == 0, keep, came), jnp.where(side == 0, came, keep)
    stay, leave = jnp.where(first, upper, lower), jnp.where(first, lower, upper)
    came = swap(leave, "section")
    values = dot(jnp.where(first, stay, came), order_low)
    upstream = dot(jnp.where(first, came, stay), order_low)
    frames = lax.dynamic_index_in_dim(lengths, side, 0, keepdims=False)
    spots = lax.broadcasted_iota(jnp.int32, (span, 1), 0)
    biases = [
        jnp.where(spots + offset * span < frames, 0.0, -1e30).astype(F32)
        for offset in (core, 1 - core)
    ]

    index = spot * 2 + side
    cut = vectors.shape[-1]
    spread = lax.dynamic_update_slice_in_dim(
        jnp.zeros((vectors.shape[1], width), F32), vectors[0], index * cut, 1
    )
    spread = spread + swap(spread, "tensor")
    bit = 1
    while bit < count:
        spread = spread + pair_swap(spread, bit)
        bit *= 2
    theirs = swap(spread, "section")
    is_feature = jnp.array(FEATURE_ROWS)[:, None]

    def own_table(table):
        heads = jnp.roll(table[:8].reshape(8, 2, -1), side, 1).reshape(8, width)
        rise = jnp.roll(table[8:].reshape(2, 2, width), side, 0).reshape(4, width)
        return jnp.where(is_feature, to_own(table), jnp.concatenate([heads, rise]))

    def plain_table(table):
        heads = jnp.roll(table[:8].reshape(8, 2, -1), side, 1).reshape(8, width)
        rise = jnp.roll(table[8:].reshape(2, 2, width), side, 0).reshape(4, width)
        return jnp.where(is_feature, from_own(table), jnp.concatenate([heads, rise]))

    tables = [
        own_table(jnp.where(first, spread, theirs)),
        own_table(jnp.where(first, theirs, spread)),
    ]

    own = jnp.concatenate([w_qkv[0].reshape(rows, -1), w_out[0].T, w_up[0], w_down[0].T], 1)
    halves = (own[:half], own[half:])
    came = swap(jnp.where(first, halves[1], halves[0]), "section")
    one, two = jnp.where(first, halves[0], came), jnp.where(first, came, halves[1])
    cuts = [slice(n * unit, (n + 1) * unit) for n in range(3)]
    chunks = [layer[:, c] for layer in (one, two) for c in cuts]

    a0 = Line(gather_chunk(chunks[0]))
    join((), a0)
    join((), a0)
    ready = join(chunks[1], a0)
    b0 = Line(gather_chunk(ready))
    join((), b0)
    join((), b0)
    ready, *_ = join((chunks[2],), a0, b0)
    c0 = Line(gather_chunk(ready))
    join((), c0)
    join((), c0)
    (ready,) = join((chunks[3],), a0, b0, c0)
    a1 = Line(gather_chunk(ready))
    join((), a0)
    w_a0 = a0.result
    normed_0, mixed_0, other_0, attended_0, logs_0 = attention_forward(
        values, w_a0, tables[0], biases
    )
    join((), a1)
    join((), a1)
    attended_0, ready = join((attended_0, chunks[4]), b0, c0, a1)
    b1 = Line(gather_chunk(ready))
    middle_0, short_0 = middle_forward(values, attended_0, w_a0, tables[0])
    short_0 = join(short_0, b0)
    w_b0 = b0.result
    hidden_0, slope_0 = hidden_forward(short_0, w_b0, tables[0])
    join((), b1)
    join((), b1)
    hidden_0, slope_0, ready = join((hidden_0, slope_0, chunks[5]), c0, a1, b1)
    c1 = Line(gather_chunk(ready))
    hidden_0 = join(hidden_0, c0)
    w_c0 = c0.result
    layer_one = hidden_down(middle_0, hidden_0, w_c0, tables[0])
    join((), c1)
    join((), c1)
    layer_one = join(layer_one, a1, b1, c1)
    layer_one = join(layer_one, a1)
    w_a1 = a1.result
    normed_1, mixed_1, other_1, attended_1, logs_1 = attention_forward(
        layer_one, w_a1, tables[1], biases
    )
    attended_1 = join(attended_1, b1, c1)
    middle_1, short_1 = middle_forward(layer_one, attended_1, w_a1, tables[1])
    short_1 = join(short_1, b1)
    w_b1 = b1.result
    hidden_1, slope_1 = hidden_forward(short_1, w_b1, tables[1])
    grad_c = by_core(upstream.astype(BF16), hidden_1)
    grad_c = join(grad_c, c1)
    sc1 = Line(scatter_chunk(*grad_c))
    w_c1 = finish(c1)
    result = hidden_down(middle_1, hidden_1, w_c1, tables[1])
    result = from_own(result)
    pushed_1 = hidden_back(upstream, w_c1, slope_1)
    pushed_1 = join(pushed_1, sc1)

    out = Line(iter_swaps(result, first, side, 1))
    grad_b = by_core(short_1, pushed_1)
    grad_mid_1, proj_1, above_1, gain_1, shift_1 = middle_back(
        upstream, pushed_1, middle_1, w_a1, w_b1, tables[1]
    )
    grad_o = by_core(proj_1, attended_1)
    grad_b, grad_o, above_1 = join((grad_b, grad_o, above_1), sc1, out)
    sb1 = Line(scatter_chunk(*beside(grad_b, grad_o)))
    flat_a = attention_back(mixed_1[0], other_1[0], biases, logs_1[0], above_1[0])
    flat_a, up = join((flat_a, above_1[1]), sc1, sb1)
    flat_b = attention_back(mixed_1[1], other_1[1], biases, logs_1[1], up)
    flat_a = far_back(flat_a)
    flat_a, flat_b = join((flat_a, flat_b), sc1, sb1, out)
    flats_1 = [flat_a, far_back(flat_b)]
    grad_q = by_core(normed_1, flats_1)
    grad_q, flats_1 = join((grad_q, flats_1), sc1)
    sq1 = Line(scatter_chunk(*grad_q))
    grad_layer, gain_1a, shift_1a = input_back(grad_mid_1, flats_1, layer_one, w_a1, tables[1])
    grad_layer = join(grad_layer, sc1, sb1, sq1)
    table_1 = table_back(upstream, pushed_1, grad_mid_1, flats_1, (gain_1a, shift_1a, gain_1, shift_1))

    grad_c = by_core(grad_layer.astype(BF16), hidden_0)
    grad_c = join(grad_c, sb1, sq1)
    sc0 = Line(scatter_chunk(*grad_c))
    pushed_0 = hidden_back(grad_layer, w_c0, slope_0)
    pushed_0 = join(pushed_0, sc0, sb1)
    grad_b = by_core(short_0, pushed_0)
    grad_mid_0, proj_0, above_0, gain_0, shift_0 = middle_back(
        grad_layer, pushed_0, middle_0, w_a0, w_b0, tables[0]
    )
    grad_o = by_core(proj_0, attended_0)
    grad_b, grad_o, above_0 = join((grad_b, grad_o, above_0), sc0, sq1, sb1)
    sb0 = Line(scatter_chunk(*beside(grad_b, grad_o)))
    flat_a = attention_back(mixed_0[0], other_0[0], biases, logs_0[0], above_0[0])
    flat_a, up = join((flat_a, above_0[1]), sc0, sb0, sq1)
    flat_b = attention_back(mixed_0[1], other_0[1], biases, logs_0[1], up)
    flat_a = far_back(flat_a)
    flat_a, flat_b = join((flat_a, flat_b), sc0, sb0, sq1)
    flats_0 = [flat_a, far_back(flat_b)]
    grad_q = by_core(normed_0, flats_0)
    grad_q, flats_0 = join((grad_q, flats_0), sc0)
    sq0 = Line(scatter_chunk(*grad_q))
    grad_values, gain_0a, shift_0a = input_back(grad_mid_0, flats_0, values, w_a0, tables[0])
    table_0 = table_back(grad_layer, pushed_0, grad_mid_0, flats_0, (gain_0a, shift_0a, gain_0, shift_0))
    grad_values = from_own(grad_values)
    grad_values = join(grad_values, sc0, sb0, sq0)
    into = Line(iter_swaps(grad_values, first, side, 0))
    tables_back = Line(iter_tables(jnp.stack([plain_table(table_0), plain_table(table_1)]), count))
    join((), into, tables_back, sq0, sb0)
    lines = [into, out, tables_back, sq0, sb0, sc0, sq1, sb1, sc1]
    while any(not line.done for line in lines):
        join((), *lines)

    boundary = jnp.where(first, into.result, out.result)

    sums_one = (sq0.result, sb0.result, sc0.result)
    sums_two = (sq1.result, sb1.result, sc1.result)
    grads = []
    for one, two in zip(sums_one, sums_two):
        lower = lax.ppermute(one.astype(BF16), "section", [(1, 0)]).astype(F32)
        upper = lax.ppermute(two.astype(BF16), "section", [(0, 1)]).astype(F32)
        grads.append(
            jnp.where(first, jnp.concatenate([one, lower]), jnp.concatenate([upper, two]))
        )
    table_grad = lax.dynamic_index_in_dim(tables_back.result, core, 0, keepdims=False)
    table_grad = lax.dynamic_slice_in_dim(table_grad, index * cut, cut, 1)
    return (
        boundary[None],
        table_grad[None],
        grads[0].reshape(w_qkv.shape),
        grads[1][:, unit:].T[None],
        grads[1][None, :, :unit],
        grads[2].T[None],
    )


def solution(mesh):
    in_specs = (
        P("section", "dp", "tensor", None),
        P("dp"),
        P("section", None, ("dp", "tensor")),
        P("section", "dp", None, "tensor"),
        P("section", "tensor", "dp"),
        P("section", "dp", "tensor"),
        P("section", "tensor", "dp"),
    )
    out_specs = (
        P("section", "dp", "tensor", None),
        P("section", None, ("dp", "tensor")),
        P("section", "dp", None, "tensor"),
        P("section", "tensor", "dp"),
        P("section", "dp", "tensor"),
        P("section", "tensor", "dp"),
    )
    return jax.shard_map(body, mesh=mesh, in_specs=in_specs, out_specs=out_specs, check_vma=False)
```

time: 1860 us -> 692 us (0.37)
  waiting for transfers between devices: 1010 us -> 129 us
  matrix products: 369 us -> 121 us
  starting transfers between devices: 11.9 us -> 143 us
  local copies, waits for them, and re-layouts: 184 us -> 82.9 us
  Pallas kernels: 0 us -> 89.7 us
  other arithmetic: 193 us -> 110 us
  blocking collectives: 65.7 us -> 0 us
    reduce_scatter x16 -> x0, waiting for transfers between devices: 620 us -> none  [the longest x6 140 us: project_rows(): lax.psum_scatter(jnp.dot(block, right, preferred_element_type=jnp.float32...]
    all_gather x15 -> x0, waiting for transfers between devices: 305 us -> none  [the longest x6 134 us: gather_rows(): return lax.all_gather(values, 'tensor', axis=0, tiled=True)]
    dot_general x162 -> x72, matrix products: 369 us -> 121 us  [the longest x66 108 us: dot(): return lax.dot_general(left, right, dims, preferred_element_type=F32)]
    ppermute x4 -> x133, starting transfers between devices: 7.96 us -> 143 us  [the longest x57 74 us: swap(): return lax.ppermute(array, axis, CROSS)]
    ppermute x4 -> x133, waiting for transfers between devices: 9.45 us -> 129 us  [the longest x36 56.2 us: ring_shift(): return lax.ppermute(array, 'dp', pairs)]
    pallas_call x0 -> x20, Pallas kernels: none -> 89.7 us  [the longest x4 50.4 us: attend_back(): pl.pallas_call(partial(attend_back_kernel, 0.125), grid=(groups,), out_sh...]
    unnamed x33 -> x0, waiting for transfers between devices: 75.1 us -> none
    all_gather x2 -> x0, blocking collectives: 65.7 us -> none  [the longest x1 38.5 us: body(): table = lax.all_gather(vectors[0], ('dp', 'tensor'), axis=1, tiled=True)]
  transfers between devices with their start and end apart: 36 -> 133, of which waited for: 32 -> 38; matrix products, arithmetic and copies ran while one was open for 12% -> 31% of each run, Pallas kernels for 0% -> 12%
where the time goes in v1:
time: 692 us; the launch traced here: 680 us
  starting transfers between devices  143 us (21%)
  waiting for transfers between devices  129 us (19%)
  matrix products  121 us (17%)
  other arithmetic  110 us (16%)
  Pallas kernels  89.7 us (13%)
  local copies, waits for them, and re-layouts  82.9 us (12%)
    dot_general x66, matrix products, dot(): return lax.dot_general(left, right, dims, preferred_element_type=F32)  108 us
    ppermute x57, starting transfers between devices, swap(): return lax.ppermute(array, axis, CROSS)  74 us
    ppermute x36, waiting for transfers between devices, ring_shift(): return lax.ppermute(array, 'dp', pairs)  56.2 us
    pallas_call x4, Pallas kernels, attend_back(): pl.pallas_call(partial(attend_back_kernel, 0.125), grid=(groups,), out_sh...  50.4 us
    ppermute x30, waiting for transfers between devices, pair_swap(): lax.ppermute(array, 'dp', [(i, i ^ bit) for i in range(lax.axis_size('dp'...  34.6 us
    unnamed x471, local copies, waits for them, and re-layouts  30.3 us
    pallas_call x4, Pallas kernels, attend(): pl.pallas_call(partial(attend_kernel, 0.125), grid=(groups,), out_shape=[...  29.9 us
    ppermute x57, waiting for transfers between devices, swap(): return lax.ppermute(array, axis, CROSS)  28.5 us
  transfers between devices with their start and end apart: 133, of which 38 were waited for; matrix products, arithmetic and copies ran while one was open for 31% of the time, Pallas kernels for 12%

profile of v1, /device:TPU:1, one launch (start us, length us, event | category | flops | bytes accessed | tf_op | source)
XLA Modules:
  0.0 680.4 jit_solution(12663935506167690232)
XLA Ops:
  22.2 4.3 collective-permute-start.6
  27.5 5.8 collective-permute-done.10
  34.7 4.3 collective-permute-done.13
  41.2 3.6 collective-permute-done.14
  44.9 5.7 collective-permute-done.15
  58.5 8.1 %collective-permute-start.1 = (bf16[512,768]{1,0:T(8,128)(2,1)S(1)}, bf16[512,768]{1,0:T(8,128)(2,1)S(1)}, u32[]{:S(2)}, u32[]{:S(2)}) collective-permute-start(bf16[512,768]{1,0:T(8,128)(2,1)S(1)} %get-tuple-element.512), channel_id=1, source_target_pairs={{0,16},{16,0},{1,17},{17,1},{2,18},{18,2},{3,19},{19,3},{4,20},{20... | collective-permute-start | bytes 2359304 | tf_op jit(solution)/shard_map/ppermute | solution.py:23
  69.0 3.7 collective-permute-done.16.refs_3_
  74.7 7.9 %collective-permute-start.23 = (bf16[2,384,1536]{2,1,0:T(8,128)(2,1)S(1)}, bf16[2,384,1536]{2,1,0:T(8,128)(2,1)S(1)}, u32[]{:S(2)}, u32[]{:S(2)}) collective-permute-start(bf16[2,384,1536]{2,1,0:T(8,128)(2,1)S(1)} %bitcast.369), channel_id=1, source_target_pairs={{0,16},{16,0},{1,17},{17,1},{2,18},{18,2},{3,19},{19,3},{4,20},{20... | collective-permute-start | bytes 7077896 | tf_op jit(solution)/shard_map/ppermute | solution.py:23
  97.3 6.1 collective-permute-done.30
  105.3 4.7 collective-permute-done.31
  111.5 7.4 %attend.4 = (bf16[512,384]{1,0:T(8,128)(2,1)S(1)}, f32[3,8,512]{2,1,0:T(8,128)S(1)}) custom-call(bf16[512,1152]{1,0:T(8,128)(2,1)S(1)} %copy-done.9, bf16[512,1152]{1,0:T(8,128)(2,1)S(1)} %copy-done.9, bf16[512,768]{1,0:T(8,128)(2,1)} %collective-permute-done.24.k1_ref.v1_ref, bf16[512,1152]{1,0:T(8,128)(2,1)S(1)} %copy-done.9, ...), custom_call_target="tpu_custom_call" | custom-call | flops 3221225472 | bytes 4718592 | tf_op jit(solution)/shard_map/attend/pallas_call | solution.py:213
  119.5 7.5 %attend.5 = (bf16[512,384]{1,0:T(8,128)(2,1)S(1)}, f32[3,8,512]{2,1,0:T(8,128)S(1)}) custom-call(bf16[512,1152]{1,0:T(8,128)(2,1)S(1)} %fusion.26.q_ref.k0_ref.v0_ref, bf16[512,1152]{1,0:T(8,128)(2,1)S(1)} %fusion.26.q_ref.k0_ref.v0_ref, bf16[512,768]{1,0:T(8,128)(2,1)} %collective-permute-done.25.k1_ref.v1_ref, ...), custom_call_target="tpu_custom_call" | custom-call | flops 3221225472 | bytes 4718592 | tf_op jit(solution)/shard_map/attend/pallas_call | solution.py:213
  141.1 5.5 collective-permute-done.39
  161.1 4.3 collective-permute-done.41
  166.5 5.1 collective-permute-done.42
  209.1 7.4 %attend.7 = (bf16[512,384]{1,0:T(8,128)(2,1)S(1)}, f32[3,8,512]{2,1,0:T(8,128)S(1)}) custom-call(bf16[512,1152]{1,0:T(8,128)(2,1)S(1)} %fusion.28.q_ref.k0_ref.v0_ref, bf16[512,1152]{1,0:T(8,128)(2,1)S(1)} %fusion.28.q_ref.k0_ref.v0_ref, bf16[512,768]{1,0:T(8,128)(2,1)} %collective-permute-done.51.k1_ref.v1_ref, ...), custom_call_target="tpu_custom_call" | custom-call | flops 3221225472 | bytes 4718592 | tf_op jit(solution)/shard_map/attend/pallas_call | solution.py:213
  216.6 7.6 %attend.6 = (bf16[512,384]{1,0:T(8,128)(2,1)S(1)}, f32[3,8,512]{2,1,0:T(8,128)S(1)}) custom-call(bf16[512,1152]{1,0:T(8,128)(2,1)S(1)} %fusion.27.q_ref.k0_ref.v0_ref, bf16[512,1152]{1,0:T(8,128)(2,1)S(1)} %fusion.27.q_ref.k0_ref.v0_ref, bf16[512,768]{1,0:T(8,128)(2,1)} %collective-permute-done.50.k1_ref.v1_ref, ...), custom_call_target="tpu_custom_call" | custom-call | flops 3221225472 | bytes 4718592 | tf_op jit(solution)/shard_map/attend/pallas_call | solution.py:213
  256.6 6.1 collective-permute-done.59
  323.7 12.9 %attend_back.4 = (bf16[512,384]{1,0:T(8,128)(2,1)}, bf16[512,384]{1,0:T(8,128)(2,1)}, bf16[512,384]{1,0:T(8,128)(2,1)}, bf16[512,384]{1,0:T(8,128)(2,1)}, bf16[512,384]{1,0:T(8,128)(2,1)}) custom-call(bf16[512,1152]{1,0:T(8,128)(2,1)} %copy-done.11, bf16[512,1152]{1,0:T(8,128)(2,1)} %copy-done.11, bf16[512,768]{1,0:T(8,128)(2,1)} %collective-permute-done.50.k1_ref.v1_ref, ...), custom_call_target="tpu_custom_call" | custom-call | flops 8053063680 | bytes 7077888 | tf_op jit(solution)/shard_map/attend_back/pallas_call | solution.py:283
  356.5 12.4 %attend_back.5 = (bf16[512,384]{1,0:T(8,128)(2,1)}, bf16[512,384]{1,0:T(8,128)(2,1)}, bf16[512,384]{1,0:T(8,128)(2,1)}, bf16[512,384]{1,0:T(8,128)(2,1)}, bf16[512,384]{1,0:T(8,128)(2,1)}) custom-call(bf16[512,1152]{1,0:T(8,128)(2,1)} %copy-done.10, bf16[512,1152]{1,0:T(8,128)(2,1)} %copy-done.10, bf16[512,768]{1,0:T(8,128)(2,1)} %collective-permute-done.51.k1_ref.v1_ref, ...), custom_call_target="tpu_custom_call" | custom-call | flops 8053063680 | bytes 7077888 | tf_op jit(solution)/shard_map/attend_back/pallas_call | solution.py:283
  375.3 7.2 %collective-permute-done.73 = bf16[2,48,1920]{2,1,0:T(8,128)(2,1)S(1)} collective-permute-done((bf16[2,48,1920]{2,1,0:T(8,128)(2,1)S(1)}, bf16[2,48,1920]{2,1,0:T(8,128)(2,1)S(1)}, u32[]{:S(2)}, u32[]{:S(2)}) %collective-permute-start.73) | collective-permute-done | bytes 368672 | tf_op jit(solution)/shard_map/ppermute | solution.py:27
  431.7 3.7 collective-permute-start.84
  499.0 12.4 %attend_back.6 = (bf16[512,384]{1,0:T(8,128)(2,1)}, bf16[512,384]{1,0:T(8,128)(2,1)}, bf16[512,384]{1,0:T(8,128)(2,1)}, bf16[512,384]{1,0:T(8,128)(2,1)}, bf16[512,384]{1,0:T(8,128)(2,1)}) custom-call(bf16[512,1152]{1,0:T(8,128)(2,1)} %copy-done.8, bf16[512,1152]{1,0:T(8,128)(2,1)} %copy-done.8, bf16[512,768]{1,0:T(8,128)(2,1)} %collective-permute-done.24.k1_ref.v1_ref, ...), custom_call_target="tpu_custom_call" | custom-call | flops 8053063680 | bytes 7077888 | tf_op jit(solution)/shard_map/attend_back/pallas_call | solution.py:283
  512.7 3.7 collective-permute-start.92
  524.4 11.3 %collective-permute-done.93 = bf16[4,48,1536]{2,1,0:T(8,128)(2,1)S(1)} collective-permute-done((bf16[4,48,1536]{2,1,0:T(8,128)(2,1)S(1)}, bf16[4,48,1536]{2,1,0:T(8,128)(2,1)S(1)}, u32[]{:S(2)}, u32[]{:S(2)}) %collective-permute-start.93) | collective-permute-done | bytes 589856 | tf_op jit(solution)/shard_map/ppermute | solution.py:27
  540.8 12.7 %attend_back.7 = (bf16[512,384]{1,0:T(8,128)(2,1)}, bf16[512,384]{1,0:T(8,128)(2,1)}, bf16[512,384]{1,0:T(8,128)(2,1)}, bf16[512,384]{1,0:T(8,128)(2,1)}, bf16[512,384]{1,0:T(8,128)(2,1)}) custom-call(bf16[512,1152]{1,0:T(8,128)(2,1)} %copy-done.7, bf16[512,1152]{1,0:T(8,128)(2,1)} %copy-done.7, bf16[512,768]{1,0:T(8,128)(2,1)} %collective-permute-done.25.k1_ref.v1_ref, ...), custom_call_target="tpu_custom_call" | custom-call | flops 8053063680 | bytes 7077888 | tf_op jit(solution)/shard_map/attend_back/pallas_call | solution.py:283
  559.6 7.0 %collective-permute-done.101 = bf16[2,48,1920]{2,1,0:T(8,128)(2,1)S(1)} collective-permute-done((bf16[2,48,1920]{2,1,0:T(8,128)(2,1)S(1)}, bf16[2,48,1920]{2,1,0:T(8,128)(2,1)S(1)}, u32[]{:S(2)}, u32[]{:S(2)}) %collective-permute-start.101) | collective-permute-done | bytes 368672 | tf_op jit(solution)/shard_map/ppermute | solution.py:27
  590.0 3.8 collective-permute-start.104
  628.8 9.5 %collective-permute-done.115 = f32[2,12,768]{2,1,0:T(8,128)S(1)} collective-permute-done((f32[2,12,768]{2,1,0:T(8,128)S(1)}, f32[2,12,768]{2,1,0:T(8,128)S(1)}, u32[]{:S(2)}, u32[]{:S(2)}) %collective-permute-start.115) | collective-permute-done | bytes 73760 | tf_op jit(solution)/shard_map/ppermute | solution.py:23
  646.1 9.4 %collective-permute-done.128 = bf16[48,1152]{1,0:T(8,128)(2,1)} collective-permute-done((bf16[48,1152]{1,0:T(8,128)(2,1)}, bf16[48,1152]{1,0:T(8,128)(2,1)}, u32[]{:S(2)}, u32[]{:S(2)}) %collective-permute-start.128) | collective-permute-done | bytes 110624 | tf_op jit(solution)/shard_map/ppermute | solution.py:631
  661.3 6.5 collective-permute-start.129
  673.7 4.4 collective-permute-start.127
  (1098 shorter events, 453.6 us)
Async XLA Ops:
  15.1 41.8 %collective-permute-start = (bf16[512,768]{1,0:T(8,128)(2,1)}, bf16[512,768]{1,0:T(8,128)(2,1)}, u32[]{:S(2)}, u32[]{:S(2)}) collective-permute-start(bf16[512,768]{1,0:T(8,128)(2,1)} %dynamic-slice_bitcast_fusion), channel_id=1, source_target_pairs={{0,1},{1,0},{2,3},{3,2},{4,5},{5,4},{6,7},{7,6},{8,9},{9,8},{10,11... | collective-permute-start | bytes 2359304 | tf_op jit(solution)/shard_map/ppermute | solution.py:23
  51.6 22.4 %collective-permute-start.19 = (bf16[4,48,1536]{2,1,0:T(8,128)(2,1)S(1)}, bf16[4,48,1536]{2,1,0:T(8,128)(2,1)S(1)}, u32[]{:S(2)}, u32[]{:S(2)}) collective-permute-start(bf16[4,48,1536]{2,1,0:T(8,128)(2,1)S(1)} %pad_maximum_fusion.22.refs_0_), channel_id=1, source_target_pairs={{0,1},{1,0},{2,3},{3,2},{4,5},{5,4},{6,7},{7,6},{8,9},{9,8},{10,11... | collective-permute-start | bytes 1769480 | tf_op jit(solution)/shard_map/ppermute | solution.py:23
  53.0 21.1 %collective-permute-start.18 = (bf16[4,48,1536]{2,1,0:T(8,128)(2,1)S(1)}, bf16[4,48,1536]{2,1,0:T(8,128)(2,1)S(1)}, u32[]{:S(2)}, u32[]{:S(2)}) collective-permute-start(bf16[4,48,1536]{2,1,0:T(8,128)(2,1)S(1)} %pad_maximum_fusion.22.refs_0_), channel_id=1, source_target_pairs={{0,2},{2,0},{4,6},{6,4},{8,10},{10,8},{12,14},{14,12},{1,3},{3,1},... | collective-permute-start | bytes 1769480 | tf_op jit(solution)/shard_map/ppermute | solution.py:27
  58.5 26.3 %collective-permute-start.1 = (bf16[512,768]{1,0:T(8,128)(2,1)S(1)}, bf16[512,768]{1,0:T(8,128)(2,1)S(1)}, u32[]{:S(2)}, u32[]{:S(2)}) collective-permute-start(bf16[512,768]{1,0:T(8,128)(2,1)S(1)} %get-tuple-element.512), channel_id=1, source_target_pairs={{0,16},{16,0},{1,17},{17,1},{2,18},{18,2},{3,19},{19,3},{4,20},{20... | collective-permute-start | bytes 2359304 | tf_op jit(solution)/shard_map/ppermute | solution.py:23
  94.4 25.1 %collective-permute-start.25 = (bf16[512,768]{1,0:T(8,128)(2,1)}, bf16[512,768]{1,0:T(8,128)(2,1)}, u32[]{:S(2)}, u32[]{:S(2)}) collective-permute-start(bf16[512,768]{1,0:T(8,128)(2,1)} %slice.947), channel_id=1, source_target_pairs={{0,16},{16,0},{1,17},{17,1},{2,18},{18,2},{3,19},{19,3},{4,20},{20... | collective-permute-start | bytes 2359304 | tf_op jit(solution)/shard_map/ppermute | solution.py:23
  104.7 22.3 %collective-permute-start.29 = (bf16[4,48,1536]{2,1,0:T(8,128)(2,1)S(1)}, bf16[4,48,1536]{2,1,0:T(8,128)(2,1)S(1)}, u32[]{:S(2)}, u32[]{:S(2)}) collective-permute-start(bf16[4,48,1536]{2,1,0:T(8,128)(2,1)S(1)} %pad_maximum_fusion.23.refs_0_), channel_id=1, source_target_pairs={{0,1},{1,0},{2,3},{3,2},{4,5},{5,4},{6,7},{7,6},{8,9},{9,8},{10,11... | collective-permute-start | bytes 1769480 | tf_op jit(solution)/shard_map/ppermute | solution.py:23
  105.0 22.0 %collective-permute-start.28 = (bf16[4,48,1536]{2,1,0:T(8,128)(2,1)S(1)}, bf16[4,48,1536]{2,1,0:T(8,128)(2,1)S(1)}, u32[]{:S(2)}, u32[]{:S(2)}) collective-permute-start(bf16[4,48,1536]{2,1,0:T(8,128)(2,1)S(1)} %pad_maximum_fusion.23.refs_0_), channel_id=1, source_target_pairs={{0,2},{2,0},{4,6},{6,4},{8,10},{10,8},{12,14},{14,12},{1,3},{3,1},... | collective-permute-start | bytes 1769480 | tf_op jit(solution)/shard_map/ppermute | solution.py:27
  131.2 23.6 %collective-permute-start.37 = (bf16[4,48,1536]{2,1,0:T(8,128)(2,1)S(1)}, bf16[4,48,1536]{2,1,0:T(8,128)(2,1)S(1)}, u32[]{:S(2)}, u32[]{:S(2)}) collective-permute-start(bf16[4,48,1536]{2,1,0:T(8,128)(2,1)S(1)} %pad_maximum_fusion.24.refs_0_), channel_id=1, source_target_pairs={{0,1},{1,0},{2,3},{3,2},{4,5},{5,4},{6,7},{7,6},{8,9},{9,8},{10,11... | collective-permute-start | bytes 1769480 | tf_op jit(solution)/shard_map/ppermute | solution.py:23
  132.3 22.6 %collective-permute-start.36 = (bf16[4,48,1536]{2,1,0:T(8,128)(2,1)S(1)}, bf16[4,48,1536]{2,1,0:T(8,128)(2,1)S(1)}, u32[]{:S(2)}, u32[]{:S(2)}) collective-permute-start(bf16[4,48,1536]{2,1,0:T(8,128)(2,1)S(1)} %pad_maximum_fusion.24.refs_0_), channel_id=1, source_target_pairs={{0,2},{2,0},{4,6},{6,4},{8,10},{10,8},{12,14},{14,12},{1,3},{3,1},... | collective-permute-start | bytes 1769480 | tf_op jit(solution)/shard_map/ppermute | solution.py:27
  133.8 21.0 %collective-permute-start.35 = (bf16[2,48,1536]{2,1,0:T(8,128)(2,1)S(1)}, bf16[2,48,1536]{2,1,0:T(8,128)(2,1)S(1)}, u32[]{:S(2)}, u32[]{:S(2)}) collective-permute-start(bf16[2,48,1536]{2,1,0:T(8,128)(2,1)S(1)} %slice.750), channel_id=1, source_target_pairs={{0,2},{2,0},{4,6},{6,4},{8,10},{10,8},{12,14},{14,12},{1,3},{3,1},... | collective-permute-start | bytes 884744 | tf_op jit(solution)/shard_map/ppermute | solution.py:27
  158.7 21.2 %collective-permute-start.47 = (bf16[4,48,1536]{2,1,0:T(8,128)(2,1)S(1)}, bf16[4,48,1536]{2,1,0:T(8,128)(2,1)S(1)}, u32[]{:S(2)}, u32[]{:S(2)}) collective-permute-start(bf16[4,48,1536]{2,1,0:T(8,128)(2,1)S(1)} %pad_maximum_fusion.25.refs_0_), channel_id=1, source_target_pairs={{0,1},{1,0},{2,3},{3,2},{4,5},{5,4},{6,7},{7,6},{8,9},{9,8},{10,11... | collective-permute-start | bytes 1769480 | tf_op jit(solution)/shard_map/ppermute | solution.py:23
  159.7 20.1 %collective-permute-start.46 = (bf16[4,48,1536]{2,1,0:T(8,128)(2,1)S(1)}, bf16[4,48,1536]{2,1,0:T(8,128)(2,1)S(1)}, u32[]{:S(2)}, u32[]{:S(2)}) collective-permute-start(bf16[4,48,1536]{2,1,0:T(8,128)(2,1)S(1)} %pad_maximum_fusion.25.refs_0_), channel_id=1, source_target_pairs={{0,2},{2,0},{4,6},{6,4},{8,10},{10,8},{12,14},{14,12},{1,3},{3,1},... | collective-permute-start | bytes 1769480 | tf_op jit(solution)/shard_map/ppermute | solution.py:27
  206.0 20.9 %collective-permute-start.55 = (bf16[4,48,1536]{2,1,0:T(8,128)(2,1)S(1)}, bf16[4,48,1536]{2,1,0:T(8,128)(2,1)S(1)}, u32[]{:S(2)}, u32[]{:S(2)}) collective-permute-start(bf16[4,48,1536]{2,1,0:T(8,128)(2,1)S(1)} %pad_maximum_fusion.26.refs_0_), channel_id=1, source_target_pairs={{0,1},{1,0},{2,3},{3,2},{4,5},{5,4},{6,7},{7,6},{8,9},{9,8},{10,11... | collective-permute-start | bytes 1769480 | tf_op jit(solution)/shard_map/ppermute | solution.py:23
  206.3 20.6 %collective-permute-start.54 = (bf16[4,48,1536]{2,1,0:T(8,128)(2,1)S(1)}, bf16[4,48,1536]{2,1,0:T(8,128)(2,1)S(1)}, u32[]{:S(2)}, u32[]{:S(2)}) collective-permute-start(bf16[4,48,1536]{2,1,0:T(8,128)(2,1)S(1)} %pad_maximum_fusion.26.refs_0_), channel_id=1, source_target_pairs={{0,2},{2,0},{4,6},{6,4},{8,10},{10,8},{12,14},{14,12},{1,3},{3,1},... | collective-permute-start | bytes 1769480 | tf_op jit(solution)/shard_map/ppermute | solution.py:27
  232.0 21.9 %collective-permute-start.58 = (bf16[2,48,1536]{2,1,0:T(8,128)(2,1)S(1)}, bf16[2,48,1536]{2,1,0:T(8,128)(2,1)S(1)}, u32[]{:S(2)}, u32[]{:S(2)}) collective-permute-start(bf16[2,48,1536]{2,1,0:T(8,128)(2,1)S(1)} %slice.790), channel_id=1, source_target_pairs={{0,2},{2,0},{4,6},{6,4},{8,10},{10,8},{12,14},{14,12},{1,3},{3,1},... | collective-permute-start | bytes 884744 | tf_op jit(solution)/shard_map/ppermute | solution.py:27
  232.9 21.1 %collective-permute-start.57 = (bf16[2,48,1536]{2,1,0:T(8,128)(2,1)S(1)}, bf16[2,48,1536]{2,1,0:T(8,128)(2,1)S(1)}, u32[]{:S(2)}, u32[]{:S(2)}) collective-permute-start(bf16[2,48,1536]{2,1,0:T(8,128)(2,1)S(1)} %slice.789), channel_id=1, source_target_pairs={{0,1},{1,0},{2,3},{3,2},{4,5},{5,4},{6,7},{7,6},{8,9},{9,8},{10,11... | collective-permute-start | bytes 884744 | tf_op jit(solution)/shard_map/ppermute | solution.py:23
  317.0 27.8 %collective-permute-start.66 = (bf16[4,48,1536]{2,1,0:T(8,128)(2,1)}, bf16[4,48,1536]{2,1,0:T(8,128)(2,1)}, u32[]{:S(2)}, u32[]{:S(2)}) collective-permute-start(bf16[4,48,1536]{2,1,0:T(8,128)(2,1)} %pad_maximum_fusion.27), channel_id=1, source_target_pairs={{0,2},{2,0},{4,6},{6,4},{8,10},{10,8},{12,14},{14,12},{1,3},{3,1},... | collective-permute-start | bytes 1769480 | tf_op jit(solution)/shard_map/ppermute | solution.py:27
  318.6 28.9 %collective-permute-start.67 = (bf16[4,48,1536]{2,1,0:T(8,128)(2,1)}, bf16[4,48,1536]{2,1,0:T(8,128)(2,1)}, u32[]{:S(2)}, u32[]{:S(2)}) collective-permute-start(bf16[4,48,1536]{2,1,0:T(8,128)(2,1)} %pad_maximum_fusion.28), channel_id=1, source_target_pairs={{0,1},{1,0},{2,3},{3,2},{4,5},{5,4},{6,7},{7,6},{8,9},{9,8},{10,11... | collective-permute-start | bytes 1769480 | tf_op jit(solution)/shard_map/ppermute | solution.py:23
  320.6 26.9 %collective-permute-start.69 = (bf16[384,1920]{1,0:T(8,128)(2,1)}, bf16[384,1920]{1,0:T(8,128)(2,1)}, u32[]{:S(2)}, u32[]{:S(2)}) collective-permute-start(bf16[384,1920]{1,0:T(8,128)(2,1)} %pad_maximum_fusion.1), channel_id=1, source_target_pairs={{0,16},{16,0},{1,17},{17,1},{2,18},{18,2},{3,19},{19,3},{4,20},{20... | collective-permute-start | bytes 4423688 | tf_op jit(solution)/shard_map/ppermute | solution.py:23
  323.7 23.8 %collective-permute-start.68 = (bf16[384,1920]{1,0:T(8,128)(2,1)}, bf16[384,1920]{1,0:T(8,128)(2,1)}, u32[]{:S(2)}, u32[]{:S(2)}) collective-permute-start(bf16[384,1920]{1,0:T(8,128)(2,1)} %pad_maximum_fusion), channel_id=1, source_target_pairs={{0,16},{16,0},{1,17},{17,1},{2,18},{18,2},{3,19},{19,3},{4,20},{20... | collective-permute-start | bytes 4423688 | tf_op jit(solution)/shard_map/ppermute | solution.py:23
  344.9 30.4 %collective-permute-start.74 = (bf16[512,768]{1,0:T(8,128)(2,1)}, bf16[512,768]{1,0:T(8,128)(2,1)}, u32[]{:S(2)}, u32[]{:S(2)}) collective-permute-start(bf16[512,768]{1,0:T(8,128)(2,1)} %fusion.82), channel_id=1, source_target_pairs={{16,17},{17,16},{18,19},{19,18},{20,21},{21,20},{22,23},{23,22},{2... | collective-permute-start | bytes 2359304 | tf_op jit(solution)/shard_map/ppermute | solution.py:419
  353.7 21.6 %collective-permute-start.71 = (bf16[48,1536]{1,0:T(8,128)(2,1)}, bf16[48,1536]{1,0:T(8,128)(2,1)}, u32[]{:S(2)}, u32[]{:S(2)}) collective-permute-start(bf16[48,1536]{1,0:T(8,128)(2,1)} %fusion.167), channel_id=1, source_target_pairs={{0,12},{2,14},{4,0},{6,2},{8,4},{10,6},{12,8},{14,10},{1,13},{3,15... | collective-permute-start | bytes 442376 | tf_op jit(solution)/shard_map/ppermute | solution.py:33
  436.3 52.2 %collective-permute-start.89 = (bf16[4,48,1152]{2,1,0:T(8,128)(2,1)}, bf16[4,48,1152]{2,1,0:T(8,128)(2,1)}, u32[]{:S(2)}, u32[]{:S(2)}) collective-permute-start(bf16[4,48,1152]{2,1,0:T(8,128)(2,1)} %pad_maximum_fusion.31), channel_id=1, source_target_pairs={{0,2},{2,0},{4,6},{6,4},{8,10},{10,8},{12,14},{14,12},{1,3},{3,1},... | collective-permute-start | bytes 1327112 | tf_op jit(solution)/shard_map/ppermute | solution.py:27
  438.3 50.2 %collective-permute-start.90 = (bf16[4,48,1152]{2,1,0:T(8,128)(2,1)}, bf16[4,48,1152]{2,1,0:T(8,128)(2,1)}, u32[]{:S(2)}, u32[]{:S(2)}) collective-permute-start(bf16[4,48,1152]{2,1,0:T(8,128)(2,1)} %pad_maximum_fusion.32), channel_id=1, source_target_pairs={{0,1},{1,0},{2,3},{3,2},{4,5},{5,4},{6,7},{7,6},{8,9},{9,8},{10,11... | collective-permute-start | bytes 1327112 | tf_op jit(solution)/shard_map/ppermute | solution.py:23
  468.9 21.6 %collective-permute-start.88 = (bf16[2,48,1536]{2,1,0:T(8,128)(2,1)}, bf16[2,48,1536]{2,1,0:T(8,128)(2,1)}, u32[]{:S(2)}, u32[]{:S(2)}) collective-permute-start(bf16[2,48,1536]{2,1,0:T(8,128)(2,1)} %bitcast.432), channel_id=1, source_target_pairs={{0,2},{2,0},{4,6},{6,4},{8,10},{10,8},{12,14},{14,12},{1,3},{3,1},... | collective-permute-start | bytes 884744 | tf_op jit(solution)/shard_map/ppermute | solution.py:27
  470.0 20.4 %collective-permute-start.87 = (bf16[2,48,1536]{2,1,0:T(8,128)(2,1)}, bf16[2,48,1536]{2,1,0:T(8,128)(2,1)}, u32[]{:S(2)}, u32[]{:S(2)}) collective-permute-start(bf16[2,48,1536]{2,1,0:T(8,128)(2,1)} %bitcast.431), channel_id=1, source_target_pairs={{0,1},{1,0},{2,3},{3,2},{4,5},{5,4},{6,7},{7,6},{8,9},{9,8},{10,11... | collective-permute-start | bytes 884744 | tf_op jit(solution)/shard_map/ppermute | solution.py:23
  494.5 26.3 %collective-permute-start.97 = (bf16[48,1152]{1,0:T(8,128)(2,1)S(1)}, bf16[48,1152]{1,0:T(8,128)(2,1)S(1)}, u32[]{:S(2)}, u32[]{:S(2)}) collective-permute-start(bf16[48,1152]{1,0:T(8,128)(2,1)S(1)} %fusion.169), channel_id=1, source_target_pairs={{0,12},{2,14},{4,0},{6,2},{8,4},{10,6},{12,8},{14,10},{1,13},{3,15... | collective-permute-start | bytes 331784 | tf_op jit(solution)/shard_map/ppermute | solution.py:33
  497.3 24.7 %collective-permute-start.130 = (bf16[48,1920]{1,0:T(8,128)(2,1)S(1)}, bf16[48,1920]{1,0:T(8,128)(2,1)S(1)}, u32[]{:S(2)}, u32[]{:S(2)}) collective-permute-start(bf16[48,1920]{1,0:T(8,128)(2,1)S(1)} %get-tuple-element.492), channel_id=1, source_target_pairs={{0,16},{1,17},{2,18},{3,19},{4,20},{5,21},{6,22},{7,23},{8,24},{9,... | collective-permute-start | bytes 552968 | tf_op jit(solution)/shard_map/ppermute | solution.py:631
  512.7 23.7 %collective-permute-start.92 = (bf16[512,768]{1,0:T(8,128)(2,1)S(1)}, bf16[512,768]{1,0:T(8,128)(2,1)S(1)}, u32[]{:S(2)}, u32[]{:S(2)}) collective-permute-start(bf16[512,768]{1,0:T(8,128)(2,1)S(1)} %pad_maximum_fusion.14), channel_id=1, source_target_pairs={{0,16},{16,0},{1,17},{17,1},{2,18},{18,2},{3,19},{19,3},{4,20},{20... | collective-permute-start | bytes 2359304 | tf_op jit(solution)/shard_map/ppermute | solution.py:23
  576.1 30.3 %collective-permute-start.106 = (bf16[4,48,1920]{2,1,0:T(8,128)(2,1)}, bf16[4,48,1920]{2,1,0:T(8,128)(2,1)}, u32[]{:S(2)}, u32[]{:S(2)}) collective-permute-start(bf16[4,48,1920]{2,1,0:T(8,128)(2,1)} %pad_maximum_fusion.20), channel_id=1, source_target_pairs={{0,1},{1,0},{2,3},{3,2},{4,5},{5,4},{6,7},{7,6},{8,9},{9,8},{10,11... | collective-permute-start | bytes 2211848 | tf_op jit(solution)/shard_map/ppermute | solution.py:23
  578.3 28.1 %collective-permute-start.105 = (bf16[4,48,1920]{2,1,0:T(8,128)(2,1)}, bf16[4,48,1920]{2,1,0:T(8,128)(2,1)}, u32[]{:S(2)}, u32[]{:S(2)}) collective-permute-start(bf16[4,48,1920]{2,1,0:T(8,128)(2,1)} %pad_maximum_fusion.19), channel_id=1, source_target_pairs={{0,2},{2,0},{4,6},{6,4},{8,10},{10,8},{12,14},{14,12},{1,3},{3,1},... | collective-permute-start | bytes 2211848 | tf_op jit(solution)/shard_map/ppermute | solution.py:27
  585.8 20.5 %collective-permute-start.107 = (bf16[384,1152]{1,0:T(8,128)(2,1)}, bf16[384,1152]{1,0:T(8,128)(2,1)}, u32[]{:S(2)}, u32[]{:S(2)}) collective-permute-start(bf16[384,1152]{1,0:T(8,128)(2,1)} %convolution_convert_fusion.17), channel_id=1, source_target_pairs={{0,16},{16,0},{1,17},{17,1},{2,18},{18,2},{3,19},{19,3},{4,20},{20... | collective-permute-start | bytes 2654216 | tf_op jit(solution)/shard_map/ppermute | solution.py:23
  (332 other events, 2256.3 us)

commit v2 on v1

v2 whole, which is shorter than its diff:
```python
from functools import partial

import jax
import jax.numpy as jnp
from jax import lax
from jax.experimental import pallas as pl
from jax.experimental.pallas import tpu as pltpu
from jax.sharding import PartitionSpec as P

BF16 = jnp.bfloat16
F32 = jnp.float32
ROWS = (((0,), (0,)), ((), ()))
COLS = (((1,), (1,)), ((), ()))
PLAIN = (((1,), (0,)), ((), ()))
CROSS = ((0, 1), (1, 0))


def cost(flops, size, exps=0):
    return pl.CostEstimate(flops=flops, bytes_accessed=size, transcendentals=exps)


def dot(left, right, dims=PLAIN):
    return lax.dot_general(left, right, dims, preferred_element_type=F32)


def swap(array, axis):
    return lax.ppermute(array, axis, CROSS)


def pair_swap(array, bit=1):
    return lax.ppermute(array, "dp", [(i, i ^ bit) for i in range(lax.axis_size("dp"))])


def ring_shift(array, by):
    ring = lax.axis_size("dp") // 2
    pairs = [(2 * z + x, 2 * ((z + by) % ring) + x) for z in range(ring) for x in (0, 1)]
    return lax.ppermute(array, "dp", pairs)


def tied(state, after):
    return lax.optimization_barrier((state, after))[0] if after else state


class Line:
    def __init__(self, steps, after=()):
        self.steps, self.result, self.done = steps, None, False
        self.take(next(steps), after)

    def take(self, step, after):
        self.sent = tied([array for _, array in step], after)
        self.pending = [send(array) for (send, _), array in zip(step, self.sent)]

    def advance(self, arrays, after):
        try:
            self.take(self.steps.send(arrays), after)
        except StopIteration as end:
            self.result, self.done, self.pending, self.sent = end.value, True, [], []


def join(state, *lines):
    lines = [line for line in lines if not line.done]
    state, arrays = lax.optimization_barrier((state, [line.pending for line in lines]))
    sent = []
    for line, own in zip(lines, arrays):
        line.advance(own, sent)
        sent = sent + line.sent
    return tied(state, sent)


def over(axis):
    return lambda array: swap(array, axis)


def around(by):
    return lambda array: ring_shift(array, by)


def ring_gather(piece):
    ring = lax.axis_size("dp") // 2
    if ring <= 4:
        came = yield [(around(k), piece) for k in range(1, ring)]
        return [piece, *came]

    def step(k, state):
        moving, held = state
        moving = ring_shift(moving, 1)
        return moving, lax.dynamic_update_index_in_dim(held, moving, k, 0)

    held = jnp.zeros((ring,) + piece.shape, piece.dtype).at[0].set(piece)
    held = lax.fori_loop(1, ring, step, (piece, held))[1]
    return [held.reshape(-1, piece.shape[1])]


def ring_scatter(parts):
    ring = len(parts)
    if ring <= 4:
        came = yield [(around(-k), parts[k]) for k in range(1, ring)]
        return sum((part.astype(F32) for part in came), parts[0])

    stacked = jnp.stack([part.astype(BF16) for part in parts[1:]])

    def step(k, total):
        mine = lax.dynamic_index_in_dim(stacked, ring - 2 - k, 0, keepdims=False)
        return mine.astype(F32) + ring_shift(total.astype(BF16), -1).astype(F32)

    total = lax.fori_loop(1, ring - 1, step, stacked[ring - 2].astype(F32))
    return parts[0] + ring_shift(total.astype(BF16), -1).astype(F32)


def copy_kernel(plan, count, *refs):
    sources, outs, sems = refs[:count], refs[count:-1], refs[-1]
    copies = []
    for source, (out, row) in zip(sources, plan):
        copies.append(
            pltpu.make_async_copy(
                source, outs[out].at[pl.ds(row, source.shape[0])], sems.at[len(copies)]
            )
        )
    for copy in copies:
        copy.start()
    for copy in copies:
        copy.wait()


def stack_rows(*groups):
    sources = [part for group in groups for part in group]
    plan, outs = [], []
    for index, group in enumerate(groups):
        row = 0
        for part in group:
            plan.append((index, row))
            row += part.shape[0]
        outs.append(jax.ShapeDtypeStruct((row,) + group[0].shape[1:], group[0].dtype))
    return pl.pallas_call(
        partial(copy_kernel, plan, len(sources)),
        out_shape=outs,
        in_specs=[pl.BlockSpec(memory_space=pl.ANY)] * len(sources),
        out_specs=[pl.BlockSpec(memory_space=pltpu.VMEM)] * len(outs),
        scratch_shapes=[pltpu.SemaphoreType.DMA((len(sources),))],
        compiler_params=pltpu.CompilerParams(vmem_limit_bytes=(1 << 20) + sum(2 * out.size for out in outs)),
        cost_estimate=cost(0, sum(4 * part.size for part in sources)),
        name="stack_rows",
    )(*sources)


def gather_chunk(piece):
    rows, columns = piece.shape
    low = (lax.axis_size("dp") // 4) * rows
    near = yield from ring_gather(piece)
    near = stack_rows(near)[0] if len(near) > 1 and rows % 16 == 0 else jnp.concatenate(near)
    over_x, over_y = yield [(pair_swap, near), (over("tensor"), near)]
    first, second = yield [(over("tensor"), over_x[:low]), (pair_swap, over_y[low:])]
    mine = stack_rows([near, over_x, over_y, first, second])[0]
    mine = mine.reshape(2, -1, columns)
    (theirs,) = yield [(over("section"), mine)]
    return stack_rows([mine[0], theirs[0]], [mine[1], theirs[1]])


def pick_kernel(ring, column, place, mine, theirs, out0, out1, sems):
    z, x, y = place[0], place[1], place[2]
    rows, columns = mine.shape[1], out0.shape[1]
    copies = []
    for ds, source in enumerate((mine, theirs)):
        for dx in (0, 1):
            for k in range(ring):
                owner = 2 * lax.rem(z - k + ring, ring) + (x + dx) % 2
                row = ((ds * 2 + dx) * ring + k) * rows
                for dy, out in enumerate((out0, out1)):
                    copies.append(
                        pltpu.make_async_copy(
                            source.at[2 * owner + (y + dy) % 2, :, pl.ds(column, columns)],
                            out.at[pl.ds(row, rows)],
                            sems.at[len(copies)],
                        )
                    )
    for copy in copies:
        copy.start()
    for copy in copies:
        copy.wait()


def pick(place, mine, theirs, column, columns):
    groups, rows, _ = mine.shape
    ring = groups // 4
    if rows % 16:
        return pick_plain(place, mine, theirs, column, columns)
    out = like((groups * rows, columns))
    return pl.pallas_call(
        partial(pick_kernel, ring, column),
        out_shape=[out, out],
        in_specs=[pl.BlockSpec(memory_space=pltpu.SMEM)] + [pl.BlockSpec(memory_space=pl.ANY)] * 2,
        out_specs=[pl.BlockSpec(memory_space=pltpu.VMEM)] * 2,
        scratch_shapes=[pltpu.SemaphoreType.DMA((2 * groups,))],
        compiler_params=pltpu.CompilerParams(vmem_limit_bytes=6 * 1024 * 1024),
        cost_estimate=cost(0, 4 * groups * rows * columns),
        name="pick",
    )(place, mine, theirs)


def pick_plain(place, mine, theirs, column, columns):
    groups, rows, _ = mine.shape
    ring = groups // 4
    near = jnp.arange(groups // 2) % ring
    owner = 2 * ((place[0] - near + ring) % ring) + (place[1] + jnp.arange(groups // 2) // ring) % 2
    outs = []
    for dy in (0, 1):
        which = 2 * owner + (place[2] + dy) % 2
        parts = [part[:, :, column : column + columns][which] for part in (mine, theirs)]
        outs.append(jnp.concatenate(parts).reshape(-1, columns))
    return outs


def total_of(own, came):
    return own[0].astype(F32) + came[0].astype(F32)


def corner_kernel(low, own, came, first, second):
    total = total_of(own, came)
    first[...] = total[:low].astype(BF16)
    second[...] = total[low:].astype(BF16)


def sides_kernel(low, own_x, came_x, own_y, came_y, first, second, over_x, over_y):
    total = total_of(own_x, came_x)
    over_x[:low] = (total[:low] + first[...].astype(F32)).astype(BF16)
    over_x[low:] = total[low:].astype(BF16)
    total = total_of(own_y, came_y)
    over_y[:low] = total[:low].astype(BF16)
    over_y[low:] = (total[low:] + second[...].astype(F32)).astype(BF16)


def near_kernel(own, came, over_x, over_y, *near):
    total = total_of(own, came) + over_x[...].astype(F32) + over_y[...].astype(F32)
    rows = near[0].shape[0]
    for k, out in enumerate(near):
        out[...] = total[k * rows : (k + 1) * rows].astype(out.dtype)


def call(kernel, name, ins, outs, flops=0, exps=0, limit=5, specs=None, aliases=None):
    size = lambda a: a.size * a.dtype.itemsize
    return pl.pallas_call(
        kernel,
        out_shape=outs,
        in_specs=specs or [pl.BlockSpec(memory_space=pltpu.VMEM)] * len(ins),
        out_specs=[pl.BlockSpec(memory_space=pltpu.VMEM)] * len(outs),
        compiler_params=pltpu.CompilerParams(vmem_limit_bytes=limit * 1024 * 1024),
        cost_estimate=cost(flops, sum(size(a) for a in ins) + sum(size(o) for o in outs), exps),
        name=name,
    )(*ins)


def like(shape, kind=BF16):
    return jax.ShapeDtypeStruct(shape, kind)


def scatter_chunk(own, other, core):
    ring = lax.axis_size("dp") // 2
    columns = own.shape[2]
    quarter = own.shape[1] // 2
    rows = quarter // ring
    low = (ring // 2) * rows
    (came,) = yield [(over("section"), other)]
    block = lambda t, x: pl.BlockSpec((1, quarter, columns), lambda i: (t, x, 0))
    whole = lambda size: pl.BlockSpec((size, columns), lambda i: (0, 0))

    def run(kernel, name, blocks, extra, outs):
        ins = [array for _ in blocks for array in (own, came)] + extra
        specs = [block(*spot) for spot in blocks for _ in (0, 1)]
        return pl.pallas_call(
            kernel,
            grid=(1,),
            out_shape=outs,
            in_specs=specs + [whole(array.shape[0]) for array in extra],
            out_specs=[whole(out.shape[0]) for out in outs],
            compiler_params=pltpu.CompilerParams(vmem_limit_bytes=14 * 1024 * 1024),
            cost_estimate=cost(0, 6 * quarter * columns * len(blocks)),
            name=name,
        )(*ins)

    first, second = run(
        partial(corner_kernel, low), "corner", [(1, 1)], [],
        [like((low, columns)), like((quarter - low, columns))],
    )
    first, second = yield [(over("tensor"), first), (pair_swap, second)]
    over_x, over_y = run(
        partial(sides_kernel, low), "sides", [(0, 1), (1, 0)], [first, second],
        [like((quarter, columns))] * 2,
    )
    over_x, over_y = yield [(pair_swap, over_x), (over("tensor"), over_y)]
    kinds = [F32] + [BF16] * (ring - 1)
    near = run(
        near_kernel, "near", [(0, 0)], [over_x, over_y], [like((rows, columns), k) for k in kinds]
    )
    total = yield from ring_scatter(near)
    to_core = lambda array: lax.ppermute(array, "section", [(1 - core, core)])
    (came,) = yield [(to_core, total.astype(BF16))]
    return total, came.astype(F32)


def attend_kernel(scale, q_ref, k0_ref, k1_ref, v0_ref, v1_ref, b0_ref, b1_ref, o_ref, lse_ref):
    span = q_ref.shape[0]
    lane = lax.broadcasted_iota(jnp.int32, (span, 128), 1)
    q = q_ref[...]
    k0, k1 = k0_ref[...], k1_ref[...]
    v0, v1 = v0_ref[...], v1_ref[...]
    b0, b1 = b0_ref[...], b1_ref[...]
    outs = []
    for head in (0, 1):
        own = (lane >= 64 * head) & (lane < 64 * head + 64)
        qh = jnp.where(own, q * jnp.asarray(scale, BF16), jnp.zeros_like(q))
        s0 = dot(k0, qh, COLS) + b0
        s1 = dot(k1, qh, COLS) + b1
        peak = jnp.maximum(jnp.max(s0, 0, keepdims=True), jnp.max(s1, 0, keepdims=True))
        p0 = jnp.exp(s0 - peak)
        p1 = jnp.exp(s1 - peak)
        total = jnp.sum(p0, 0, keepdims=True) + jnp.sum(p1, 0, keepdims=True)
        out = dot(v0, p0.astype(BF16), ROWS) + dot(v1, p1.astype(BF16), ROWS)
        outs.append(out / total)
        lse_ref[0, head : head + 1, :] = peak + jnp.log(total)
    row = lax.broadcasted_iota(jnp.int32, (128, span), 0)
    o_ref[...] = jnp.where(row < 64, outs[0], outs[1]).T.astype(BF16)


def attend(query, own, other, biases):
    _, span, width = query.shape
    groups = width // 128
    block = lambda first: pl.BlockSpec((None, span, 128), lambda t, g: (t, 0, first * groups + g))
    bias = pl.BlockSpec((span, 1), lambda t, g: (0, 0))
    return pl.pallas_call(
        partial(attend_kernel, 0.125),
        grid=(2, groups),
        out_shape=[like(query.shape), like((2, groups, 8, span), F32)],
        in_specs=[block(0), block(0), block(0), block(1), block(1), bias, bias],
        out_specs=[block(0), pl.BlockSpec((None, 1, 8, span), lambda t, g: (t, g, 0, 0))],
        compiler_params=pltpu.CompilerParams(vmem_limit_bytes=9 * 1024 * 1024),
        cost_estimate=cost(32 * groups * span * span * 2 * 128, 16 * span * width, 8 * groups * span * span),
        name="attend",
    )(query, own, other, own, other, *biases)


def attend_back_kernel(
    scale, q_ref, k0_ref, k1_ref, v0_ref, v1_ref, b0_ref, b1_ref, lse_ref, do_ref,
    near_ref, far_ref,
):
    span = q_ref.shape[0]
    lane = lax.broadcasted_iota(jnp.int32, (span, 128), 1)
    q, above = q_ref[...], do_ref[...]
    keys = (k0_ref[...], k1_ref[...])
    values = (v0_ref[...], v1_ref[...])
    biases = (b0_ref[...], b1_ref[...])
    dqs, dks, dvs = [], [], []
    for head in (0, 1):
        own = (lane >= 64 * head) & (lane < 64 * head + 64)
        qh = jnp.where(own, q * jnp.asarray(scale, BF16), jnp.zeros_like(q))
        ah = jnp.where(own, above, jnp.zeros_like(above))
        lse = lse_ref[0, head : head + 1, :]
        probs, pushed = [], []
        for part in (0, 1):
            probs.append(jnp.exp(dot(keys[part], qh, COLS) + biases[part] - lse))
            pushed.append(dot(values[part], ah, COLS))
        inner = jnp.sum(probs[0] * pushed[0], 0, keepdims=True) + jnp.sum(
            probs[1] * pushed[1], 0, keepdims=True
        )
        dq = None
        for part in (0, 1):
            slopes = (probs[part] * (pushed[part] - inner)).astype(BF16)
            piece = dot(keys[part], slopes, ROWS)
            dq = piece if dq is None else dq + piece
            dk = dot(slopes, qh)
            dv = dot(probs[part].astype(BF16), ah)
            if head == 0:
                dks.append(dk)
                dvs.append(dv)
            else:
                dks[part] = dks[part] + dk
                dvs[part] = dvs[part] + dv
        dqs.append(dq)
    row = lax.broadcasted_iota(jnp.int32, (128, span), 0)
    near_ref[0] = (jnp.where(row < 64, dqs[0], dqs[1]) * scale).T.astype(BF16)
    near_ref[1] = dks[0].astype(BF16)
    near_ref[2] = dvs[0].astype(BF16)
    far_ref[0] = dks[1].astype(BF16)
    far_ref[1] = dvs[1].astype(BF16)


def attend_back(query, own, other, biases, lse, above, t):
    _, span, width = query.shape
    groups = width // 128
    block = lambda first: pl.BlockSpec((None, span, 128), lambda g: (t, 0, first * groups + g))
    bias = pl.BlockSpec((span, 1), lambda g: (0, 0))
    return pl.pallas_call(
        partial(attend_back_kernel, 0.125),
        grid=(groups,),
        out_shape=[like((3, span, width)), like((2, span, width))],
        in_specs=[block(0), block(0), block(0), block(1), block(1), bias, bias]
        + [pl.BlockSpec((None, 1, 8, span), lambda g: (t, g, 0, 0)), block(0)],
        out_specs=[
            pl.BlockSpec((3, span, 128), lambda g: (0, 0, g)),
            pl.BlockSpec((2, span, 128), lambda g: (0, 0, g)),
        ],
        compiler_params=pltpu.CompilerParams(vmem_limit_bytes=14 * 1024 * 1024),
        cost_estimate=cost(40 * groups * span * span * 2 * 128, 12 * span * width, 4 * groups * span * span),
        name="attend_back",
    )(query, own, other, own, other, *biases, lse, above)


def normalised(values):
    centred = values - jnp.mean(values, -1, keepdims=True)
    scale = lax.rsqrt(jnp.mean(centred * centred, -1, keepdims=True) + 1e-05)
    return centred * scale, scale


def mixed_kernel(values, w0, w1, table, normed, query, own):
    third = query.shape[2]
    unit, _ = normalised(values[...])
    rows = (unit * (1.0 + table[0:1]) + table[1:2]).astype(BF16)
    normed[...] = rows
    for t, weight in enumerate((w0, w1)):
        cut = pl.ds(t * third, third)
        query[t] = (dot(rows, weight[:, :third]) + table[2:3, cut]).astype(BF16)
        own[t, :, :third] = dot(rows, weight[:, third : 2 * third]).astype(BF16)
        own[t, :, third:] = (dot(rows, weight[:, 2 * third : 3 * third]) + table[3:4, cut]).astype(BF16)


def mixed_forward(values, w_a, table):
    span, width = values.shape
    third = w_a[0].shape[1] // 4
    outs = [like((span, width)), like((2, span, third)), like((2, span, 2 * third))]
    return call(mixed_kernel, "mixed", [values, *w_a, table], outs, 2 * span * width * 6 * third)


def middle_kernel(values, attended, w0, w1, table, middle, normed):
    third = attended.shape[2]
    total = values[...] + table[4:5]
    for t, weight in enumerate((w0, w1)):
        total = total + dot(attended[t], weight[:, 3 * third :], COLS)
    middle[...] = total
    unit, _ = normalised(total)
    normed[...] = (unit * (1.0 + table[5:6]) + table[6:7]).astype(BF16)


def middle_forward(values, attended, w_a, table):
    span, width = values.shape
    outs = [like((span, width), F32), like((span, width))]
    return call(
        middle_kernel, "middle", [values, attended, *w_a, table], outs, 2 * span * width * width
    )


def hidden_kernel(normed, w0, w1, table, hidden, slope):
    width = table.shape[1]
    rows = normed[...]
    step = width // 2
    for t, weight in enumerate((w0, w1)):
        for start in range(0, hidden.shape[2], step):
            cut = slice(start, start + step)
            row = 8 + (t * hidden.shape[2] + start) // width
            column = (t * hidden.shape[2] + start) % width
            before = dot(rows, weight[:, cut]) + table[row : row + 1, column : column + step]
            share = 0.5 + 0.5 * lax.erf(before * (0.5**0.5))
            hidden[t, :, cut] = (before * share).astype(BF16)
            bell = jnp.exp(-0.5 * before * before) * 0.3989422804014327
            slope[t, :, cut] = (share + before * bell).astype(BF16)


def hidden_forward(normed, w_b, table):
    span, width = normed.shape
    unit = w_b[0].shape[1]
    outs = [like((2, span, unit))] * 2
    flops, exps = 4 * span * width * unit, 4 * span * unit
    return call(hidden_kernel, "hidden", [normed, *w_b, table], outs, flops, exps)


def down_kernel(middle, hidden, w0, w1, table, out):
    total = middle[...] + table[7:8]
    for t, weight in enumerate((w0, w1)):
        total = total + dot(hidden[t], weight[...], COLS)
    out[...] = total


def hidden_down(middle, hidden, w_c, table):
    span, width = middle.shape
    flops = 4 * span * width * w_c[0].shape[1]
    return call(down_kernel, "down", [middle, hidden, *w_c, table], [like((span, width), F32)], flops)[0]


def slope_kernel(short, w0, w1, slope, pushed):
    rows = short[...]
    step = rows.shape[1] // 2
    for t, weight in enumerate((w0, w1)):
        for start in range(0, slope.shape[2], step):
            cut = slice(start, start + step)
            grad = dot(rows, weight[:, cut]) * slope[t, :, cut].astype(F32)
            pushed[t, :, cut] = grad.astype(BF16)


def hidden_back(short, w_c, slope):
    flops = 2 * short.shape[1] * slope.size
    return call(slope_kernel, "hidden_back", [short, *w_c, slope], [like(slope.shape)], flops)[0]


def grads_kernel(count, *refs):
    outs = refs[-2:]
    start = 0
    for left, right in zip(refs[:count], refs[count : 2 * count]):
        half, size = left.shape[1] // 2, right.shape[2]
        for core, out in enumerate(outs):
            rows = left[:, core * half : (core + 1) * half].T
            for t in (0, 1):
                out[t, :, start : start + size] = dot(rows, right[t]).astype(BF16)
        start += size
    if len(refs) > 2 * count + 2:
        extra = refs[2 * count]
        half, size = extra.shape[0] // 2, extra.shape[1]
        for core, out in enumerate(outs):
            for t in (0, 1):
                out[t, :, start:] = extra[core * half : (core + 1) * half]


def grads_of(*pairs, extra=()):
    lefts, rights = [pair[0] for pair in pairs], [pair[1] for pair in pairs]
    half = lefts[0].shape[1] // 2
    total = sum(right.shape[2] for right in rights)
    flops = 8 * half * lefts[0].shape[0] * total
    total += sum(part.shape[1] for part in extra)
    outs = [like((2, half, total))] * 2
    ins = lefts + rights + list(extra)
    return call(partial(grads_kernel, len(pairs)), "grads", ins, outs, flops, limit=6)


def flat_kernel(near0, far0, near1, far1, flat):
    third = near0.shape[2]
    for t, (near, far) in enumerate(((near0, far0), (near1, far1))):
        for n in range(3):
            part = near[n]
            if n:
                part = (part.astype(F32) + far[n - 1].astype(F32)).astype(BF16)
            flat[t, :, n * third : (n + 1) * third] = part


def flat_of(near, far):
    _, span, third = near[0].shape
    ins = [near[0], far[0], near[1], far[1]]
    return call(flat_kernel, "flat", ins, [like((2, span, 3 * third))])[0]


def norm_back_kernel(gain, tail, add, parts, w0, w1, values, table, out, short, sums, columns, *above):
    size = parts.shape[2]
    weights = (w0, w1)
    grad = sum(dot(parts[t], weights[t][:, :size], COLS) for t in (0, 1))
    unit, scale = normalised(values[...])
    inner = grad * (1.0 + table[gain : gain + 1])
    inner = inner - jnp.mean(inner, -1, keepdims=True)
    inner = inner - unit * jnp.mean(inner * unit, -1, keepdims=True)
    total = add[...] + inner * scale
    out[...] = total
    low = total.astype(BF16)
    short[...] = low
    sums[0:1] = jnp.sum(grad * unit, 0, keepdims=True)
    sums[1:2] = jnp.sum(grad, 0, keepdims=True)
    sums[2:3] = jnp.sum(total, 0, keepdims=True)
    sums[3:4] = jnp.sum(add[...], 0, keepdims=True)
    for t in (0, 1):
        columns[t, 0:1] = jnp.sum(parts[t].astype(F32), 0, keepdims=True)


def norm_back(gain, add, parts, weights, values, table):
    span, width = values.shape
    size = parts.shape[2]
    outs = [
        like((span, width), F32), like((span, width)), like((8, width), F32), like((2, 8, size), F32),
    ]
    ins = [add, parts, *weights, values, table]
    return call(
        partial(norm_back_kernel, gain, 0), "norm_back", ins, outs, 4 * span * width * size
    )


def above_kernel(short, w0, w1, above):
    third = above.shape[2]
    for t, weight in enumerate((w0, w1)):
        above[t] = dot(short[...], weight[:, 3 * third :]).astype(BF16)


def attended_back(short, w_a):
    span, width = short.shape
    third = w_a[0].shape[1] // 4
    flops = 4 * span * width * third
    return call(above_kernel, "above", [short, *w_a], [like((2, span, third))], flops)[0]


def table_kernel(side, sums_in, columns_in, sums_mid, columns_mid, order, out):
    third = columns_in.shape[2] // 3
    width = order.shape[0]
    swapped = side[0] != 0

    def halves(parts):
        first = jnp.where(swapped, parts[1], parts[0])
        second = jnp.where(swapped, parts[0], parts[1])
        return [first, second]

    query = jnp.concatenate(halves([columns_in[t, 0:1, :third] for t in (0, 1)]), 1)
    value = jnp.concatenate(halves([columns_in[t, 0:1, 2 * third :] for t in (0, 1)]), 1)
    rise = halves([columns_mid[t, 0:1, :] for t in (0, 1)])
    rows = [query, value]
    for part in rise:
        rows += [part[:, :width], part[:, width:]]
    rows = jnp.concatenate(rows + [jnp.zeros((2, width), F32)], 0)
    rows = dot(rows.astype(BF16), order[...])
    table = [
        sums_in[0:2], rows[0:2], sums_mid[2:3], sums_mid[0:2], sums_mid[3:4], rows[2:6],
        jnp.zeros((out.shape[1] - 12, width), F32),
    ]
    out[...] = jnp.concatenate(table, 0).T.astype(BF16)


def table_back(side, sums_in, columns_in, sums_mid, columns_mid, order):
    ins = [side, sums_in, columns_in, sums_mid, columns_mid, order]
    specs = [pl.BlockSpec(memory_space=pltpu.SMEM)] + [pl.BlockSpec(memory_space=pltpu.VMEM)] * 5
    outs = [like((order.shape[0], 128))]
    return call(table_kernel, "table_back", ins, outs, specs=specs)[0]


def iter_swaps(rows, first, side, core):
    span, width = rows.shape
    to_core = lambda array: lax.ppermute(array, "section", [(1 - core, core)])
    (came,) = yield [(to_core, rows.astype(BF16))]
    came = came.astype(F32)
    full = jnp.stack([rows, came] if core == 0 else [came, rows])
    keep = lax.dynamic_index_in_dim(full, side, 0, keepdims=False)
    gone = lax.dynamic_index_in_dim(full, 1 - side, 0, keepdims=False).astype(BF16)
    pairs = [(2 * core, 2 * core + 1), (2 * core + 1, 2 * core)]
    (came,) = yield [(lambda array: lax.ppermute(array, ("section", "tensor"), pairs), gone)]
    came = came.astype(F32)
    return jnp.where(side == 0, jnp.stack([keep, came]), jnp.stack([came, keep]))


FEATURE_ROWS = (True, True, False, False, True, True, True, True, False, False, False, False)


def body(ends_in, lengths, vectors, w_qkv, w_out, w_up, w_down):
    core = lax.axis_index("section")
    first = core == 0
    side = lax.axis_index("tensor")
    count = lax.axis_size("dp")
    ring = count // 2
    rows = w_qkv.shape[1]
    half = rows // 2
    span, width = ends_in.shape[2:]
    third, unit = w_qkv.shape[-1], w_up.shape[-1]
    turned = side.astype(jnp.int32).reshape(1)

    at = jnp.arange(width, dtype=jnp.int32)
    row, rest = at % half, at // half
    step, rest = rest % ring, rest // ring
    spot = lax.axis_index("dp")
    owner = 2 * ((spot // 2 - step + ring) % ring) + (spot % 2 + rest % 2) % 2
    source = owner * rows + ((core + rest // 2) % 2) * half + row
    order = at[:, None] == source[None, :]
    order_low = order.astype(BF16)

    def to_own(array):
        return jnp.dot(array, order.astype(F32), precision=lax.Precision.HIGHEST)

    def from_own(array):
        return lax.dot_general(array, order.astype(F32), COLS, precision=lax.Precision.HIGHEST)

    index = spot * 2 + side
    cut = vectors.shape[-1]
    spread = lax.dynamic_update_slice_in_dim(
        jnp.zeros((vectors.shape[1], width), F32), vectors[0], index * cut, 1
    )
    own = jnp.concatenate([w_qkv[0].reshape(rows, -1), w_out[0].T, w_up[0], w_down[0].T], 1)
    halves = (own[:half], own[half:])
    came = swap(jnp.where(first, halves[1], halves[0]), "section")
    one, two = jnp.where(first, halves[0], came), jnp.where(first, came, halves[1])
    cuts = [slice(n * unit, (n + 1) * unit) for n in range(3)]
    chunks = [layer[:, c] for layer in (one,) for c in cuts]
    far_mine = lax.all_gather(two, ("dp", "tensor"), axis=0)
    a0 = Line(gather_chunk(chunks[0]))
    spread, ends = tied((spread, ends_in[0]), a0.sent)
    spread = spread + swap(spread, "tensor")
    spread, ends = lax.optimization_barrier((spread, ends))

    keep = lax.dynamic_index_in_dim(ends, side, 0, keepdims=False)
    gone = lax.dynamic_index_in_dim(ends, 1 - side, 0, keepdims=False)
    clip = swap(gone, "tensor")
    bit = 1
    while bit < count:
        spread = spread + pair_swap(spread, bit)
        bit *= 2
    theirs = swap(spread, "section")
    spread, theirs, clip, ready = join((spread, theirs, clip, chunks[1]), a0)
    b0 = Line(gather_chunk(ready))
    upper, lower = jnp.where(side == 0, keep, clip), jnp.where(side == 0, clip, keep)
    stay, leave = jnp.where(first, upper, lower), jnp.where(first, lower, upper)
    came = swap(leave, "section")
    values = dot(jnp.where(first, stay, came), order_low)
    upstream = dot(jnp.where(first, came, stay), order_low)
    up_short = upstream.astype(BF16)
    frames = lax.dynamic_index_in_dim(lengths, side, 0, keepdims=False)
    spots = lax.broadcasted_iota(jnp.int32, (span, 1), 0)
    biases = [
        jnp.where(spots + offset * span < frames, 0.0, -1e30).astype(F32)
        for offset in (core, 1 - core)
    ]
    is_feature = jnp.array(FEATURE_ROWS)[:, None]

    def sides_turned(table):
        heads = table[:8].reshape(8, 2, -1)
        rise = table[8:].reshape(2, 2, width)
        heads = jnp.where(side == 0, heads, heads[:, ::-1]).reshape(8, width)
        rise = jnp.where(side == 0, rise, rise[::-1]).reshape(4, width)
        return jnp.concatenate([heads, rise])

    def own_table(table):
        return jnp.where(is_feature, to_own(table), sides_turned(table))

    tables = [
        own_table(jnp.where(first, spread, theirs)),
        own_table(jnp.where(first, theirs, spread)),
    ]

    values, upstream, up_short, tables, ready = join(
        (values, upstream, up_short, tables, chunks[2]), a0, b0
    )
    c0 = Line(gather_chunk(ready))
    join((), a0)
    join((), a0)
    w_a0 = a0.result
    normed_0, query_0, own_0 = mixed_forward(values, w_a0, tables[0])
    other_0 = swap(own_0, "section")
    query_0, own_0, other_0 = join((query_0, own_0, other_0), b0)
    attended_0, logs_0 = attend(query_0, own_0, other_0, biases)
    attended_0 = join(attended_0, b0, c0)
    middle_0, short_0 = middle_forward(values, attended_0, w_a0, tables[0])
    short_0 = join(short_0, b0)
    w_b0 = b0.result
    hidden_0, slope_0 = hidden_forward(short_0, w_b0, tables[0])
    hidden_0, slope_0, far_mine = join((hidden_0, slope_0, far_mine), c0)
    far_theirs = swap(far_mine, "section")
    join((), c0)
    hidden_0 = join(hidden_0, c0)
    w_c0 = c0.result
    layer_one = hidden_down(middle_0, hidden_0, w_c0, tables[0])
    place = jnp.stack([spot // 2, spot % 2, side]).astype(jnp.int32)
    w_a1, w_b1, w_c1 = (pick(place, far_mine, far_theirs, n * unit, unit) for n in range(3))
    normed_1, query_1, own_1 = mixed_forward(layer_one, w_a1, tables[1])
    other_1 = swap(own_1, "section")
    attended_1, logs_1 = attend(query_1, own_1, other_1, biases)
    middle_1, short_1 = middle_forward(layer_one, attended_1, w_a1, tables[1])
    hidden_1, slope_1 = hidden_forward(short_1, w_b1, tables[1])
    grad_c = grads_of((up_short, hidden_1))
    sc1 = Line(scatter_chunk(*grad_c, 1))

    pushed_1 = hidden_back(up_short, w_c1, slope_1)
    pushed_1 = join(pushed_1, sc1)
    grad_mid_1, proj_1, sums_mid, columns_mid = norm_back(
        5, upstream, pushed_1, w_b1, middle_1, tables[1]
    )
    above_1 = attended_back(proj_1, w_a1)
    grad_bo = grads_of((short_1, pushed_1), (proj_1, attended_1))
    grad_bo, above_1 = join((grad_bo, above_1), sc1)
    sb1 = Line(scatter_chunk(*grad_bo, 1))
    near_a, far_a = attend_back(query_1, own_1, other_1, biases, logs_1, above_1, 0)
    near_a, far_a, above_1 = join((near_a, far_a, above_1), sb1, sc1)
    near_b, far_b = attend_back(query_1, own_1, other_1, biases, logs_1, above_1, 1)
    near_b, far_a, far_b = join((near_b, far_a, far_b), sb1)
    far_a, far_b = swap(far_a, "section"), swap(far_b, "section")
    flat_1 = flat_of((near_a, near_b), (far_a, far_b))
    grad_layer, back_short, sums_in, columns_in = norm_back(
        0, grad_mid_1, flat_1, w_a1, layer_one, tables[1]
    )
    table_1 = table_back(turned, sums_in, columns_in, sums_mid, columns_mid, order_low)
    grad_q = grads_of((normed_1, flat_1), extra=(table_1,))
    grad_q, back_short = join((grad_q, back_short), sb1, sc1)
    sq1 = Line(scatter_chunk(*grad_q, 1))
    grad_c = grads_of((back_short, hidden_0))
    pushed_0 = hidden_back(back_short, w_c0, slope_0)
    grad_c, pushed_0 = join((grad_c, pushed_0), sq1)
    sc0 = Line(scatter_chunk(*grad_c, 0))
    grad_mid_0, proj_0, sums_mid, columns_mid = norm_back(
        5, grad_layer, pushed_0, w_b0, middle_0, tables[0]
    )
    above_0 = attended_back(proj_0, w_a0)
    grad_bo = grads_of((short_0, pushed_0), (proj_0, attended_0))
    result = from_own(hidden_down(middle_1, hidden_1, w_c1, tables[1]))
    grad_bo, result, above_0 = join((grad_bo, result, above_0), sc0, sq1, sc1)
    out = Line(iter_swaps(result, first, side, 1))
    sb0 = Line(scatter_chunk(*grad_bo, 0))
    near_a, far_a = attend_back(query_0, own_0, other_0, biases, logs_0, above_0, 0)
    near_a, far_a, above_0 = join((near_a, far_a, above_0), sb0, sc0, sq1, sb1, out)
    near_b, far_b = attend_back(query_0, own_0, other_0, biases, logs_0, above_0, 1)
    near_b, far_a, far_b = join((near_b, far_a, far_b), sb0, sc0, sb1, sc1)
    far_a, far_b = swap(far_a, "section"), swap(far_b, "section")
    flat_0 = flat_of((near_a, near_b), (far_a, far_b))
    grad_values, _, sums_in, columns_in = norm_back(
        0, grad_mid_0, flat_0, w_a0, values, tables[0]
    )
    table_0 = table_back(turned, sums_in, columns_in, sums_mid, columns_mid, order_low)
    grad_q = grads_of((normed_0, flat_0), extra=(table_0,))
    grad_q = join(grad_q, sb0, sc0, sq1, out)
    sq0 = Line(scatter_chunk(*grad_q, 0))
    into = Line(iter_swaps(from_own(grad_values), first, side, 0), sq0.sent)
    join((), sq0, sc0, sq1)
    join((), sq0, into)
    join((), sq0, sb0)
    lines = [sq0, into, out, sb0, sc0, sq1, sb1, sc1]
    while any(not line.done for line in lines):
        join((), *lines)

    boundary = jnp.where(first, into.result, out.result)

    def cut_up(total, sizes):
        parts, start = [], 0
        for size in sizes:
            parts.append(total[:, start : start + size])
            start += size
        return parts

    three = 3 * third

    def sorted_parts(c, bo, qv):
        return (*cut_up(qv, (three, 128)), *cut_up(bo, (unit, third)), c)

    sums_0 = (sc0.result, sb0.result, sq0.result)
    sums_1 = (sc1.result, sb1.result, sq1.result)
    mine = [sorted_parts(*(total for total, _ in sums)) for sums in (sums_0, sums_1)]
    came = [sorted_parts(*(part for _, part in sums)) for sums in (sums_0, sums_1)]
    grads = [
        jnp.where(first, jnp.concatenate([g, g_far]), jnp.concatenate([h_far, h]))
        for g, g_far, h, h_far in zip(mine[0], came[0], mine[1], came[1])
    ]
    g_q, g_v, g_b, g_o, g_c = grads
    table_grad = lax.dynamic_slice_in_dim(g_v[:, :12], side * cut, cut, 0).T
    return (
        boundary[None],
        table_grad[None],
        g_q.reshape(w_qkv.shape),
        g_o.T[None],
        g_b[None],
        g_c.T[None],
    )


def solution(mesh):
    in_specs = (
        P("section", "dp", "tensor", None),
        P("dp"),
        P("section", None, ("dp", "tensor")),
        P("section", "dp", None, "tensor"),
        P("section", "tensor", "dp"),
        P("section", "dp", "tensor"),
        P("section", "tensor", "dp"),
    )
    out_specs = (
        P("section", "dp", "tensor", None),
        P("section", None, ("dp", "tensor")),
        P("section", "dp", None, "tensor"),
        P("section", "tensor", "dp"),
        P("section", "dp", "tensor"),
        P("section", "tensor", "dp"),
    )
    return jax.shard_map(body, mesh=mesh, in_specs=in_specs, out_specs=out_specs, check_vma=False)
```

time: 692 us -> 502 us (0.73)
  matrix products: 121 us -> 13 us
  other arithmetic: 110 us -> 24.4 us
  Pallas kernels: 89.7 us -> 165 us
  local copies, waits for them, and re-layouts: 82.9 us -> 28.2 us
  starting transfers between devices: 143 us -> 115 us
  between operations: 4.73 us -> 16.3 us
    dot_general x66 -> x2, matrix products: 108 us -> 4.58 us  [dot(): return lax.dot_general(left, right, dims, preferred_element_type=F32)]
    pallas_call x4 -> x49, Pallas kernels: 29.9 us -> 111 us  [the longest x26 68.1 us: call(): pl.pallas_call(kernel, out_shape=outs, in_specs=specs or [pl.BlockSpec(me...]
    ppermute x57 -> x39, starting transfers between devices: 74 us -> 44.1 us  [swap(): return lax.ppermute(array, axis, CROSS)]
    add x24 -> x1, other arithmetic: 23.1 us -> 0.01 us  [body(): spread = spread + swap(spread, 'tensor')]
    concatenate x39 -> x0, other arithmetic: 20.5 us -> none  [the longest x4 5.23 us: attention_back(): far = swap(jnp.concatenate([dk_far, dv_far], 1), 'section')]
    convert_element_type x52 -> x12, other arithmetic: 27.1 us -> 7.53 us  [the longest x6 4.4 us: scatter_chunk(): came, = (yield [(to_core, total.astype(BF16))])]
    ppermute x30 -> x21, waiting for transfers between devices: 34.6 us -> 51.1 us  [pair_swap(): lax.ppermute(array, 'dp', [(i, i ^ bit) for i in range(lax.axis_size('dp'...]
    unnamed x471 -> x165, local copies, waits for them, and re-layouts: 30.3 us -> 14.6 us
  transfers between devices with their start and end apart: 133 -> 98, of which waited for: 38 -> 35; matrix products, arithmetic and copies ran while one was open for 31% -> 9% of each run, Pallas kernels for 12% -> 27%
where the time goes in v2:
time: 502 us; the launch traced here: 494 us
  Pallas kernels  165 us (33%)
  waiting for transfers between devices  132 us (26%)
  starting transfers between devices  115 us (23%)
  local copies, waits for them, and re-layouts  28.2 us (6%)
  other arithmetic  24.4 us (5%)
  between operations  16.3 us (3%)
  matrix products  13 us (3%)
    pallas_call x26, Pallas kernels, call(): pl.pallas_call(kernel, out_shape=outs, in_specs=specs or [pl.BlockSpec(me...  68.1 us
    ppermute x27, waiting for transfers between devices, ring_shift(): return lax.ppermute(array, 'dp', pairs)  64.1 us
    ppermute x21, waiting for transfers between devices, pair_swap(): lax.ppermute(array, 'dp', [(i, i ^ bit) for i in range(lax.axis_size('dp'...  51.1 us
    pallas_call x4, Pallas kernels, attend_back(): pl.pallas_call(partial(attend_back_kernel, 0.125), grid=(groups,), out_sh...  44.8 us
    ppermute x39, starting transfers between devices, swap(): return lax.ppermute(array, axis, CROSS)  44.1 us
    ppermute x27, starting transfers between devices, ring_shift(): return lax.ppermute(array, 'dp', pairs)  27.3 us
    pallas_call x2, Pallas kernels, attend(): pl.pallas_call(partial(attend_kernel, 0.125), grid=(2, groups), out_shape...  27 us
    ppermute x21, starting transfers between devices, pair_swap(): lax.ppermute(array, 'dp', [(i, i ^ bit) for i in range(lax.axis_size('dp'...  18.4 us
  transfers between devices with their start and end apart: 98, of which 35 were waited for; matrix products, arithmetic and copies ran while one was open for 9% of the time, Pallas kernels for 27%

profile of v2, /device:TPU:1, one launch (start us, length us, event | category | flops | bytes accessed | tf_op | source)
XLA Modules:
  0.0 493.6 jit_solution(14418523656985007526)
XLA Ops:
  33.3 4.9 collective-permute-start.5
  38.8 13.9 %collective-permute-done.8.refs_2_ = bf16[48,1536]{1,0:T(8,128)(2,1)S(1)} collective-permute-done((bf16[48,1536]{1,0:T(8,128)(2,1)S(1)}, bf16[48,1536]{1,0:T(8,128)(2,1)S(1)}, u32[]{:S(2)}, u32[]{:S(2)}) %collective-permute-start.8) | collective-permute-done | bytes 147488 | tf_op jit(solution)/shard_map/ppermute | solution.py:37
  63.7 3.6 fusion.72
  68.3 11.4 %collective-permute-done.14.refs_2_ = bf16[48,1536]{1,0:T(8,128)(2,1)S(1)} collective-permute-done((bf16[48,1536]{1,0:T(8,128)(2,1)S(1)}, bf16[48,1536]{1,0:T(8,128)(2,1)S(1)}, u32[]{:S(2)}, u32[]{:S(2)}) %collective-permute-start.14) | collective-permute-done | bytes 147488 | tf_op jit(solution)/shard_map/ppermute | solution.py:37
  81.6 4.5 collective-permute-done.17.refs_4_
  86.7 5.3 %collective-permute-start.18 = (bf16[2,384,1536]{2,1,0:T(8,128)(2,1)S(1)}, bf16[2,384,1536]{2,1,0:T(8,128)(2,1)S(1)}, u32[]{:S(2)}, u32[]{:S(2)}) collective-permute-start(bf16[2,384,1536]{2,1,0:T(8,128)(2,1)S(1)} %bitcast.98), channel_id=1, source_target_pairs={{0,16},{16,0},{1,17},{17,1},{2,18},{18,2},{3,19},{19,3},{4,20},{20... | collective-permute-start | bytes 7077896 | tf_op jit(solution)/shard_map/ppermute | solution.py:27
  97.4 4.1 mixed.2
  109.6 21.6 %collective-permute-done.20.refs_1_ = bf16[192,1536]{1,0:T(8,128)(2,1)S(1)} collective-permute-done((bf16[192,1536]{1,0:T(8,128)(2,1)S(1)}, bf16[192,1536]{1,0:T(8,128)(2,1)S(1)}, u32[]{:S(2)}, u32[]{:S(2)}) %collective-permute-start.20) | collective-permute-done | bytes 589856 | tf_op jit(solution)/shard_map/ppermute | solution.py:31
  135.9 13.8 %attend.2 = (bf16[2,512,384]{2,1,0:T(8,128)(2,1)S(1)}, f32[2,3,8,512]{3,2,1,0:T(8,128)S(1)}) custom-call(bf16[2,512,384]{2,1,0:T(8,128)(2,1)S(1)} %copy-done.44, bf16[2,512,768]{2,1,0:T(8,128)(2,1)} %get-tuple-element.364.k0_ref.v0_ref, bf16[2,512,768]{2,1,0:T(8,128)(2,1)} %collective-permute-done.19.k1_ref.v1_ref, ...), custom_call_target="tpu_custom_call" | custom-call | flops 6442450944 | bytes 3145728 | tf_op jit(solution)/shard_map/attend/pallas_call | solution.py:329
  159.7 4.9 hidden.2
  173.0 7.2 %collective-permute-done.32.refs_4_ = bf16[96,1536]{1,0:T(8,128)(2,1)S(1)} collective-permute-done((bf16[96,1536]{1,0:T(8,128)(2,1)S(1)}, bf16[96,1536]{1,0:T(8,128)(2,1)S(1)}, u32[]{:S(2)}, u32[]{:S(2)}) %collective-permute-start.32) | collective-permute-done | bytes 294944 | tf_op jit(solution)/shard_map/ppermute | solution.py:31
  183.7 3.9 collective-permute-done.33
  201.6 13.1 %attend.3 = (bf16[2,512,384]{2,1,0:T(8,128)(2,1)S(1)}, f32[2,3,8,512]{3,2,1,0:T(8,128)S(1)}) custom-call(bf16[2,512,384]{2,1,0:T(8,128)(2,1)S(1)} %get-tuple-element.403.q_ref, bf16[2,512,768]{2,1,0:T(8,128)(2,1)S(1)} %get-tuple-element.404.k0_ref.v0_ref, bf16[2,512,768]{2,1,0:T(8,128)(2,1)S(1)} %collective-permute-done.34.k1_ref.v1_ref, ...), custom_call_target="tpu_custom_call" | custom-call | flops 6442450944 | bytes 3145728 | tf_op jit(solution)/shard_map/attend/pallas_call | solution.py:329
  216.2 4.9 hidden.3
  232.3 3.6 norm_back.4
  242.5 10.9 %attend_back.4 = (bf16[3,512,384]{2,1,0:T(8,128)(2,1)S(1)}, bf16[2,512,384]{2,1,0:T(8,128)(2,1)S(1)}) custom-call(bf16[2,512,384]{2,1,0:T(8,128)(2,1)S(1)} %get-tuple-element.403.q_ref, bf16[2,512,768]{2,1,0:T(8,128)(2,1)S(1)} %get-tuple-element.404.k0_ref.v0_ref, bf16[2,512,768]{2,1,0:T(8,128)(2,1)S(1)} %collective-permute-done.34.k1_ref.v1_ref, ...), custom_call_target="tpu_custom_call" | custom-call | flops 8053063680 | bytes 2359296 | tf_op jit(solution)/shard_map/attend_back/pallas_call | solution.py:391
  257.8 10.8 %attend_back.5 = (bf16[3,512,384]{2,1,0:T(8,128)(2,1)S(1)}, bf16[2,512,384]{2,1,0:T(8,128)(2,1)S(1)}) custom-call(bf16[2,512,384]{2,1,0:T(8,128)(2,1)S(1)} %get-tuple-element.403.q_ref, bf16[2,512,768]{2,1,0:T(8,128)(2,1)S(1)} %get-tuple-element.404.k0_ref.v0_ref, bf16[2,512,768]{2,1,0:T(8,128)(2,1)S(1)} %collective-permute-done.34.k1_ref.v1_ref, ...), custom_call_target="tpu_custom_call" | custom-call | flops 8053063680 | bytes 2359296 | tf_op jit(solution)/shard_map/attend_back/pallas_call | solution.py:391
  283.3 5.3 %collective-permute-done.48 = bf16[48,1536]{1,0:T(8,128)(2,1)S(1)} collective-permute-done((bf16[48,1536]{1,0:T(8,128)(2,1)S(1)}, bf16[48,1536]{1,0:T(8,128)(2,1)S(1)}, u32[]{:S(2)}, u32[]{:S(2)}) %collective-permute-start.48) | collective-permute-done | bytes 147488 | tf_op jit(solution)/shard_map/ppermute | solution.py:37
  307.7 3.6 norm_back.6
  327.2 11.2 %collective-permute-done.61 = bf16[48,1920]{1,0:T(8,128)(2,1)S(1)} collective-permute-done((bf16[48,1920]{1,0:T(8,128)(2,1)S(1)}, bf16[48,1920]{1,0:T(8,128)(2,1)S(1)}, u32[]{:S(2)}, u32[]{:S(2)}) %collective-permute-start.61) | collective-permute-done | bytes 184352 | tf_op jit(solution)/shard_map/ppermute | solution.py:37
  340.3 11.6 %attend_back.6 = (bf16[3,512,384]{2,1,0:T(8,128)(2,1)S(1)}, bf16[2,512,384]{2,1,0:T(8,128)(2,1)S(1)}) custom-call(bf16[2,512,384]{2,1,0:T(8,128)(2,1)S(1)} %copy-done.45, bf16[2,512,768]{2,1,0:T(8,128)(2,1)} %get-tuple-element.364.k0_ref.v0_ref, bf16[2,512,768]{2,1,0:T(8,128)(2,1)} %collective-permute-done.19.k1_ref.v1_ref, ...), custom_call_target="tpu_custom_call" | custom-call | flops 8053063680 | bytes 2359296 | tf_op jit(solution)/shard_map/attend_back/pallas_call | solution.py:391
  351.9 4.4 collective-permute-done.58.over_x
  363.9 11.6 %attend_back.7 = (bf16[3,512,384]{2,1,0:T(8,128)(2,1)S(1)}, bf16[2,512,384]{2,1,0:T(8,128)(2,1)S(1)}) custom-call(bf16[2,512,384]{2,1,0:T(8,128)(2,1)S(1)} %copy-done.45, bf16[2,512,768]{2,1,0:T(8,128)(2,1)} %get-tuple-element.364.k0_ref.v0_ref, bf16[2,512,768]{2,1,0:T(8,128)(2,1)} %collective-permute-done.19.k1_ref.v1_ref, ...), custom_call_target="tpu_custom_call" | custom-call | flops 8053063680 | bytes 2359296 | tf_op jit(solution)/shard_map/attend_back/pallas_call | solution.py:391
  386.6 5.3 %collective-permute-done.76 = bf16[48,1280]{1,0:T(8,128)(2,1)S(1)} collective-permute-done((bf16[48,1280]{1,0:T(8,128)(2,1)S(1)}, bf16[48,1280]{1,0:T(8,128)(2,1)S(1)}, u32[]{:S(2)}, u32[]{:S(2)}) %collective-permute-start.76) | collective-permute-done | bytes 122912 | tf_op jit(solution)/shard_map/ppermute | solution.py:37
  394.4 3.7 collective-permute-start.73
  398.2 4.2 norm_back.7
  406.6 6.8 %collective-permute-done.74 = bf16[48,1536]{1,0:T(8,128)(2,1)S(1)} collective-permute-done((bf16[48,1536]{1,0:T(8,128)(2,1)S(1)}, bf16[48,1536]{1,0:T(8,128)(2,1)S(1)}, u32[]{:S(2)}, u32[]{:S(2)}) %collective-permute-start.74) | collective-permute-done | bytes 147488 | tf_op jit(solution)/shard_map/ppermute | solution.py:37
  416.5 3.7 fusion.73
  426.7 4.3 collective-permute-start.81
  466.1 4.0 collective-permute-start.95
  470.8 4.2 collective-permute-done.92
  475.1 4.0 collective-permute-start.96
  (484 shorter events, 246.8 us)
Async XLA Ops:
  7.2 162.2 %all-gather.3.cloned.1.call-start = ((), (), s32[]{:S(2)}) async-start(), calls=%async_computation | async-start | bytes 7520256 | tf_op jit(solution)/shard_map/all_gather | solution.py:679
  18.2 34.5 %collective-permute-start.6 = (bf16[512,768]{1,0:T(8,128)(2,1)}, bf16[512,768]{1,0:T(8,128)(2,1)}, u32[]{:S(2)}, u32[]{:S(2)}) collective-permute-start(bf16[512,768]{1,0:T(8,128)(2,1)} %dynamic-slice_bitcast_fusion), channel_id=1, source_target_pairs={{0,1},{1,0},{2,3},{3,2},{4,5},{5,4},{6,7},{7,6},{8,9},{9,8},{10,11... | collective-permute-start | bytes 2359304 | tf_op jit(solution)/shard_map/ppermute | solution.py:27
  31.9 20.7 %collective-permute-start.8 = (bf16[48,1536]{1,0:T(8,128)(2,1)S(1)}, bf16[48,1536]{1,0:T(8,128)(2,1)S(1)}, u32[]{:S(2)}, u32[]{:S(2)}) collective-permute-start(bf16[48,1536]{1,0:T(8,128)(2,1)S(1)} %get-tuple-element.677.refs_0_), channel_id=1, source_target_pairs={{0,8},{2,10},{4,12},{6,14},{8,0},{10,2},{12,4},{14,6},{1,9},{3,11}... | collective-permute-start | bytes 442376 | tf_op jit(solution)/shard_map/ppermute | solution.py:37
  33.3 19.3 %collective-permute-start.7 = (bf16[48,1536]{1,0:T(8,128)(2,1)S(1)}, bf16[48,1536]{1,0:T(8,128)(2,1)S(1)}, u32[]{:S(2)}, u32[]{:S(2)}) collective-permute-start(bf16[48,1536]{1,0:T(8,128)(2,1)S(1)} %get-tuple-element.677.refs_0_), channel_id=1, source_target_pairs={{0,4},{2,6},{4,8},{6,10},{8,12},{10,14},{12,0},{14,2},{1,5},{3,7},... | collective-permute-start | bytes 442376 | tf_op jit(solution)/shard_map/ppermute | solution.py:37
  33.3 19.3 %collective-permute-start.5 = (f32[12,768]{1,0:T(8,128)S(1)}, f32[12,768]{1,0:T(8,128)S(1)}, u32[]{:S(2)}, u32[]{:S(2)}) collective-permute-start(f32[12,768]{1,0:T(8,128)S(1)} %add.244), channel_id=1, source_target_pairs={{0,16},{16,0},{1,17},{17,1},{2,18},{18,2},{3,19},{19,3},{4,20},{20... | collective-permute-start | bytes 110600 | tf_op jit(solution)/shard_map/ppermute | solution.py:27
  53.6 26.1 %collective-permute-start.14 = (bf16[48,1536]{1,0:T(8,128)(2,1)S(1)}, bf16[48,1536]{1,0:T(8,128)(2,1)S(1)}, u32[]{:S(2)}, u32[]{:S(2)}) collective-permute-start(bf16[48,1536]{1,0:T(8,128)(2,1)S(1)} %get-tuple-element.334.refs_0_), channel_id=1, source_target_pairs={{0,8},{2,10},{4,12},{6,14},{8,0},{10,2},{12,4},{14,6},{1,9},{3,11}... | collective-permute-start | bytes 442376 | tf_op jit(solution)/shard_map/ppermute | solution.py:37
  54.0 25.7 %collective-permute-start.13 = (bf16[48,1536]{1,0:T(8,128)(2,1)S(1)}, bf16[48,1536]{1,0:T(8,128)(2,1)S(1)}, u32[]{:S(2)}, u32[]{:S(2)}) collective-permute-start(bf16[48,1536]{1,0:T(8,128)(2,1)S(1)} %get-tuple-element.334.refs_0_), channel_id=1, source_target_pairs={{0,4},{2,6},{4,8},{6,10},{8,12},{10,14},{12,0},{14,2},{1,5},{3,7},... | collective-permute-start | bytes 442376 | tf_op jit(solution)/shard_map/ppermute | solution.py:37
  55.4 24.3 %collective-permute-start.12 = (bf16[192,1536]{1,0:T(8,128)(2,1)S(1)}, bf16[192,1536]{1,0:T(8,128)(2,1)S(1)}, u32[]{:S(2)}, u32[]{:S(2)}) collective-permute-start(bf16[192,1536]{1,0:T(8,128)(2,1)S(1)} %stack_rows.9.refs_0_), channel_id=1, source_target_pairs={{0,1},{1,0},{2,3},{3,2},{4,5},{5,4},{6,7},{7,6},{8,9},{9,8},{10,11... | collective-permute-start | bytes 1769480 | tf_op jit(solution)/shard_map/ppermute | solution.py:27
  62.3 17.7 %collective-permute-start.11 = (bf16[192,1536]{1,0:T(8,128)(2,1)S(1)}, bf16[192,1536]{1,0:T(8,128)(2,1)S(1)}, u32[]{:S(2)}, u32[]{:S(2)}) collective-permute-start(bf16[192,1536]{1,0:T(8,128)(2,1)S(1)} %stack_rows.9.refs_0_), channel_id=1, source_target_pairs={{0,2},{2,0},{4,6},{6,4},{8,10},{10,8},{12,14},{14,12},{1,3},{3,1},... | collective-permute-start | bytes 1769480 | tf_op jit(solution)/shard_map/ppermute | solution.py:31
  103.3 29.2 %collective-permute-start.19 = (bf16[2,512,768]{2,1,0:T(8,128)(2,1)}, bf16[2,512,768]{2,1,0:T(8,128)(2,1)}, u32[]{:S(2)}, u32[]{:S(2)}) collective-permute-start(bf16[2,512,768]{2,1,0:T(8,128)(2,1)} %get-tuple-element.364.k0_ref.v0_ref), channel_id=1, source_target_pairs={{0,16},{16,0},{1,17},{17,1},{2,18},{18,2},{3,19},{19,3},{4,20},{20... | collective-permute-start | bytes 4718600 | tf_op jit(solution)/shard_map/ppermute | solution.py:27
  103.7 27.5 %collective-permute-start.20 = (bf16[192,1536]{1,0:T(8,128)(2,1)S(1)}, bf16[192,1536]{1,0:T(8,128)(2,1)S(1)}, u32[]{:S(2)}, u32[]{:S(2)}) collective-permute-start(bf16[192,1536]{1,0:T(8,128)(2,1)S(1)} %stack_rows.10.refs_0_), channel_id=1, source_target_pairs={{0,2},{2,0},{4,6},{6,4},{8,10},{10,8},{12,14},{14,12},{1,3},{3,1},... | collective-permute-start | bytes 1769480 | tf_op jit(solution)/shard_map/ppermute | solution.py:31
  104.1 28.4 %collective-permute-start.21 = (bf16[192,1536]{1,0:T(8,128)(2,1)S(1)}, bf16[192,1536]{1,0:T(8,128)(2,1)}, u32[]{:S(2)}, u32[]{:S(2)}) collective-permute-start(bf16[192,1536]{1,0:T(8,128)(2,1)S(1)} %stack_rows.10.refs_0_), channel_id=1, source_target_pairs={{0,1},{1,0},{2,3},{3,2},{4,5},{5,4},{6,7},{7,6},{8,9},{9,8},{10,11... | collective-permute-start | bytes 1769480 | tf_op jit(solution)/shard_map/ppermute | solution.py:27
  106.5 43.4 %collective-permute-start.26 = (bf16[48,1536]{1,0:T(8,128)(2,1)}, bf16[48,1536]{1,0:T(8,128)(2,1)S(1)}, u32[]{:S(2)}, u32[]{:S(2)}) collective-permute-start(bf16[48,1536]{1,0:T(8,128)(2,1)} %get-tuple-element.367.refs_0_), channel_id=1, source_target_pairs={{0,12},{2,14},{4,0},{6,2},{8,4},{10,6},{12,8},{14,10},{1,13},{3,15... | collective-permute-start | bytes 442376 | tf_op jit(solution)/shard_map/ppermute | solution.py:37
  109.6 40.3 %collective-permute-start.25 = (bf16[48,1536]{1,0:T(8,128)(2,1)}, bf16[48,1536]{1,0:T(8,128)(2,1)S(1)}, u32[]{:S(2)}, u32[]{:S(2)}) collective-permute-start(bf16[48,1536]{1,0:T(8,128)(2,1)} %get-tuple-element.367.refs_0_), channel_id=1, source_target_pairs={{0,8},{2,10},{4,12},{6,14},{8,0},{10,2},{12,4},{14,6},{1,9},{3,11}... | collective-permute-start | bytes 442376 | tf_op jit(solution)/shard_map/ppermute | solution.py:37
  131.2 18.6 %collective-permute-start.24 = (bf16[48,1536]{1,0:T(8,128)(2,1)}, bf16[48,1536]{1,0:T(8,128)(2,1)S(1)}, u32[]{:S(2)}, u32[]{:S(2)}) collective-permute-start(bf16[48,1536]{1,0:T(8,128)(2,1)} %get-tuple-element.367.refs_0_), channel_id=1, source_target_pairs={{0,4},{2,6},{4,8},{6,10},{8,12},{10,14},{12,0},{14,2},{1,5},{3,7},... | collective-permute-start | bytes 442376 | tf_op jit(solution)/shard_map/ppermute | solution.py:37
  170.4 22.3 %collective-permute-start.30 = (bf16[16,48,4608]{2,1,0:T(8,128)(2,1)}, bf16[16,48,4608]{2,1,0:T(8,128)(2,1)S(1)}, u32[]{:S(2)}, u32[]{:S(2)}) collective-permute-start(bf16[16,48,4608]{2,1,0:T(8,128)(2,1)} %bitcast.91), channel_id=1, source_target_pairs={{0,16},{16,0},{1,17},{17,1},{2,18},{18,2},{3,19},{19,3},{4,20},{20... | collective-permute-start | bytes 21233672 | tf_op jit(solution)/shard_map/ppermute | solution.py:27
  316.8 39.5 %collective-permute-start.55 = (bf16[2,384,1920]{2,1,0:T(8,128)(2,1)S(1)}, bf16[2,384,1920]{2,1,0:T(8,128)(2,1)S(1)}, u32[]{:S(2)}, u32[]{:S(2)}) collective-permute-start(bf16[2,384,1920]{2,1,0:T(8,128)(2,1)S(1)} %get-tuple-element.523), channel_id=1, source_target_pairs={{0,16},{16,0},{1,17},{17,1},{2,18},{18,2},{3,19},{19,3},{4,20},{20... | collective-permute-start | bytes 8847368 | tf_op jit(solution)/shard_map/ppermute | solution.py:27
  318.6 21.3 %collective-permute-start.56 = (bf16[96,1536]{1,0:T(8,128)(2,1)S(1)}, bf16[96,1536]{1,0:T(8,128)(2,1)S(1)}, u32[]{:S(2)}, u32[]{:S(2)}) collective-permute-start(bf16[96,1536]{1,0:T(8,128)(2,1)S(1)} %get-tuple-element.512), channel_id=1, source_target_pairs={{0,1},{1,0},{2,3},{3,2},{4,5},{5,4},{6,7},{7,6},{8,9},{9,8},{10,11... | collective-permute-start | bytes 884744 | tf_op jit(solution)/shard_map/ppermute | solution.py:27
  325.7 30.6 %collective-permute-start.63 = (bf16[512,768]{1,0:T(8,128)(2,1)S(1)}, bf16[512,768]{1,0:T(8,128)(2,1)S(1)}, u32[]{:S(2)}, u32[]{:S(2)}) collective-permute-start(bf16[512,768]{1,0:T(8,128)(2,1)S(1)} %convert_element_type.128), channel_id=1, source_target_pairs={{0,16},{1,17},{2,18},{3,19},{4,20},{5,21},{6,22},{7,23},{8,24},{9,... | collective-permute-start | bytes 2359304 | tf_op jit(solution)/shard_map/ppermute | solution.py:626
  356.5 19.0 %collective-permute-start.64 = (bf16[96,1920]{1,0:T(8,128)(2,1)S(1)}, bf16[96,1920]{1,0:T(8,128)(2,1)S(1)}, u32[]{:S(2)}, u32[]{:S(2)}) collective-permute-start(bf16[96,1920]{1,0:T(8,128)(2,1)S(1)} %get-tuple-element.530), channel_id=1, source_target_pairs={{0,1},{1,0},{2,3},{3,2},{4,5},{5,4},{6,7},{7,6},{8,9},{9,8},{10,11... | collective-permute-start | bytes 1105928 | tf_op jit(solution)/shard_map/ppermute | solution.py:27
  356.9 18.6 %collective-permute-start.65 = (bf16[96,1920]{1,0:T(8,128)(2,1)S(1)}, bf16[96,1920]{1,0:T(8,128)(2,1)S(1)}, u32[]{:S(2)}, u32[]{:S(2)}) collective-permute-start(bf16[96,1920]{1,0:T(8,128)(2,1)S(1)} %get-tuple-element.531), channel_id=1, source_target_pairs={{0,2},{2,0},{4,6},{6,4},{8,10},{10,8},{12,14},{14,12},{1,3},{3,1},... | collective-permute-start | bytes 1105928 | tf_op jit(solution)/shard_map/ppermute | solution.py:31
  358.4 18.8 %collective-permute-start.66 = (bf16[192,1536]{1,0:T(8,128)(2,1)S(1)}, bf16[192,1536]{1,0:T(8,128)(2,1)S(1)}, u32[]{:S(2)}, u32[]{:S(2)}) collective-permute-start(bf16[192,1536]{1,0:T(8,128)(2,1)S(1)} %get-tuple-element.536), channel_id=1, source_target_pairs={{0,2},{2,0},{4,6},{6,4},{8,10},{10,8},{12,14},{14,12},{1,3},{3,1},... | collective-permute-start | bytes 1769480 | tf_op jit(solution)/shard_map/ppermute | solution.py:31
  358.8 18.5 %collective-permute-start.67 = (bf16[192,1536]{1,0:T(8,128)(2,1)S(1)}, bf16[192,1536]{1,0:T(8,128)(2,1)S(1)}, u32[]{:S(2)}, u32[]{:S(2)}) collective-permute-start(bf16[192,1536]{1,0:T(8,128)(2,1)S(1)} %get-tuple-element.537), channel_id=1, source_target_pairs={{0,1},{1,0},{2,3},{3,2},{4,5},{5,4},{6,7},{7,6},{8,9},{9,8},{10,11... | collective-permute-start | bytes 1769480 | tf_op jit(solution)/shard_map/ppermute | solution.py:27
  381.5 32.0 %collective-permute-start.79 = (bf16[512,768]{1,0:T(8,128)(2,1)S(1)}, bf16[512,768]{1,0:T(8,128)(2,1)S(1)}, u32[]{:S(2)}, u32[]{:S(2)}) collective-permute-start(bf16[512,768]{1,0:T(8,128)(2,1)S(1)} %fusion.24), channel_id=1, source_target_pairs={{16,17},{17,16},{18,19},{19,18},{20,21},{21,20},{22,23},{23,22},{2... | collective-permute-start | bytes 2359304 | tf_op jit(solution)/shard_map/ppermute | solution.py:633
  384.5 29.0 %collective-permute-start.71 = (bf16[192,1920]{1,0:T(8,128)(2,1)S(1)}, bf16[192,1920]{1,0:T(8,128)(2,1)S(1)}, u32[]{:S(2)}, u32[]{:S(2)}) collective-permute-start(bf16[192,1920]{1,0:T(8,128)(2,1)S(1)} %get-tuple-element.563), channel_id=1, source_target_pairs={{0,2},{2,0},{4,6},{6,4},{8,10},{10,8},{12,14},{14,12},{1,3},{3,1},... | collective-permute-start | bytes 2211848 | tf_op jit(solution)/shard_map/ppermute | solution.py:31
  385.2 28.3 %collective-permute-start.72 = (bf16[192,1920]{1,0:T(8,128)(2,1)S(1)}, bf16[192,1920]{1,0:T(8,128)(2,1)S(1)}, u32[]{:S(2)}, u32[]{:S(2)}) collective-permute-start(bf16[192,1920]{1,0:T(8,128)(2,1)S(1)} %get-tuple-element.564), channel_id=1, source_target_pairs={{0,1},{1,0},{2,3},{3,2},{4,5},{5,4},{6,7},{7,6},{8,9},{9,8},{10,11... | collective-permute-start | bytes 2211848 | tf_op jit(solution)/shard_map/ppermute | solution.py:27
  416.0 19.6 %collective-permute-start.80 = (bf16[2,384,1280]{2,1,0:T(8,128)(2,1)}, bf16[2,384,1280]{2,1,0:T(8,128)(2,1)}, u32[]{:S(2)}, u32[]{:S(2)}) collective-permute-start(bf16[2,384,1280]{2,1,0:T(8,128)(2,1)} %get-tuple-element.602), channel_id=1, source_target_pairs={{0,16},{16,0},{1,17},{17,1},{2,18},{18,2},{3,19},{19,3},{4,20},{20... | collective-permute-start | bytes 5898248 | tf_op jit(solution)/shard_map/ppermute | solution.py:27
  420.2 20.1 %collective-permute-start.85 = (bf16[512,768]{1,0:T(8,128)(2,1)}, bf16[512,768]{1,0:T(8,128)(2,1)}, u32[]{:S(2)}, u32[]{:S(2)}) collective-permute-start(bf16[512,768]{1,0:T(8,128)(2,1)} %get-tuple-element.606), channel_id=1, source_target_pairs={{16,0},{17,1},{18,2},{19,3},{20,4},{21,5},{22,6},{23,7},{24,8},{25... | collective-permute-start | bytes 2359304 | tf_op jit(solution)/shard_map/ppermute | solution.py:626
  433.3 18.3 %collective-permute-start.88 = (bf16[48,1920]{1,0:T(8,128)(2,1)}, bf16[48,1920]{1,0:T(8,128)(2,1)}, u32[]{:S(2)}, u32[]{:S(2)}) collective-permute-start(bf16[48,1920]{1,0:T(8,128)(2,1)} %get-tuple-element.588), channel_id=1, source_target_pairs={{0,12},{2,14},{4,0},{6,2},{8,4},{10,6},{12,8},{14,10},{1,13},{3,15... | collective-permute-start | bytes 552968 | tf_op jit(solution)/shard_map/ppermute | solution.py:37
  434.2 23.9 %collective-permute-start.89 = (bf16[48,1920]{1,0:T(8,128)(2,1)}, bf16[48,1920]{1,0:T(8,128)(2,1)}, u32[]{:S(2)}, u32[]{:S(2)}) collective-permute-start(bf16[48,1920]{1,0:T(8,128)(2,1)} %get-tuple-element.589), channel_id=1, source_target_pairs={{0,8},{2,10},{4,12},{6,14},{8,0},{10,2},{12,4},{14,6},{1,9},{3,11}... | collective-permute-start | bytes 552968 | tf_op jit(solution)/shard_map/ppermute | solution.py:37
  440.3 17.7 %collective-permute-start.90 = (bf16[48,1920]{1,0:T(8,128)(2,1)S(1)}, bf16[48,1920]{1,0:T(8,128)(2,1)}, u32[]{:S(2)}, u32[]{:S(2)}) collective-permute-start(bf16[48,1920]{1,0:T(8,128)(2,1)S(1)} %get-tuple-element.590), channel_id=1, source_target_pairs={{0,4},{2,6},{4,8},{6,10},{8,12},{10,14},{12,0},{14,2},{1,5},{3,7},... | collective-permute-start | bytes 552968 | tf_op jit(solution)/shard_map/ppermute | solution.py:37
  451.5 23.5 %collective-permute-start.94 = (bf16[512,768]{1,0:T(8,128)(2,1)}, bf16[512,768]{1,0:T(8,128)(2,1)}, u32[]{:S(2)}, u32[]{:S(2)}) collective-permute-start(bf16[512,768]{1,0:T(8,128)(2,1)} %fusion.25), channel_id=1, source_target_pairs={{0,1},{1,0},{2,3},{3,2},{4,5},{5,4},{6,7},{7,6},{8,9},{9,8},{10,11... | collective-permute-start | bytes 2359304 | tf_op jit(solution)/shard_map/ppermute | solution.py:633
  (146 other events, 1246.0 us)
Sparse Core Ops, SparseCore 0:
  12.4 137.0 all-gather.2

commit v3 on v2

--- a/solution.py
+++ b/solution.py
@@ -676,7 +676,7 @@
     one, two = jnp.where(first, halves[0], came), jnp.where(first, came, halves[1])
     cuts = [slice(n * unit, (n + 1) * unit) for n in range(3)]
     chunks = [layer[:, c] for layer in (one,) for c in cuts]
-    far_mine = lax.all_gather(two, ("dp", "tensor"), axis=0)
+    far_mine = lax.all_gather(two[:, : 2 * unit], ("dp", "tensor"), axis=0)
     a0 = Line(gather_chunk(chunks[0]))
     spread, ends = tied((spread, ends_in[0]), a0.sent)
     spread = spread + swap(spread, "tensor")
@@ -737,20 +737,26 @@
     short_0 = join(short_0, b0)
     w_b0 = b0.result
     hidden_0, slope_0 = hidden_forward(short_0, w_b0, tables[0])
-    hidden_0, slope_0, far_mine = join((hidden_0, slope_0, far_mine), c0)
+    hidden_0, slope_0, far_mine, ready = join((hidden_0, slope_0, far_mine, two[:, 2 * unit :]), c0)
     far_theirs = swap(far_mine, "section")
+    c1 = Line(gather_chunk(ready))
     join((), c0)
     hidden_0 = join(hidden_0, c0)
     w_c0 = c0.result
     layer_one = hidden_down(middle_0, hidden_0, w_c0, tables[0])
     place = jnp.stack([spot // 2, spot % 2, side]).astype(jnp.int32)
-    w_a1, w_b1, w_c1 = (pick(place, far_mine, far_theirs, n * unit, unit) for n in range(3))
+    layer_one = join(layer_one, c1)
+    w_a1, w_b1 = (pick(place, far_mine, far_theirs, n * unit, unit) for n in (0, 1))
     normed_1, query_1, own_1 = mixed_forward(layer_one, w_a1, tables[1])
     other_1 = swap(own_1, "section")
     attended_1, logs_1 = attend(query_1, own_1, other_1, biases)
+    attended_1 = join(attended_1, c1)
     middle_1, short_1 = middle_forward(layer_one, attended_1, w_a1, tables[1])
     hidden_1, slope_1 = hidden_forward(short_1, w_b1, tables[1])
+    hidden_1, slope_1 = join((hidden_1, slope_1), c1)
     grad_c = grads_of((up_short, hidden_1))
+    grad_c = join(grad_c, c1)
+    w_c1 = c1.result
     sc1 = Line(scatter_chunk(*grad_c, 1))
 
     pushed_1 = hidden_back(up_short, w_c1, slope_1)

time: 502 us -> 497 us (0.990)
  waiting for transfers between devices: 132 us -> 117 us
  starting transfers between devices: 115 us -> 124 us
    ppermute x27 -> x30, waiting for transfers between devices: 64.1 us -> 45.3 us  [ring_shift(): return lax.ppermute(array, 'dp', pairs)]
    ppermute x39 -> x42, waiting for transfers between devices: 16.5 us -> 29.9 us  [swap(): return lax.ppermute(array, axis, CROSS)]
    ppermute x21 -> x23, waiting for transfers between devices: 51.1 us -> 41.3 us  [pair_swap(): lax.ppermute(array, 'dp', [(i, i ^ bit) for i in range(lax.axis_size('dp'...]
    ppermute x39 -> x42, starting transfers between devices: 44.1 us -> 52.1 us  [swap(): return lax.ppermute(array, axis, CROSS)]
    pallas_call x9 -> x12, Pallas kernels: 9.02 us -> 11.5 us  [stack_rows(): pl.pallas_call(partial(copy_kernel, plan, len(sources)), out_shape=outs,...]
    unnamed x165 -> x177, local copies, waits for them, and re-layouts: 14.6 us -> 16.1 us
    ppermute x27 -> x30, starting transfers between devices: 27.3 us -> 28 us  [ring_shift(): return lax.ppermute(array, 'dp', pairs)]
    ppermute x21 -> x23, starting transfers between devices: 18.4 us -> 18.1 us  [pair_swap(): lax.ppermute(array, 'dp', [(i, i ^ bit) for i in range(lax.axis_size('dp'...]
  transfers between devices with their start and end apart: 98 -> 106, of which waited for: 35 -> 35; matrix products, arithmetic and copies ran while one was open for 9% -> 8% of each run, Pallas kernels for 27% -> 32%
where the time goes in v3:
time: 497 us; the launch traced here: 489 us
  Pallas kernels  166 us (33%)
  starting transfers between devices  124 us (25%)
  waiting for transfers between devices  117 us (24%)
  local copies, waits for them, and re-layouts  29.2 us (6%)
  other arithmetic  21.9 us (4%)
  between operations  16.5 us (3%)
  matrix products  14.1 us (3%)
    pallas_call x26, Pallas kernels, call(): pl.pallas_call(kernel, out_shape=outs, in_specs=specs or [pl.BlockSpec(me...  68.2 us
    ppermute x42, starting transfers between devices, swap(): return lax.ppermute(array, axis, CROSS)  52.1 us
    ppermute x30, waiting for transfers between devices, ring_shift(): return lax.ppermute(array, 'dp', pairs)  45.3 us
    pallas_call x4, Pallas kernels, attend_back(): pl.pallas_call(partial(attend_back_kernel, 0.125), grid=(groups,), out_sh...  44.8 us
    ppermute x23, waiting for transfers between devices, pair_swap(): lax.ppermute(array, 'dp', [(i, i ^ bit) for i in range(lax.axis_size('dp'...  41.3 us
    ppermute x42, waiting for transfers between devices, swap(): return lax.ppermute(array, axis, CROSS)  29.9 us
    ppermute x30, starting transfers between devices, ring_shift(): return lax.ppermute(array, 'dp', pairs)  28 us
    pallas_call x2, Pallas kernels, attend(): pl.pallas_call(partial(attend_kernel, 0.125), grid=(2, groups), out_shape...  27 us
  transfers between devices with their start and end apart: 106, of which 35 were waited for; matrix products, arithmetic and copies ran while one was open for 8% of the time, Pallas kernels for 32%

profile of v3, /device:TPU:1, one launch (start us, length us, event | category | flops | bytes accessed | tf_op | source)
XLA Modules:
  0.0 489.3 jit_solution(17828051249307770317)
XLA Ops:
  30.9 6.4 %collective-permute-start.5 = (f32[12,768]{1,0:T(8,128)S(1)}, f32[12,768]{1,0:T(8,128)S(1)}, u32[]{:S(2)}, u32[]{:S(2)}) collective-permute-start(f32[12,768]{1,0:T(8,128)S(1)} %add.244), channel_id=1, source_target_pairs={{0,16},{16,0},{1,17},{17,1},{2,18},{18,2},{3,19},{19,3},{4,20},{20... | collective-permute-start | bytes 110600 | tf_op jit(solution)/shard_map/ppermute | solution.py:27
  49.9 3.8 collective-permute-start.10
  56.9 3.6 fusion.73
  68.4 7.7 %collective-permute-done.16.refs_3_ = bf16[96,1536]{1,0:T(8,128)(2,1)S(1)} collective-permute-done((bf16[96,1536]{1,0:T(8,128)(2,1)S(1)}, bf16[96,1536]{1,0:T(8,128)(2,1)S(1)}, u32[]{:S(2)}, u32[]{:S(2)}) %collective-permute-start.16) | collective-permute-done | bytes 294944 | tf_op jit(solution)/shard_map/ppermute | solution.py:27
  78.3 4.5 collective-permute-start.18
  88.1 4.1 mixed.2
  98.0 21.8 %collective-permute-done.20.refs_1_ = bf16[192,1536]{1,0:T(8,128)(2,1)S(1)} collective-permute-done((bf16[192,1536]{1,0:T(8,128)(2,1)S(1)}, bf16[192,1536]{1,0:T(8,128)(2,1)S(1)}, u32[]{:S(2)}, u32[]{:S(2)}) %collective-permute-start.20) | collective-permute-done | bytes 589856 | tf_op jit(solution)/shard_map/ppermute | solution.py:31
  123.0 13.8 %attend.2 = (bf16[2,512,384]{2,1,0:T(8,128)(2,1)S(1)}, f32[2,3,8,512]{3,2,1,0:T(8,128)S(1)}) custom-call(bf16[2,512,384]{2,1,0:T(8,128)(2,1)S(1)} %copy-done.52, bf16[2,512,768]{2,1,0:T(8,128)(2,1)} %get-tuple-element.384.k0_ref.v0_ref, bf16[2,512,768]{2,1,0:T(8,128)(2,1)} %collective-permute-done.19.k1_ref.v1_ref, ...), custom_call_target="tpu_custom_call" | custom-call | flops 6442450944 | bytes 3145728 | tf_op jit(solution)/shard_map/attend/pallas_call | solution.py:329
  150.7 4.9 %hidden.2 = (bf16[2,512,1536]{2,1,0:T(8,128)(2,1)S(1)}, bf16[2,512,1536]{2,1,0:T(8,128)(2,1)S(1)}) custom-call(bf16[512,768]{1,0:T(8,128)(2,1)S(1)} %get-tuple-element.398.normed.refs_0_, bf16[768,1536]{1,0:T(8,128)(2,1)S(1)} %get-tuple-element.400.w0, bf16[768,1536]{1,0:T(8,128)(2,1)S(1)} %get-tuple-element.401.w1, f32[12,768]{1,0:T(8,128)S(1)} %copy-done.20), custom_call_target="tpu_custom_call" | custom-call | flops 2415919104 | bytes 11833344 | tf_op jit(solution)/shard_map/hidden/pallas_call | solution.py:241
  163.7 7.0 %collective-permute-done.30.refs_3_ = bf16[96,1536]{1,0:T(8,128)(2,1)S(1)} collective-permute-done((bf16[96,1536]{1,0:T(8,128)(2,1)S(1)}, bf16[96,1536]{1,0:T(8,128)(2,1)S(1)}, u32[]{:S(2)}, u32[]{:S(2)}) %collective-permute-start.30) | collective-permute-done | bytes 294944 | tf_op jit(solution)/shard_map/ppermute | solution.py:27
  183.8 3.6 collective-permute-done.34.refs_2_
  198.8 13.1 %attend.3 = (bf16[2,512,384]{2,1,0:T(8,128)(2,1)S(1)}, f32[2,3,8,512]{3,2,1,0:T(8,128)S(1)}) custom-call(bf16[2,512,384]{2,1,0:T(8,128)(2,1)S(1)} %get-tuple-element.428.q_ref, bf16[2,512,768]{2,1,0:T(8,128)(2,1)S(1)} %get-tuple-element.429.k0_ref.v0_ref, bf16[2,512,768]{2,1,0:T(8,128)(2,1)S(1)} %collective-permute-done.37.k1_ref.v1_ref, ...), custom_call_target="tpu_custom_call" | custom-call | flops 6442450944 | bytes 3145728 | tf_op jit(solution)/shard_map/attend/pallas_call | solution.py:329
  216.2 4.9 %hidden.3 = (bf16[2,512,1536]{2,1,0:T(8,128)(2,1)S(1)}, bf16[2,512,1536]{2,1,0:T(8,128)(2,1)S(1)}) custom-call(bf16[512,768]{1,0:T(8,128)(2,1)S(1)} %get-tuple-element.435.normed.refs_0_, bf16[768,1536]{1,0:T(8,128)(2,1)S(1)} %get-tuple-element.436.w0, bf16[768,1536]{1,0:T(8,128)(2,1)S(1)} %get-tuple-element.437.w1, f32[12,768]{1,0:T(8,128)S(1)} %copy-done.23), custom_call_target="tpu_custom_call" | custom-call | flops 2415919104 | bytes 11833344 | tf_op jit(solution)/shard_map/hidden/pallas_call | solution.py:241
  229.2 3.5 hidden_back.2.parts.refs_2_
  235.3 3.6 norm_back.4
  248.2 11.0 %attend_back.4 = (bf16[3,512,384]{2,1,0:T(8,128)(2,1)S(1)}, bf16[2,512,384]{2,1,0:T(8,128)(2,1)S(1)}) custom-call(bf16[2,512,384]{2,1,0:T(8,128)(2,1)S(1)} %copy-done.57, bf16[2,512,768]{2,1,0:T(8,128)(2,1)S(1)} %copy-done.40, bf16[2,512,768]{2,1,0:T(8,128)(2,1)S(1)} %copy-done.43, bf16[2,512,768]{2,1,0:T(8,128)(2,1)S(1)} %copy-done.40, ...), custom_call_target="tpu_custom_call" | custom-call | flops 8053063680 | bytes 2359296 | tf_op jit(solution)/shard_map/attend_back/pallas_call | solution.py:391
  263.8 10.7 %attend_back.5 = (bf16[3,512,384]{2,1,0:T(8,128)(2,1)S(1)}, bf16[2,512,384]{2,1,0:T(8,128)(2,1)S(1)}) custom-call(bf16[2,512,384]{2,1,0:T(8,128)(2,1)S(1)} %copy-done.58, bf16[2,512,768]{2,1,0:T(8,128)(2,1)S(1)} %copy-done.41, bf16[2,512,768]{2,1,0:T(8,128)(2,1)S(1)} %copy-done.44, bf16[2,512,768]{2,1,0:T(8,128)(2,1)S(1)} %copy-done.41, ...), custom_call_target="tpu_custom_call" | custom-call | flops 8053063680 | bytes 2359296 | tf_op jit(solution)/shard_map/attend_back/pallas_call | solution.py:391
  290.6 5.1 %collective-permute-done.56 = bf16[48,1536]{1,0:T(8,128)(2,1)S(1)} collective-permute-done((bf16[48,1536]{1,0:T(8,128)(2,1)S(1)}, bf16[48,1536]{1,0:T(8,128)(2,1)S(1)}, u32[]{:S(2)}, u32[]{:S(2)}) %collective-permute-start.56) | collective-permute-done | bytes 147488 | tf_op jit(solution)/shard_map/ppermute | solution.py:37
  301.2 3.5 hidden_back.3.parts.refs_2_
  312.7 3.6 norm_back.6
  332.3 11.2 %collective-permute-done.69 = bf16[48,1920]{1,0:T(8,128)(2,1)S(1)} collective-permute-done((bf16[48,1920]{1,0:T(8,128)(2,1)S(1)}, bf16[48,1920]{1,0:T(8,128)(2,1)S(1)}, u32[]{:S(2)}, u32[]{:S(2)}) %collective-permute-start.69) | collective-permute-done | bytes 184352 | tf_op jit(solution)/shard_map/ppermute | solution.py:37
  345.8 11.6 %attend_back.6 = (bf16[3,512,384]{2,1,0:T(8,128)(2,1)S(1)}, bf16[2,512,384]{2,1,0:T(8,128)(2,1)S(1)}) custom-call(bf16[2,512,384]{2,1,0:T(8,128)(2,1)S(1)} %copy-done.53, bf16[2,512,768]{2,1,0:T(8,128)(2,1)} %get-tuple-element.384.k0_ref.v0_ref, bf16[2,512,768]{2,1,0:T(8,128)(2,1)} %collective-permute-done.19.k1_ref.v1_ref, ...), custom_call_target="tpu_custom_call" | custom-call | flops 8053063680 | bytes 2359296 | tf_op jit(solution)/shard_map/attend_back/pallas_call | solution.py:391
  357.4 3.9 collective-permute-done.66.over_x
  367.0 11.6 %attend_back.7 = (bf16[3,512,384]{2,1,0:T(8,128)(2,1)S(1)}, bf16[2,512,384]{2,1,0:T(8,128)(2,1)S(1)}) custom-call(bf16[2,512,384]{2,1,0:T(8,128)(2,1)S(1)} %copy-done.53, bf16[2,512,768]{2,1,0:T(8,128)(2,1)} %get-tuple-element.384.k0_ref.v0_ref, bf16[2,512,768]{2,1,0:T(8,128)(2,1)} %collective-permute-done.19.k1_ref.v1_ref, ...), custom_call_target="tpu_custom_call" | custom-call | flops 8053063680 | bytes 2359296 | tf_op jit(solution)/shard_map/attend_back/pallas_call | solution.py:391
  378.6 4.2 collective-permute-done.74.over_x
  391.7 5.4 %collective-permute-done.84 = bf16[48,1280]{1,0:T(8,128)(2,1)S(1)} collective-permute-done((bf16[48,1280]{1,0:T(8,128)(2,1)S(1)}, bf16[48,1280]{1,0:T(8,128)(2,1)S(1)}, u32[]{:S(2)}, u32[]{:S(2)}) %collective-permute-start.84) | collective-permute-done | bytes 122912 | tf_op jit(solution)/shard_map/ppermute | solution.py:37
  402.9 4.1 norm_back.7
  408.1 3.5 grads.11
  411.6 6.8 %collective-permute-done.82 = bf16[48,1536]{1,0:T(8,128)(2,1)S(1)} collective-permute-done((bf16[48,1536]{1,0:T(8,128)(2,1)S(1)}, bf16[48,1536]{1,0:T(8,128)(2,1)S(1)}, u32[]{:S(2)}, u32[]{:S(2)}) %collective-permute-start.82) | collective-permute-done | bytes 147488 | tf_op jit(solution)/shard_map/ppermute | solution.py:37
  422.2 3.7 fusion.74
  462.5 6.4 %collective-permute-start.103 = (bf16[48,1920]{1,0:T(8,128)(2,1)S(1)}, bf16[48,1920]{1,0:T(8,128)(2,1)S(1)}, u32[]{:S(2)}, u32[]{:S(2)}) collective-permute-start(bf16[48,1920]{1,0:T(8,128)(2,1)S(1)} %get-tuple-element.662), channel_id=1, source_target_pairs={{16,0},{17,1},{18,2},{19,3},{20,4},{21,5},{22,6},{23,7},{24,8},{25... | collective-permute-start | bytes 552968 | tf_op jit(solution)/shard_map/ppermute | solution.py:295
  471.3 5.1 %collective-permute-start.104 = (bf16[48,1280]{1,0:T(8,128)(2,1)S(1)}, bf16[48,1280]{1,0:T(8,128)(2,1)S(1)}, u32[]{:S(2)}, u32[]{:S(2)}) collective-permute-start(bf16[48,1280]{1,0:T(8,128)(2,1)S(1)} %get-tuple-element.686), channel_id=1, source_target_pairs={{16,0},{17,1},{18,2},{19,3},{20,4},{21,5},{22,6},{23,7},{24,8},{25... | collective-permute-start | bytes 368648 | tf_op jit(solution)/shard_map/ppermute | solution.py:295
  (520 shorter events, 255.1 us)
Async XLA Ops:
  7.2 152.8 %all-gather.3.cloned.1.call-start = ((), (), s32[]{:S(2)}) async-start(), calls=%async_computation | async-start | bytes 5013504 | tf_op jit(solution)/shard_map/all_gather | solution.py:679
  17.3 24.0 %collective-permute-start.6 = (bf16[512,768]{1,0:T(8,128)(2,1)S(1)}, bf16[512,768]{1,0:T(8,128)(2,1)S(1)}, u32[]{:S(2)}, u32[]{:S(2)}) collective-permute-start(bf16[512,768]{1,0:T(8,128)(2,1)S(1)} %dynamic-slice_bitcast_fusion), channel_id=1, source_target_pairs={{0,1},{1,0},{2,3},{3,2},{4,5},{5,4},{6,7},{7,6},{8,9},{9,8},{10,11... | collective-permute-start | bytes 2359304 | tf_op jit(solution)/shard_map/ppermute | solution.py:27
  42.2 24.6 %collective-permute-start.11 = (bf16[192,1536]{1,0:T(8,128)(2,1)S(1)}, bf16[192,1536]{1,0:T(8,128)(2,1)S(1)}, u32[]{:S(2)}, u32[]{:S(2)}) collective-permute-start(bf16[192,1536]{1,0:T(8,128)(2,1)S(1)} %stack_rows.12.refs_0_), channel_id=1, source_target_pairs={{0,2},{2,0},{4,6},{6,4},{8,10},{10,8},{12,14},{14,12},{1,3},{3,1},... | collective-permute-start | bytes 1769480 | tf_op jit(solution)/shard_map/ppermute | solution.py:31
  43.4 23.3 %collective-permute-start.12 = (bf16[192,1536]{1,0:T(8,128)(2,1)S(1)}, bf16[192,1536]{1,0:T(8,128)(2,1)S(1)}, u32[]{:S(2)}, u32[]{:S(2)}) collective-permute-start(bf16[192,1536]{1,0:T(8,128)(2,1)S(1)} %stack_rows.12.refs_0_), channel_id=1, source_target_pairs={{0,1},{1,0},{2,3},{3,2},{4,5},{5,4},{6,7},{7,6},{8,9},{9,8},{10,11... | collective-permute-start | bytes 1769480 | tf_op jit(solution)/shard_map/ppermute | solution.py:27
  43.7 18.8 %collective-permute-start.13 = (bf16[48,1536]{1,0:T(8,128)(2,1)S(1)}, bf16[48,1536]{1,0:T(8,128)(2,1)S(1)}, u32[]{:S(2)}, u32[]{:S(2)}) collective-permute-start(bf16[48,1536]{1,0:T(8,128)(2,1)S(1)} %get-tuple-element.354.refs_0_), channel_id=1, source_target_pairs={{0,4},{2,6},{4,8},{6,10},{8,12},{10,14},{12,0},{14,2},{1,5},{3,7},... | collective-permute-start | bytes 442376 | tf_op jit(solution)/shard_map/ppermute | solution.py:37
  47.1 17.1 %collective-permute-start.14 = (bf16[48,1536]{1,0:T(8,128)(2,1)S(1)}, bf16[48,1536]{1,0:T(8,128)(2,1)S(1)}, u32[]{:S(2)}, u32[]{:S(2)}) collective-permute-start(bf16[48,1536]{1,0:T(8,128)(2,1)S(1)} %get-tuple-element.354.refs_0_), channel_id=1, source_target_pairs={{0,8},{2,10},{4,12},{6,14},{8,0},{10,2},{12,4},{14,6},{1,9},{3,11}... | collective-permute-start | bytes 442376 | tf_op jit(solution)/shard_map/ppermute | solution.py:37
  94.1 27.3 %collective-permute-start.19 = (bf16[2,512,768]{2,1,0:T(8,128)(2,1)}, bf16[2,512,768]{2,1,0:T(8,128)(2,1)}, u32[]{:S(2)}, u32[]{:S(2)}) collective-permute-start(bf16[2,512,768]{2,1,0:T(8,128)(2,1)} %get-tuple-element.384.k0_ref.v0_ref), channel_id=1, source_target_pairs={{0,16},{16,0},{1,17},{17,1},{2,18},{18,2},{3,19},{19,3},{4,20},{20... | collective-permute-start | bytes 4718600 | tf_op jit(solution)/shard_map/ppermute | solution.py:27
  94.4 25.4 %collective-permute-start.20 = (bf16[192,1536]{1,0:T(8,128)(2,1)S(1)}, bf16[192,1536]{1,0:T(8,128)(2,1)S(1)}, u32[]{:S(2)}, u32[]{:S(2)}) collective-permute-start(bf16[192,1536]{1,0:T(8,128)(2,1)S(1)} %stack_rows.13.refs_0_), channel_id=1, source_target_pairs={{0,2},{2,0},{4,6},{6,4},{8,10},{10,8},{12,14},{14,12},{1,3},{3,1},... | collective-permute-start | bytes 1769480 | tf_op jit(solution)/shard_map/ppermute | solution.py:31
  95.3 26.0 %collective-permute-start.21 = (bf16[192,1536]{1,0:T(8,128)(2,1)S(1)}, bf16[192,1536]{1,0:T(8,128)(2,1)}, u32[]{:S(2)}, u32[]{:S(2)}) collective-permute-start(bf16[192,1536]{1,0:T(8,128)(2,1)S(1)} %stack_rows.13.refs_0_), channel_id=1, source_target_pairs={{0,1},{1,0},{2,3},{3,2},{4,5},{5,4},{6,7},{7,6},{8,9},{9,8},{10,11... | collective-permute-start | bytes 1769480 | tf_op jit(solution)/shard_map/ppermute | solution.py:27
  97.4 39.5 %collective-permute-start.24 = (bf16[48,1536]{1,0:T(8,128)(2,1)}, bf16[48,1536]{1,0:T(8,128)(2,1)S(1)}, u32[]{:S(2)}, u32[]{:S(2)}) collective-permute-start(bf16[48,1536]{1,0:T(8,128)(2,1)} %get-tuple-element.387.refs_0_), channel_id=1, source_target_pairs={{0,4},{2,6},{4,8},{6,10},{8,12},{10,14},{12,0},{14,2},{1,5},{3,7},... | collective-permute-start | bytes 442376 | tf_op jit(solution)/shard_map/ppermute | solution.py:37
  98.0 38.9 %collective-permute-start.25 = (bf16[48,1536]{1,0:T(8,128)(2,1)}, bf16[48,1536]{1,0:T(8,128)(2,1)S(1)}, u32[]{:S(2)}, u32[]{:S(2)}) collective-permute-start(bf16[48,1536]{1,0:T(8,128)(2,1)} %get-tuple-element.387.refs_0_), channel_id=1, source_target_pairs={{0,8},{2,10},{4,12},{6,14},{8,0},{10,2},{12,4},{14,6},{1,9},{3,11}... | collective-permute-start | bytes 442376 | tf_op jit(solution)/shard_map/ppermute | solution.py:37
  119.9 17.1 %collective-permute-start.26 = (bf16[48,1536]{1,0:T(8,128)(2,1)}, bf16[48,1536]{1,0:T(8,128)(2,1)S(1)}, u32[]{:S(2)}, u32[]{:S(2)}) collective-permute-start(bf16[48,1536]{1,0:T(8,128)(2,1)} %get-tuple-element.387.refs_0_), channel_id=1, source_target_pairs={{0,12},{2,14},{4,0},{6,2},{8,4},{10,6},{12,8},{14,10},{1,13},{3,15... | collective-permute-start | bytes 442376 | tf_op jit(solution)/shard_map/ppermute | solution.py:37
  161.0 27.2 %collective-permute-start.36 = (bf16[16,48,3072]{2,1,0:T(8,128)(2,1)}, bf16[16,48,3072]{2,1,0:T(8,128)(2,1)S(1)}, u32[]{:S(2)}, u32[]{:S(2)}) collective-permute-start(bf16[16,48,3072]{2,1,0:T(8,128)(2,1)} %bitcast.96), channel_id=1, source_target_pairs={{0,16},{16,0},{1,17},{17,1},{2,18},{18,2},{3,19},{19,3},{4,20},{20... | collective-permute-start | bytes 14155784 | tf_op jit(solution)/shard_map/ppermute | solution.py:27
  195.7 16.2 %collective-permute-start.38 = (bf16[192,1536]{1,0:T(8,128)(2,1)S(1)}, bf16[192,1536]{1,0:T(8,128)(2,1)S(1)}, u32[]{:S(2)}, u32[]{:S(2)}) collective-permute-start(bf16[192,1536]{1,0:T(8,128)(2,1)S(1)} %stack_rows.21.refs_0_), channel_id=1, source_target_pairs={{0,2},{2,0},{4,6},{6,4},{8,10},{10,8},{12,14},{14,12},{1,3},{3,1},... | collective-permute-start | bytes 1769480 | tf_op jit(solution)/shard_map/ppermute | solution.py:31
  276.9 18.7 %collective-permute-start.53 = (bf16[192,1920]{1,0:T(8,128)(2,1)S(1)}, bf16[192,1920]{1,0:T(8,128)(2,1)S(1)}, u32[]{:S(2)}, u32[]{:S(2)}) collective-permute-start(bf16[192,1920]{1,0:T(8,128)(2,1)S(1)} %get-tuple-element.500), channel_id=1, source_target_pairs={{0,2},{2,0},{4,6},{6,4},{8,10},{10,8},{12,14},{14,12},{1,3},{3,1},... | collective-permute-start | bytes 2211848 | tf_op jit(solution)/shard_map/ppermute | solution.py:31
  277.5 18.2 %collective-permute-start.54 = (bf16[192,1920]{1,0:T(8,128)(2,1)S(1)}, bf16[192,1920]{1,0:T(8,128)(2,1)S(1)}, u32[]{:S(2)}, u32[]{:S(2)}) collective-permute-start(bf16[192,1920]{1,0:T(8,128)(2,1)S(1)} %get-tuple-element.501), channel_id=1, source_target_pairs={{0,1},{1,0},{2,3},{3,2},{4,5},{5,4},{6,7},{7,6},{8,9},{9,8},{10,11... | collective-permute-start | bytes 2211848 | tf_op jit(solution)/shard_map/ppermute | solution.py:27
  321.3 40.0 %collective-permute-start.63 = (bf16[2,384,1920]{2,1,0:T(8,128)(2,1)S(1)}, bf16[2,384,1920]{2,1,0:T(8,128)(2,1)S(1)}, u32[]{:S(2)}, u32[]{:S(2)}) collective-permute-start(bf16[2,384,1920]{2,1,0:T(8,128)(2,1)S(1)} %get-tuple-element.563), channel_id=1, source_target_pairs={{0,16},{16,0},{1,17},{17,1},{2,18},{18,2},{3,19},{19,3},{4,20},{20... | collective-permute-start | bytes 8847368 | tf_op jit(solution)/shard_map/ppermute | solution.py:27
  323.1 21.9 %collective-permute-start.64 = (bf16[96,1536]{1,0:T(8,128)(2,1)S(1)}, bf16[96,1536]{1,0:T(8,128)(2,1)S(1)}, u32[]{:S(2)}, u32[]{:S(2)}) collective-permute-start(bf16[96,1536]{1,0:T(8,128)(2,1)S(1)} %get-tuple-element.552), channel_id=1, source_target_pairs={{0,1},{1,0},{2,3},{3,2},{4,5},{5,4},{6,7},{7,6},{8,9},{9,8},{10,11... | collective-permute-start | bytes 884744 | tf_op jit(solution)/shard_map/ppermute | solution.py:27
  325.9 17.5 %collective-permute-start.69 = (bf16[48,1920]{1,0:T(8,128)(2,1)S(1)}, bf16[48,1920]{1,0:T(8,128)(2,1)S(1)}, u32[]{:S(2)}, u32[]{:S(2)}) collective-permute-start(bf16[48,1920]{1,0:T(8,128)(2,1)S(1)} %get-tuple-element.520), channel_id=1, source_target_pairs={{0,8},{2,10},{4,12},{6,14},{8,0},{10,2},{12,4},{14,6},{1,9},{3,11}... | collective-permute-start | bytes 552968 | tf_op jit(solution)/shard_map/ppermute | solution.py:37
  327.2 17.0 %collective-permute-start.70 = (bf16[48,1920]{1,0:T(8,128)(2,1)S(1)}, bf16[48,1920]{1,0:T(8,128)(2,1)S(1)}, u32[]{:S(2)}, u32[]{:S(2)}) collective-permute-start(bf16[48,1920]{1,0:T(8,128)(2,1)S(1)} %get-tuple-element.521), channel_id=1, source_target_pairs={{0,4},{2,6},{4,8},{6,10},{8,12},{10,14},{12,0},{14,2},{1,5},{3,7},... | collective-permute-start | bytes 552968 | tf_op jit(solution)/shard_map/ppermute | solution.py:37
  330.8 30.6 %collective-permute-start.71 = (bf16[512,768]{1,0:T(8,128)(2,1)S(1)}, bf16[512,768]{1,0:T(8,128)(2,1)S(1)}, u32[]{:S(2)}, u32[]{:S(2)}) collective-permute-start(bf16[512,768]{1,0:T(8,128)(2,1)S(1)} %convert_element_type.128), channel_id=1, source_target_pairs={{0,16},{1,17},{2,18},{3,19},{4,20},{5,21},{6,22},{7,23},{8,24},{9,... | collective-permute-start | bytes 2359304 | tf_op jit(solution)/shard_map/ppermute | solution.py:626
  344.2 17.1 %collective-permute-start.66 = (bf16[192,1280]{1,0:T(8,128)(2,1)S(1)}, bf16[192,1280]{1,0:T(8,128)(2,1)S(1)}, u32[]{:S(2)}, u32[]{:S(2)}) collective-permute-start(bf16[192,1280]{1,0:T(8,128)(2,1)S(1)} %get-tuple-element.558), channel_id=1, source_target_pairs={{0,2},{2,0},{4,6},{6,4},{8,10},{10,8},{12,14},{14,12},{1,3},{3,1},... | collective-permute-start | bytes 1474568 | tf_op jit(solution)/shard_map/ppermute | solution.py:31
  344.9 16.4 %collective-permute-start.67 = (bf16[192,1280]{1,0:T(8,128)(2,1)S(1)}, bf16[192,1280]{1,0:T(8,128)(2,1)S(1)}, u32[]{:S(2)}, u32[]{:S(2)}) collective-permute-start(bf16[192,1280]{1,0:T(8,128)(2,1)S(1)} %get-tuple-element.559), channel_id=1, source_target_pairs={{0,1},{1,0},{2,3},{3,2},{4,5},{5,4},{6,7},{7,6},{8,9},{9,8},{10,11... | collective-permute-start | bytes 1474568 | tf_op jit(solution)/shard_map/ppermute | solution.py:27
  361.5 17.1 %collective-permute-start.72 = (bf16[96,1920]{1,0:T(8,128)(2,1)S(1)}, bf16[96,1920]{1,0:T(8,128)(2,1)S(1)}, u32[]{:S(2)}, u32[]{:S(2)}) collective-permute-start(bf16[96,1920]{1,0:T(8,128)(2,1)S(1)} %get-tuple-element.570), channel_id=1, source_target_pairs={{0,1},{1,0},{2,3},{3,2},{4,5},{5,4},{6,7},{7,6},{8,9},{9,8},{10,11... | collective-permute-start | bytes 1105928 | tf_op jit(solution)/shard_map/ppermute | solution.py:27
  363.6 19.2 %collective-permute-start.74 = (bf16[192,1536]{1,0:T(8,128)(2,1)S(1)}, bf16[192,1536]{1,0:T(8,128)(2,1)S(1)}, u32[]{:S(2)}, u32[]{:S(2)}) collective-permute-start(bf16[192,1536]{1,0:T(8,128)(2,1)S(1)} %get-tuple-element.576), channel_id=1, source_target_pairs={{0,2},{2,0},{4,6},{6,4},{8,10},{10,8},{12,14},{14,12},{1,3},{3,1},... | collective-permute-start | bytes 1769480 | tf_op jit(solution)/shard_map/ppermute | solution.py:31
  364.4 18.5 %collective-permute-start.75 = (bf16[192,1536]{1,0:T(8,128)(2,1)S(1)}, bf16[192,1536]{1,0:T(8,128)(2,1)S(1)}, u32[]{:S(2)}, u32[]{:S(2)}) collective-permute-start(bf16[192,1536]{1,0:T(8,128)(2,1)S(1)} %get-tuple-element.577), channel_id=1, source_target_pairs={{0,1},{1,0},{2,3},{3,2},{4,5},{5,4},{6,7},{7,6},{8,9},{9,8},{10,11... | collective-permute-start | bytes 1769480 | tf_op jit(solution)/shard_map/ppermute | solution.py:27
  387.0 31.4 %collective-permute-start.87 = (bf16[512,768]{1,0:T(8,128)(2,1)S(1)}, bf16[512,768]{1,0:T(8,128)(2,1)S(1)}, u32[]{:S(2)}, u32[]{:S(2)}) collective-permute-start(bf16[512,768]{1,0:T(8,128)(2,1)S(1)} %fusion.24), channel_id=1, source_target_pairs={{16,17},{17,16},{18,19},{19,18},{20,21},{21,20},{22,23},{23,22},{2... | collective-permute-start | bytes 2359304 | tf_op jit(solution)/shard_map/ppermute | solution.py:633
  389.5 28.9 %collective-permute-start.79 = (bf16[192,1920]{1,0:T(8,128)(2,1)S(1)}, bf16[192,1920]{1,0:T(8,128)(2,1)S(1)}, u32[]{:S(2)}, u32[]{:S(2)}) collective-permute-start(bf16[192,1920]{1,0:T(8,128)(2,1)S(1)} %get-tuple-element.603), channel_id=1, source_target_pairs={{0,2},{2,0},{4,6},{6,4},{8,10},{10,8},{12,14},{14,12},{1,3},{3,1},... | collective-permute-start | bytes 2211848 | tf_op jit(solution)/shard_map/ppermute | solution.py:31
  390.3 28.2 %collective-permute-start.80 = (bf16[192,1920]{1,0:T(8,128)(2,1)S(1)}, bf16[192,1920]{1,0:T(8,128)(2,1)S(1)}, u32[]{:S(2)}, u32[]{:S(2)}) collective-permute-start(bf16[192,1920]{1,0:T(8,128)(2,1)S(1)} %get-tuple-element.604), channel_id=1, source_target_pairs={{0,1},{1,0},{2,3},{3,2},{4,5},{5,4},{6,7},{7,6},{8,9},{9,8},{10,11... | collective-permute-start | bytes 2211848 | tf_op jit(solution)/shard_map/ppermute | solution.py:27
  433.7 16.8 %collective-permute-start.96 = (bf16[48,1920]{1,0:T(8,128)(2,1)}, bf16[48,1920]{1,0:T(8,128)(2,1)}, u32[]{:S(2)}, u32[]{:S(2)}) collective-permute-start(bf16[48,1920]{1,0:T(8,128)(2,1)} %get-tuple-element.628), channel_id=1, source_target_pairs={{0,12},{2,14},{4,0},{6,2},{8,4},{10,6},{12,8},{14,10},{1,13},{3,15... | collective-permute-start | bytes 552968 | tf_op jit(solution)/shard_map/ppermute | solution.py:37
  434.9 20.5 %collective-permute-start.97 = (bf16[48,1920]{1,0:T(8,128)(2,1)}, bf16[48,1920]{1,0:T(8,128)(2,1)}, u32[]{:S(2)}, u32[]{:S(2)}) collective-permute-start(bf16[48,1920]{1,0:T(8,128)(2,1)} %get-tuple-element.629), channel_id=1, source_target_pairs={{0,8},{2,10},{4,12},{6,14},{8,0},{10,2},{12,4},{14,6},{1,9},{3,11}... | collective-permute-start | bytes 552968 | tf_op jit(solution)/shard_map/ppermute | solution.py:37
  450.5 19.4 %collective-permute-start.102 = (bf16[512,768]{1,0:T(8,128)(2,1)}, bf16[512,768]{1,0:T(8,128)(2,1)}, u32[]{:S(2)}, u32[]{:S(2)}) collective-permute-start(bf16[512,768]{1,0:T(8,128)(2,1)} %fusion.25), channel_id=1, source_target_pairs={{0,1},{1,0},{2,3},{3,2},{4,5},{5,4},{6,7},{7,6},{8,9},{9,8},{10,11... | collective-permute-start | bytes 2359304 | tf_op jit(solution)/shard_map/ppermute | solution.py:633
  (160 other events, 1398.5 us)
Sparse Core Ops, SparseCore 0:
  38.2 100.0 all-gather.2

commit v4 on v3

--- a/solution.py
+++ b/solution.py
@@ -726,11 +726,11 @@
     )
     c0 = Line(gather_chunk(ready))
     join((), a0)
-    join((), a0)
+    join((), a0, b0)
     w_a0 = a0.result
     normed_0, query_0, own_0 = mixed_forward(values, w_a0, tables[0])
     other_0 = swap(own_0, "section")
-    query_0, own_0, other_0 = join((query_0, own_0, other_0), b0)
+    query_0, own_0, other_0 = tied((query_0, own_0, other_0), b0.sent)
     attended_0, logs_0 = attend(query_0, own_0, other_0, biases)
     attended_0 = join(attended_0, b0, c0)
     middle_0, short_0 = middle_forward(values, attended_0, w_a0, tables[0])
@@ -783,7 +783,7 @@
     sq1 = Line(scatter_chunk(*grad_q, 1))
     grad_c = grads_of((back_short, hidden_0))
     pushed_0 = hidden_back(back_short, w_c0, slope_0)
-    grad_c, pushed_0 = join((grad_c, pushed_0), sq1)
+    grad_c, pushed_0 = join((grad_c, pushed_0), sq1, sb1)
     sc0 = Line(scatter_chunk(*grad_c, 0))
     grad_mid_0, proj_0, sums_mid, columns_mid = norm_back(
         5, grad_layer, pushed_0, w_b0, middle_0, tables[0]

time: 497 us -> 498 us (level)
  waiting for transfers between devices: 117 us -> 105 us
  starting transfers between devices: 124 us -> 132 us
    ppermute x23, waiting for transfers between devices: 41.3 us -> 30.8 us  [pair_swap(): lax.ppermute(array, 'dp', [(i, i ^ bit) for i in range(lax.axis_size('dp'...]
    ppermute x30, starting transfers between devices: 28 us -> 38.1 us  [ring_shift(): return lax.ppermute(array, 'dp', pairs)]
    unnamed x177 -> x169, local copies, waits for them, and re-layouts: 16.1 us -> 19.9 us
  transfers between devices with their start and end apart: 106 -> 106, of which waited for: 35 -> 34; matrix products, arithmetic and copies ran while one was open for 8% -> 8% of each run, Pallas kernels for 32% -> 32%
where the time goes in v4:
time: 498 us; the launch traced here: 490 us
  Pallas kernels  167 us (34%)
  starting transfers between devices  132 us (27%)
  waiting for transfers between devices  105 us (21%)
  local copies, waits for them, and re-layouts  33.2 us (7%)
  other arithmetic  21.8 us (4%)
  between operations  16.4 us (3%)
  matrix products  13.9 us (3%)
    pallas_call x26, Pallas kernels, call(): pl.pallas_call(kernel, out_shape=outs, in_specs=specs or [pl.BlockSpec(me...  71.2 us
    ppermute x42, starting transfers between devices, swap(): return lax.ppermute(array, axis, CROSS)  51.1 us
    ppermute x30, waiting for transfers between devices, ring_shift(): return lax.ppermute(array, 'dp', pairs)  46 us
    pallas_call x4, Pallas kernels, attend_back(): pl.pallas_call(partial(attend_back_kernel, 0.125), grid=(groups,), out_sh...  44.8 us
    ppermute x30, starting transfers between devices, ring_shift(): return lax.ppermute(array, 'dp', pairs)  38.1 us
    ppermute x23, waiting for transfers between devices, pair_swap(): lax.ppermute(array, 'dp', [(i, i ^ bit) for i in range(lax.axis_size('dp'...  30.8 us
    ppermute x42, waiting for transfers between devices, swap(): return lax.ppermute(array, axis, CROSS)  27.1 us
    pallas_call x2, Pallas kernels, attend(): pl.pallas_call(partial(attend_kernel, 0.125), grid=(2, groups), out_shape...  27 us
  transfers between devices with their start and end apart: 106, of which 34 were waited for; matrix products, arithmetic and copies ran while one was open for 8% of the time, Pallas kernels for 32%

profile of v4, /device:TPU:1, one launch (start us, length us, event | category | flops | bytes accessed | tf_op | source)
XLA Modules:
  0.0 490.1 jit_solution(16030294957726201677)
XLA Ops:
  31.0 6.4 %collective-permute-start.5 = (f32[12,768]{1,0:T(8,128)S(1)}, f32[12,768]{1,0:T(8,128)S(1)}, u32[]{:S(2)}, u32[]{:S(2)}) collective-permute-start(f32[12,768]{1,0:T(8,128)S(1)} %add.244), channel_id=1, source_target_pairs={{0,16},{16,0},{1,17},{17,1},{2,18},{18,2},{3,19},{19,3},{4,20},{20... | collective-permute-start | bytes 110600 | tf_op jit(solution)/shard_map/ppermute | solution.py:27
  50.0 3.7 collective-permute-start.10
  56.9 3.6 fusion.73
  68.5 7.6 %collective-permute-done.16.refs_3_ = bf16[96,1536]{1,0:T(8,128)(2,1)S(1)} collective-permute-done((bf16[96,1536]{1,0:T(8,128)(2,1)S(1)}, bf16[96,1536]{1,0:T(8,128)(2,1)S(1)}, u32[]{:S(2)}, u32[]{:S(2)}) %collective-permute-start.16) | collective-permute-done | bytes 294944 | tf_op jit(solution)/shard_map/ppermute | solution.py:27
  78.3 4.5 collective-permute-start.18
  84.9 13.6 %collective-permute-done.19.refs_1_ = bf16[192,1536]{1,0:T(8,128)(2,1)S(1)} collective-permute-done((bf16[192,1536]{1,0:T(8,128)(2,1)S(1)}, bf16[192,1536]{1,0:T(8,128)(2,1)S(1)}, u32[]{:S(2)}, u32[]{:S(2)}) %collective-permute-start.19) | collective-permute-done | bytes 589856 | tf_op jit(solution)/shard_map/ppermute | solution.py:31
  101.2 4.1 mixed.2
  116.6 13.9 %attend.2 = (bf16[2,512,384]{2,1,0:T(8,128)(2,1)S(1)}, f32[2,3,8,512]{3,2,1,0:T(8,128)S(1)}) custom-call(bf16[2,512,384]{2,1,0:T(8,128)(2,1)S(1)} %copy-done.45, bf16[2,512,768]{2,1,0:T(8,128)(2,1)} %get-tuple-element.380.k0_ref.v0_ref, bf16[2,512,768]{2,1,0:T(8,128)(2,1)} %collective-permute-done.21.k1_ref.v1_ref, ...), custom_call_target="tpu_custom_call" | custom-call | flops 6442450944 | bytes 3145728 | tf_op jit(solution)/shard_map/attend/pallas_call | solution.py:329
  142.3 4.9 %hidden.2 = (bf16[2,512,1536]{2,1,0:T(8,128)(2,1)S(1)}, bf16[2,512,1536]{2,1,0:T(8,128)(2,1)S(1)}) custom-call(bf16[512,768]{1,0:T(8,128)(2,1)S(1)} %get-tuple-element.394.normed.refs_0_, bf16[768,1536]{1,0:T(8,128)(2,1)S(1)} %get-tuple-element.396.w0, bf16[768,1536]{1,0:T(8,128)(2,1)S(1)} %get-tuple-element.397.w1, f32[12,768]{1,0:T(8,128)S(1)} %copy-done.22), custom_call_target="tpu_custom_call" | custom-call | flops 2415919104 | bytes 11833344 | tf_op jit(solution)/shard_map/hidden/pallas_call | solution.py:241
  155.3 7.1 %collective-permute-done.30.refs_3_ = bf16[96,1536]{1,0:T(8,128)(2,1)S(1)} collective-permute-done((bf16[96,1536]{1,0:T(8,128)(2,1)S(1)}, bf16[96,1536]{1,0:T(8,128)(2,1)S(1)}, u32[]{:S(2)}, u32[]{:S(2)}) %collective-permute-start.30) | collective-permute-done | bytes 294944 | tf_op jit(solution)/shard_map/ppermute | solution.py:27
  166.2 5.8 %collective-permute-start.33 = (bf16[48,1536]{1,0:T(8,128)(2,1)S(1)}, bf16[48,1536]{1,0:T(8,128)(2,1)S(1)}, u32[]{:S(2)}, u32[]{:S(2)}) collective-permute-start(bf16[48,1536]{1,0:T(8,128)(2,1)S(1)} %copy-done.29), channel_id=1, source_target_pairs={{0,4},{2,6},{4,8},{6,10},{8,12},{10,14},{12,0},{14,2},{1,5},{3,7},... | collective-permute-start | bytes 442376 | tf_op jit(solution)/shard_map/ppermute | solution.py:37
  193.5 13.1 %attend.3 = (bf16[2,512,384]{2,1,0:T(8,128)(2,1)S(1)}, f32[2,3,8,512]{3,2,1,0:T(8,128)S(1)}) custom-call(bf16[2,512,384]{2,1,0:T(8,128)(2,1)S(1)} %get-tuple-element.424.q_ref, bf16[2,512,768]{2,1,0:T(8,128)(2,1)S(1)} %get-tuple-element.425.k0_ref.v0_ref, bf16[2,512,768]{2,1,0:T(8,128)(2,1)S(1)} %collective-permute-done.37.k1_ref.v1_ref, ...), custom_call_target="tpu_custom_call" | custom-call | flops 6442450944 | bytes 3145728 | tf_op jit(solution)/shard_map/attend/pallas_call | solution.py:329
  210.9 4.9 %hidden.3 = (bf16[2,512,1536]{2,1,0:T(8,128)(2,1)S(1)}, bf16[2,512,1536]{2,1,0:T(8,128)(2,1)S(1)}) custom-call(bf16[512,768]{1,0:T(8,128)(2,1)S(1)} %get-tuple-element.431.normed.refs_0_, bf16[768,1536]{1,0:T(8,128)(2,1)S(1)} %get-tuple-element.432.w0, bf16[768,1536]{1,0:T(8,128)(2,1)S(1)} %get-tuple-element.433.w1, f32[12,768]{1,0:T(8,128)S(1)} %copy-done.24), custom_call_target="tpu_custom_call" | custom-call | flops 2415919104 | bytes 11833344 | tf_op jit(solution)/shard_map/hidden/pallas_call | solution.py:241
  217.9 4.1 grads.6
  232.4 3.6 norm_back.4
  237.2 5.1 %grads.7 = (bf16[2,384,1920]{2,1,0:T(8,128)(2,1)S(1)}, bf16[2,384,1920]{2,1,0:T(8,128)(2,1)}) custom-call(bf16[512,768]{1,0:T(8,128)(2,1)S(1)} %copy-done.41, bf16[512,768]{1,0:T(8,128)(2,1)S(1)} %get-tuple-element.457.refs_1_.short, bf16[2,512,1536]{2,1,0:T(8,128)(2,1)S(1)} %hidden_back.2.parts.refs_2_, ...), custom_call_target="tpu_custom_call" | custom-call | flops 3019898880 | bytes 11403264 | tf_op jit(solution)/shard_map/grads/pallas_call | solution.py:241
  245.1 11.0 %attend_back.4 = (bf16[3,512,384]{2,1,0:T(8,128)(2,1)S(1)}, bf16[2,512,384]{2,1,0:T(8,128)(2,1)S(1)}) custom-call(bf16[2,512,384]{2,1,0:T(8,128)(2,1)S(1)} %copy-done.50, bf16[2,512,768]{2,1,0:T(8,128)(2,1)S(1)} %get-tuple-element.425.k0_ref.v0_ref, bf16[2,512,768]{2,1,0:T(8,128)(2,1)S(1)} %copy-done.37, ...), custom_call_target="tpu_custom_call" | custom-call | flops 8053063680 | bytes 2359296 | tf_op jit(solution)/shard_map/attend_back/pallas_call | solution.py:391
  261.9 10.8 %attend_back.5 = (bf16[3,512,384]{2,1,0:T(8,128)(2,1)S(1)}, bf16[2,512,384]{2,1,0:T(8,128)(2,1)S(1)}) custom-call(bf16[2,512,384]{2,1,0:T(8,128)(2,1)S(1)} %copy-done.51, bf16[2,512,768]{2,1,0:T(8,128)(2,1)S(1)} %get-tuple-element.425.k0_ref.v0_ref, bf16[2,512,768]{2,1,0:T(8,128)(2,1)S(1)} %copy-done.37, ...), custom_call_target="tpu_custom_call" | custom-call | flops 8053063680 | bytes 2359296 | tf_op jit(solution)/shard_map/attend_back/pallas_call | solution.py:391
  277.1 4.7 collective-permute-start.55
  289.5 5.1 %collective-permute-done.56 = bf16[48,1536]{1,0:T(8,128)(2,1)S(1)} collective-permute-done((bf16[48,1536]{1,0:T(8,128)(2,1)S(1)}, bf16[48,1536]{1,0:T(8,128)(2,1)S(1)}, u32[]{:S(2)}, u32[]{:S(2)}) %collective-permute-start.56) | collective-permute-done | bytes 147488 | tf_op jit(solution)/shard_map/ppermute | solution.py:37
  297.1 3.7 collective-permute-start.59
  307.7 9.4 %collective-permute-done.60 = bf16[48,1920]{1,0:T(8,128)(2,1)S(1)} collective-permute-done((bf16[48,1920]{1,0:T(8,128)(2,1)S(1)}, bf16[48,1920]{1,0:T(8,128)(2,1)S(1)}, u32[]{:S(2)}, u32[]{:S(2)}) %collective-permute-start.60) | collective-permute-done | bytes 184352 | tf_op jit(solution)/shard_map/ppermute | solution.py:37
  326.4 3.6 norm_back.6
  346.3 11.6 %attend_back.6 = (bf16[3,512,384]{2,1,0:T(8,128)(2,1)S(1)}, bf16[2,512,384]{2,1,0:T(8,128)(2,1)S(1)}) custom-call(bf16[2,512,384]{2,1,0:T(8,128)(2,1)S(1)} %copy-done.46, bf16[2,512,768]{2,1,0:T(8,128)(2,1)} %get-tuple-element.380.k0_ref.v0_ref, bf16[2,512,768]{2,1,0:T(8,128)(2,1)} %collective-permute-done.21.k1_ref.v1_ref, ...), custom_call_target="tpu_custom_call" | custom-call | flops 8053063680 | bytes 2359296 | tf_op jit(solution)/shard_map/attend_back/pallas_call | solution.py:391
  363.9 11.6 %attend_back.7 = (bf16[3,512,384]{2,1,0:T(8,128)(2,1)S(1)}, bf16[2,512,384]{2,1,0:T(8,128)(2,1)S(1)}) custom-call(bf16[2,512,384]{2,1,0:T(8,128)(2,1)S(1)} %copy-done.46, bf16[2,512,768]{2,1,0:T(8,128)(2,1)} %get-tuple-element.380.k0_ref.v0_ref, bf16[2,512,768]{2,1,0:T(8,128)(2,1)} %collective-permute-done.21.k1_ref.v1_ref, ...), custom_call_target="tpu_custom_call" | custom-call | flops 8053063680 | bytes 2359296 | tf_op jit(solution)/shard_map/attend_back/pallas_call | solution.py:391
  375.5 4.6 collective-permute-done.75.over_x
  394.1 7.0 %collective-permute-done.85 = bf16[48,1280]{1,0:T(8,128)(2,1)S(1)} collective-permute-done((bf16[48,1280]{1,0:T(8,128)(2,1)S(1)}, bf16[48,1280]{1,0:T(8,128)(2,1)S(1)}, u32[]{:S(2)}, u32[]{:S(2)}) %collective-permute-start.85) | collective-permute-done | bytes 122912 | tf_op jit(solution)/shard_map/ppermute | solution.py:37
  401.3 4.2 norm_back.7
  411.0 7.4 %collective-permute-done.82 = bf16[48,1536]{1,0:T(8,128)(2,1)S(1)} collective-permute-done((bf16[48,1536]{1,0:T(8,128)(2,1)S(1)}, bf16[48,1536]{1,0:T(8,128)(2,1)S(1)}, u32[]{:S(2)}, u32[]{:S(2)}) %collective-permute-start.82) | collective-permute-done | bytes 147488 | tf_op jit(solution)/shard_map/ppermute | solution.py:37
  422.1 3.7 fusion.74
  463.5 5.9 %collective-permute-start.103 = (bf16[48,1920]{1,0:T(8,128)(2,1)S(1)}, bf16[48,1920]{1,0:T(8,128)(2,1)S(1)}, u32[]{:S(2)}, u32[]{:S(2)}) collective-permute-start(bf16[48,1920]{1,0:T(8,128)(2,1)S(1)} %get-tuple-element.658), channel_id=1, source_target_pairs={{16,0},{17,1},{18,2},{19,3},{20,4},{21,5},{22,6},{23,7},{24,8},{25... | collective-permute-start | bytes 552968 | tf_op jit(solution)/shard_map/ppermute | solution.py:295
  472.6 4.6 collective-permute-start.104
  (512 shorter events, 259.0 us)
Async XLA Ops:
  7.2 144.1 %all-gather.3.cloned.1.call-start = ((), (), s32[]{:S(2)}) async-start(), calls=%async_computation | async-start | bytes 5013504 | tf_op jit(solution)/shard_map/all_gather | solution.py:679
  17.3 24.2 %collective-permute-start.6 = (bf16[512,768]{1,0:T(8,128)(2,1)S(1)}, bf16[512,768]{1,0:T(8,128)(2,1)}, u32[]{:S(2)}, u32[]{:S(2)}) collective-permute-start(bf16[512,768]{1,0:T(8,128)(2,1)S(1)} %dynamic-slice_bitcast_fusion), channel_id=1, source_target_pairs={{0,1},{1,0},{2,3},{3,2},{4,5},{5,4},{6,7},{7,6},{8,9},{9,8},{10,11... | collective-permute-start | bytes 2359304 | tf_op jit(solution)/shard_map/ppermute | solution.py:27
  42.4 24.3 %collective-permute-start.11 = (bf16[192,1536]{1,0:T(8,128)(2,1)S(1)}, bf16[192,1536]{1,0:T(8,128)(2,1)S(1)}, u32[]{:S(2)}, u32[]{:S(2)}) collective-permute-start(bf16[192,1536]{1,0:T(8,128)(2,1)S(1)} %stack_rows.12.refs_0_), channel_id=1, source_target_pairs={{0,2},{2,0},{4,6},{6,4},{8,10},{10,8},{12,14},{14,12},{1,3},{3,1},... | collective-permute-start | bytes 1769480 | tf_op jit(solution)/shard_map/ppermute | solution.py:31
  43.7 23.0 %collective-permute-start.12 = (bf16[192,1536]{1,0:T(8,128)(2,1)S(1)}, bf16[192,1536]{1,0:T(8,128)(2,1)S(1)}, u32[]{:S(2)}, u32[]{:S(2)}) collective-permute-start(bf16[192,1536]{1,0:T(8,128)(2,1)S(1)} %stack_rows.12.refs_0_), channel_id=1, source_target_pairs={{0,1},{1,0},{2,3},{3,2},{4,5},{5,4},{6,7},{7,6},{8,9},{9,8},{10,11... | collective-permute-start | bytes 1769480 | tf_op jit(solution)/shard_map/ppermute | solution.py:27
  43.9 18.6 %collective-permute-start.13 = (bf16[48,1536]{1,0:T(8,128)(2,1)S(1)}, bf16[48,1536]{1,0:T(8,128)(2,1)S(1)}, u32[]{:S(2)}, u32[]{:S(2)}) collective-permute-start(bf16[48,1536]{1,0:T(8,128)(2,1)S(1)} %get-tuple-element.352.refs_0_), channel_id=1, source_target_pairs={{0,4},{2,6},{4,8},{6,10},{8,12},{10,14},{12,0},{14,2},{1,5},{3,7},... | collective-permute-start | bytes 442376 | tf_op jit(solution)/shard_map/ppermute | solution.py:37
  47.4 17.2 %collective-permute-start.14 = (bf16[48,1536]{1,0:T(8,128)(2,1)S(1)}, bf16[48,1536]{1,0:T(8,128)(2,1)S(1)}, u32[]{:S(2)}, u32[]{:S(2)}) collective-permute-start(bf16[48,1536]{1,0:T(8,128)(2,1)S(1)} %get-tuple-element.352.refs_0_), channel_id=1, source_target_pairs={{0,8},{2,10},{4,12},{6,14},{8,0},{10,2},{12,4},{14,6},{1,9},{3,11}... | collective-permute-start | bytes 442376 | tf_op jit(solution)/shard_map/ppermute | solution.py:37
  78.3 21.1 %collective-permute-start.18 = (bf16[2,384,1536]{2,1,0:T(8,128)(2,1)S(1)}, bf16[2,384,1536]{2,1,0:T(8,128)(2,1)S(1)}, u32[]{:S(2)}, u32[]{:S(2)}) collective-permute-start(bf16[2,384,1536]{2,1,0:T(8,128)(2,1)S(1)} %bitcast.101), channel_id=1, source_target_pairs={{0,16},{16,0},{1,17},{17,1},{2,18},{18,2},{3,19},{19,3},{4,20},{20... | collective-permute-start | bytes 7077896 | tf_op jit(solution)/shard_map/ppermute | solution.py:27
  111.9 19.3 %collective-permute-start.24 = (bf16[48,1536]{1,0:T(8,128)(2,1)}, bf16[48,1536]{1,0:T(8,128)(2,1)S(1)}, u32[]{:S(2)}, u32[]{:S(2)}) collective-permute-start(bf16[48,1536]{1,0:T(8,128)(2,1)} %get-tuple-element.383.refs_0_), channel_id=1, source_target_pairs={{0,4},{2,6},{4,8},{6,10},{8,12},{10,14},{12,0},{14,2},{1,5},{3,7},... | collective-permute-start | bytes 442376 | tf_op jit(solution)/shard_map/ppermute | solution.py:37
  112.7 20.1 %collective-permute-start.25 = (bf16[48,1536]{1,0:T(8,128)(2,1)}, bf16[48,1536]{1,0:T(8,128)(2,1)S(1)}, u32[]{:S(2)}, u32[]{:S(2)}) collective-permute-start(bf16[48,1536]{1,0:T(8,128)(2,1)} %get-tuple-element.383.refs_0_), channel_id=1, source_target_pairs={{0,8},{2,10},{4,12},{6,14},{8,0},{10,2},{12,4},{14,6},{1,9},{3,11}... | collective-permute-start | bytes 442376 | tf_op jit(solution)/shard_map/ppermute | solution.py:37
  112.7 20.1 %collective-permute-start.26 = (bf16[48,1536]{1,0:T(8,128)(2,1)}, bf16[48,1536]{1,0:T(8,128)(2,1)S(1)}, u32[]{:S(2)}, u32[]{:S(2)}) collective-permute-start(bf16[48,1536]{1,0:T(8,128)(2,1)} %get-tuple-element.383.refs_0_), channel_id=1, source_target_pairs={{0,12},{2,14},{4,0},{6,2},{8,4},{10,6},{12,8},{14,10},{1,13},{3,15... | collective-permute-start | bytes 442376 | tf_op jit(solution)/shard_map/ppermute | solution.py:37
  116.5 16.4 %collective-permute-start.22 = (bf16[96,1536]{1,0:T(8,128)(2,1)S(1)}, bf16[96,1536]{1,0:T(8,128)(2,1)S(1)}, u32[]{:S(2)}, u32[]{:S(2)}) collective-permute-start(bf16[96,1536]{1,0:T(8,128)(2,1)S(1)} %slice.179), channel_id=1, source_target_pairs={{0,1},{1,0},{2,3},{3,2},{4,5},{5,4},{6,7},{7,6},{8,9},{9,8},{10,11... | collective-permute-start | bytes 884744 | tf_op jit(solution)/shard_map/ppermute | solution.py:27
  116.5 16.3 %collective-permute-start.23 = (bf16[96,1536]{1,0:T(8,128)(2,1)S(1)}, bf16[96,1536]{1,0:T(8,128)(2,1)S(1)}, u32[]{:S(2)}, u32[]{:S(2)}) collective-permute-start(bf16[96,1536]{1,0:T(8,128)(2,1)S(1)} %slice.180), channel_id=1, source_target_pairs={{0,2},{2,0},{4,6},{6,4},{8,10},{10,8},{12,14},{14,12},{1,3},{3,1},... | collective-permute-start | bytes 884744 | tf_op jit(solution)/shard_map/ppermute | solution.py:31
  152.3 31.7 %collective-permute-start.36 = (bf16[16,48,3072]{2,1,0:T(8,128)(2,1)}, bf16[16,48,3072]{2,1,0:T(8,128)(2,1)S(1)}, u32[]{:S(2)}, u32[]{:S(2)}) collective-permute-start(bf16[16,48,3072]{2,1,0:T(8,128)(2,1)} %bitcast.96), channel_id=1, source_target_pairs={{0,16},{16,0},{1,17},{17,1},{2,18},{18,2},{3,19},{19,3},{4,20},{20... | collective-permute-start | bytes 14155784 | tf_op jit(solution)/shard_map/ppermute | solution.py:27
  242.7 16.3 %collective-permute-start.46 = (bf16[2,384,1920]{2,1,0:T(8,128)(2,1)}, bf16[2,384,1920]{2,1,0:T(8,128)(2,1)S(1)}, u32[]{:S(2)}, u32[]{:S(2)}) collective-permute-start(bf16[2,384,1920]{2,1,0:T(8,128)(2,1)} %get-tuple-element.470), channel_id=1, source_target_pairs={{0,16},{16,0},{1,17},{17,1},{2,18},{18,2},{3,19},{19,3},{4,20},{20... | collective-permute-start | bytes 8847368 | tf_op jit(solution)/shard_map/ppermute | solution.py:27
  275.0 19.6 %collective-permute-start.53 = (bf16[192,1920]{1,0:T(8,128)(2,1)S(1)}, bf16[192,1920]{1,0:T(8,128)(2,1)S(1)}, u32[]{:S(2)}, u32[]{:S(2)}) collective-permute-start(bf16[192,1920]{1,0:T(8,128)(2,1)S(1)} %get-tuple-element.496), channel_id=1, source_target_pairs={{0,2},{2,0},{4,6},{6,4},{8,10},{10,8},{12,14},{14,12},{1,3},{3,1},... | collective-permute-start | bytes 2211848 | tf_op jit(solution)/shard_map/ppermute | solution.py:31
  275.9 18.8 %collective-permute-start.54 = (bf16[192,1920]{1,0:T(8,128)(2,1)S(1)}, bf16[192,1920]{1,0:T(8,128)(2,1)S(1)}, u32[]{:S(2)}, u32[]{:S(2)}) collective-permute-start(bf16[192,1920]{1,0:T(8,128)(2,1)S(1)} %get-tuple-element.497), channel_id=1, source_target_pairs={{0,1},{1,0},{2,3},{3,2},{4,5},{5,4},{6,7},{7,6},{8,9},{9,8},{10,11... | collective-permute-start | bytes 2211848 | tf_op jit(solution)/shard_map/ppermute | solution.py:27
  295.8 21.3 %collective-permute-start.58 = (bf16[2,384,1280]{2,1,0:T(8,128)(2,1)S(1)}, bf16[2,384,1280]{2,1,0:T(8,128)(2,1)S(1)}, u32[]{:S(2)}, u32[]{:S(2)}) collective-permute-start(bf16[2,384,1280]{2,1,0:T(8,128)(2,1)S(1)} %get-tuple-element.527), channel_id=1, source_target_pairs={{0,16},{16,0},{1,17},{17,1},{2,18},{18,2},{3,19},{19,3},{4,20},{20... | collective-permute-start | bytes 5898248 | tf_op jit(solution)/shard_map/ppermute | solution.py:27
  300.8 16.3 %collective-permute-start.60 = (bf16[48,1920]{1,0:T(8,128)(2,1)S(1)}, bf16[48,1920]{1,0:T(8,128)(2,1)S(1)}, u32[]{:S(2)}, u32[]{:S(2)}) collective-permute-start(bf16[48,1920]{1,0:T(8,128)(2,1)S(1)} %get-tuple-element.516), channel_id=1, source_target_pairs={{0,8},{2,10},{4,12},{6,14},{8,0},{10,2},{12,4},{14,6},{1,9},{3,11}... | collective-permute-start | bytes 552968 | tf_op jit(solution)/shard_map/ppermute | solution.py:37
  300.8 16.3 %collective-permute-start.61 = (bf16[48,1920]{1,0:T(8,128)(2,1)S(1)}, bf16[48,1920]{1,0:T(8,128)(2,1)S(1)}, u32[]{:S(2)}, u32[]{:S(2)}) collective-permute-start(bf16[48,1920]{1,0:T(8,128)(2,1)S(1)} %get-tuple-element.517), channel_id=1, source_target_pairs={{0,4},{2,6},{4,8},{6,10},{8,12},{10,14},{12,0},{14,2},{1,5},{3,7},... | collective-permute-start | bytes 552968 | tf_op jit(solution)/shard_map/ppermute | solution.py:37
  317.4 17.2 %collective-permute-start.62 = (bf16[2,384,1536]{2,1,0:T(8,128)(2,1)S(1)}, bf16[2,384,1536]{2,1,0:T(8,128)(2,1)S(1)}, u32[]{:S(2)}, u32[]{:S(2)}) collective-permute-start(bf16[2,384,1536]{2,1,0:T(8,128)(2,1)S(1)} %get-tuple-element.546), channel_id=1, source_target_pairs={{0,16},{16,0},{1,17},{17,1},{2,18},{18,2},{3,19},{19,3},{4,20},{20... | collective-permute-start | bytes 7077896 | tf_op jit(solution)/shard_map/ppermute | solution.py:27
  335.5 23.0 %collective-permute-start.66 = (bf16[2,384,1920]{2,1,0:T(8,128)(2,1)S(1)}, bf16[2,384,1920]{2,1,0:T(8,128)(2,1)S(1)}, u32[]{:S(2)}, u32[]{:S(2)}) collective-permute-start(bf16[2,384,1920]{2,1,0:T(8,128)(2,1)S(1)} %get-tuple-element.564), channel_id=1, source_target_pairs={{0,16},{16,0},{1,17},{17,1},{2,18},{18,2},{3,19},{19,3},{4,20},{20... | collective-permute-start | bytes 8847368 | tf_op jit(solution)/shard_map/ppermute | solution.py:27
  339.1 19.4 %collective-permute-start.72 = (bf16[512,768]{1,0:T(8,128)(2,1)S(1)}, bf16[512,768]{1,0:T(8,128)(2,1)S(1)}, u32[]{:S(2)}, u32[]{:S(2)}) collective-permute-start(bf16[512,768]{1,0:T(8,128)(2,1)S(1)} %convert_element_type.132), channel_id=1, source_target_pairs={{0,16},{1,17},{2,18},{3,19},{4,20},{5,21},{6,22},{7,23},{8,24},{9,... | collective-permute-start | bytes 2359304 | tf_op jit(solution)/shard_map/ppermute | solution.py:626
  340.6 17.3 %collective-permute-start.68 = (bf16[96,1536]{1,0:T(8,128)(2,1)S(1)}, bf16[96,1536]{1,0:T(8,128)(2,1)S(1)}, u32[]{:S(2)}, u32[]{:S(2)}) collective-permute-start(bf16[96,1536]{1,0:T(8,128)(2,1)S(1)} %get-tuple-element.554), channel_id=1, source_target_pairs={{0,2},{2,0},{4,6},{6,4},{8,10},{10,8},{12,14},{14,12},{1,3},{3,1},... | collective-permute-start | bytes 884744 | tf_op jit(solution)/shard_map/ppermute | solution.py:31
  358.7 16.8 %collective-permute-start.73 = (bf16[96,1920]{1,0:T(8,128)(2,1)S(1)}, bf16[96,1920]{1,0:T(8,128)(2,1)S(1)}, u32[]{:S(2)}, u32[]{:S(2)}) collective-permute-start(bf16[96,1920]{1,0:T(8,128)(2,1)S(1)} %get-tuple-element.571), channel_id=1, source_target_pairs={{0,1},{1,0},{2,3},{3,2},{4,5},{5,4},{6,7},{7,6},{8,9},{9,8},{10,11... | collective-permute-start | bytes 1105928 | tf_op jit(solution)/shard_map/ppermute | solution.py:27
  360.7 19.4 %collective-permute-start.75 = (bf16[192,1536]{1,0:T(8,128)(2,1)S(1)}, bf16[192,1536]{1,0:T(8,128)(2,1)S(1)}, u32[]{:S(2)}, u32[]{:S(2)}) collective-permute-start(bf16[192,1536]{1,0:T(8,128)(2,1)S(1)} %get-tuple-element.577), channel_id=1, source_target_pairs={{0,2},{2,0},{4,6},{6,4},{8,10},{10,8},{12,14},{14,12},{1,3},{3,1},... | collective-permute-start | bytes 1769480 | tf_op jit(solution)/shard_map/ppermute | solution.py:31
  361.7 18.5 %collective-permute-start.76 = (bf16[192,1536]{1,0:T(8,128)(2,1)S(1)}, bf16[192,1536]{1,0:T(8,128)(2,1)S(1)}, u32[]{:S(2)}, u32[]{:S(2)}) collective-permute-start(bf16[192,1536]{1,0:T(8,128)(2,1)S(1)} %get-tuple-element.578), channel_id=1, source_target_pairs={{0,1},{1,0},{2,3},{3,2},{4,5},{5,4},{6,7},{7,6},{8,9},{9,8},{10,11... | collective-permute-start | bytes 1769480 | tf_op jit(solution)/shard_map/ppermute | solution.py:27
  384.3 34.0 %collective-permute-start.87 = (bf16[512,768]{1,0:T(8,128)(2,1)S(1)}, bf16[512,768]{1,0:T(8,128)(2,1)S(1)}, u32[]{:S(2)}, u32[]{:S(2)}) collective-permute-start(bf16[512,768]{1,0:T(8,128)(2,1)S(1)} %fusion.24), channel_id=1, source_target_pairs={{16,17},{17,16},{18,19},{19,18},{20,21},{21,20},{22,23},{23,22},{2... | collective-permute-start | bytes 2359304 | tf_op jit(solution)/shard_map/ppermute | solution.py:633
  386.7 31.7 %collective-permute-start.79 = (bf16[192,1920]{1,0:T(8,128)(2,1)S(1)}, bf16[192,1920]{1,0:T(8,128)(2,1)S(1)}, u32[]{:S(2)}, u32[]{:S(2)}) collective-permute-start(bf16[192,1920]{1,0:T(8,128)(2,1)S(1)} %get-tuple-element.599), channel_id=1, source_target_pairs={{0,2},{2,0},{4,6},{6,4},{8,10},{10,8},{12,14},{14,12},{1,3},{3,1},... | collective-permute-start | bytes 2211848 | tf_op jit(solution)/shard_map/ppermute | solution.py:31
  387.6 30.8 %collective-permute-start.80 = (bf16[192,1920]{1,0:T(8,128)(2,1)S(1)}, bf16[192,1920]{1,0:T(8,128)(2,1)S(1)}, u32[]{:S(2)}, u32[]{:S(2)}) collective-permute-start(bf16[192,1920]{1,0:T(8,128)(2,1)S(1)} %get-tuple-element.600), channel_id=1, source_target_pairs={{0,1},{1,0},{2,3},{3,2},{4,5},{5,4},{6,7},{7,6},{8,9},{9,8},{10,11... | collective-permute-start | bytes 2211848 | tf_op jit(solution)/shard_map/ppermute | solution.py:27
  433.7 16.4 %collective-permute-start.96 = (bf16[48,1920]{1,0:T(8,128)(2,1)}, bf16[48,1920]{1,0:T(8,128)(2,1)}, u32[]{:S(2)}, u32[]{:S(2)}) collective-permute-start(bf16[48,1920]{1,0:T(8,128)(2,1)} %get-tuple-element.624), channel_id=1, source_target_pairs={{0,12},{2,14},{4,0},{6,2},{8,4},{10,6},{12,8},{14,10},{1,13},{3,15... | collective-permute-start | bytes 552968 | tf_op jit(solution)/shard_map/ppermute | solution.py:37
  434.9 20.1 %collective-permute-start.97 = (bf16[48,1920]{1,0:T(8,128)(2,1)}, bf16[48,1920]{1,0:T(8,128)(2,1)}, u32[]{:S(2)}, u32[]{:S(2)}) collective-permute-start(bf16[48,1920]{1,0:T(8,128)(2,1)} %get-tuple-element.625), channel_id=1, source_target_pairs={{0,8},{2,10},{4,12},{6,14},{8,0},{10,2},{12,4},{14,6},{1,9},{3,11}... | collective-permute-start | bytes 552968 | tf_op jit(solution)/shard_map/ppermute | solution.py:37
  450.1 21.2 %collective-permute-start.102 = (bf16[512,768]{1,0:T(8,128)(2,1)}, bf16[512,768]{1,0:T(8,128)(2,1)}, u32[]{:S(2)}, u32[]{:S(2)}) collective-permute-start(bf16[512,768]{1,0:T(8,128)(2,1)} %fusion.25), channel_id=1, source_target_pairs={{0,1},{1,0},{2,3},{3,2},{4,5},{5,4},{6,7},{7,6},{8,9},{9,8},{10,11... | collective-permute-start | bytes 2359304 | tf_op jit(solution)/shard_map/ppermute | solution.py:633
  (156 other events, 1293.4 us)
Sparse Core Ops, SparseCore 0:
  38.3 99.0 all-gather.2
